TPU v7x, 512 devices: a whole 4x8x8 slice. The times are simulated.
512 devices in a mesh: rep: 32 (over y_lo, z, core), fsdp: 16 (over y_hi, x).
Axes of the slice: x: 4, y: 8 (y_hi: 4, y_lo: 2; y = y_hi * 2 + y_lo), z: 8, core: 2. Of those that a mesh axis runs over, the one named last changes fastest.
Arguments:
- attn_out: bfloat16 [81920, 2560], P('rep', 'fsdp'), may hold values from -6 to 6
- out_grad: bfloat16 [81920, 2560], P(('rep', 'fsdp')), may hold values from -6 to 6
- momentum: bfloat16 [32, 2560, 2560], P('rep', 'fsdp'), may hold values from -6 to 6
- kept: int32 [16], replicated, may hold values from 0 to 63, as said below
Outputs:
- update: bfloat16 [2560, 2560], P('fsdp')
- new_momentum: bfloat16 [32, 2560, 2560], P('rep', 'fsdp')
Inputs may be any that keep to these rules, and one draw needn't show every extreme that they name: `kept`: 16 distinct frequencies, among them 0 and 63.
All inputs are finite; a program needn't handle non-finite values.
Results may differ from a plain program's by a relative error of at most 0.001.
Values may be sent and summed in bfloat16 or wider, within the bound.
No kernel may reach another device: no remote copies, remote signals or barrier semaphores. Data moves between devices by JAX's collectives and lax.ppermute only.
A program may use at most 64 MiB of HBM per device.

v0:
```python
import math

import jax
import jax.numpy as jnp
from jax import lax
from jax.sharding import PartitionSpec as P

GROUP = 64
KEEP = 16


BETA = 0.999


def basis_table(kept):
    freq = kept.astype(jnp.float32)
    points = jnp.arange(GROUP, dtype=jnp.float32) + 0.5
    weight = jnp.where(kept == 0, math.sqrt(1.0 / GROUP), math.sqrt(2.0 / GROUP)).astype(
        jnp.float32
    )
    return weight[None, :] * jnp.cos(math.pi * points[:, None] * freq[None, :] / GROUP)


def encode(moment, basis):
    rows, width = moment.shape
    blocks = moment.reshape(rows, width // GROUP, GROUP)
    coeff = jnp.einsum("rcn,nk->rck", blocks, basis, precision=lax.Precision.HIGHEST)
    return coeff.reshape(rows, width // GROUP * KEEP)


def decode(coeff, basis):
    rows = coeff.shape[0]
    blocks = coeff.reshape(rows, coeff.shape[1] // KEEP, KEEP)
    values = jnp.einsum("rck,nk->rcn", blocks, basis, precision=lax.Precision.HIGHEST)
    return values.reshape(rows, values.shape[1] * GROUP)


def finish(grad, stored, basis, replicas, reducer):
    moment = BETA * stored.astype(jnp.float32) + grad
    coeff = encode(moment, basis)
    fresh = (moment - decode(coeff, basis)).astype(jnp.bfloat16)
    total = reducer(coeff)
    update = decode(total / replicas, basis).astype(jnp.bfloat16)
    return (update, fresh)


def per_device(attn_out, out_grad, momentum, kept):
    basis = basis_table(kept)
    replicas = lax.axis_size("rep")
    scale = 1.0 / math.sqrt(attn_out.shape[0])
    stored = momentum[0]
    grad = (
        lax.dot_general(
            attn_out,
            lax.all_gather(out_grad, "fsdp", axis=0, tiled=True),
            (((0,), (0,)), ((), ())),
            preferred_element_type=jnp.float32,
        )
        * scale
    )

    def reduce_whole(coeff):
        return lax.psum(coeff, "rep")

    update, fresh = finish(grad, stored, basis, replicas, reduce_whole)
    return (update, fresh[None])


def solution(mesh):
    placed = (P("rep", "fsdp"), P(("rep", "fsdp"), None), P("rep", "fsdp", None), P())
    return jax.shard_map(
        per_device,
        mesh=mesh,
        in_specs=placed,
        out_specs=(P("fsdp", None), P("rep", "fsdp", None)),
        check_vma=False,
    )
```

profile of v0, /device:TPU:1, one launch (start us, length us, event | category | flops | bytes accessed | tf_op | source)
XLA Modules:
  0.0 440.0 jit_solution(11715753491367248227)
XLA Ops:
  7.2 0.0 copy-start
  7.2 0.0 all-gather.2.cloned.1.call-start
  7.2 0.7 all-gather.2.cloned.1.call-update
  7.9 0.7 convert_element_type.17
  8.6 0.7 compare_select_fusion
  9.2 177.7 %all-gather.2.cloned.1.call-done = bf16[2560,2560]{1,0:T(8,128)(2,1)} async-done(((bf16[160,2560]{1,0:T(8,128)(2,1)}), bf16[2560,2560]{1,0:T(8,128)(2,1)}) %all-gather.2.cloned.1.call-update) | async-done | bytes 13107216 | tf_op jit(solution)/shard_map/all_gather | solution.py:55
  187.0 0.0 copy-done
  187.0 7.2 %fusion = f32[160,2560]{1,0:T(8,128)S(1)} fusion(bf16[2560,160]{0,1:T(8,128)(2,1)S(1)} %copy-done, bf16[2560,2560]{1,0:T(8,128)(2,1)} %all-gather.2.cloned.1.call-done, bf16[1,160,2560]{2,1,0:T(8,128)(2,1)} %param.6), kind=kOutput, calls=%fused_computation.1 | convolution fusion | flops 2098790400 | bytes 16384000 | tf_op jit(solution)/shard_map/dot_general | solution.py:53
  194.1 2.0 copy.12
  196.2 3.2 fusion.5
  199.4 0.0 copy-start.1
  199.5 3.9 fusion.2
  203.3 0.0 copy-done.1
  203.3 0.0 all-reduce.2.cloned.1.call-start
  203.3 3.0 copy.13
  206.3 0.0 all-reduce.2.cloned.1.call-update
  206.4 2.5 fusion.1
  208.9 219.5 %all-reduce.2.cloned.1.call-done = f32[160,640]{0,1:T(8,128)} async-done(((f32[160,640]{0,1:T(8,128)}), f32[160,640]{0,1:T(8,128)}) %all-reduce.2.cloned.1.call-update) | async-done | bytes 409616 | tf_op jit(solution)/shard_map/psum | solution.py:63
  428.3 1.1 broadcast_multiply_fusion
  429.5 2.4 convolution_convert_fusion
  431.8 1.3 copy.11
  (1 shorter events, 0.0 us)
Async XLA Ops:
  7.2 179.8 %copy-start = (bf16[2560,160]{0,1:T(8,128)(2,1)S(1)}, bf16[2560,160]{0,1:T(8,128)(2,1)}, u32[]{:S(2)}) copy-start(bf16[2560,160]{0,1:T(8,128)(2,1)} %param.4) | copy-start | bytes 2457604
  7.2 179.8 %all-gather.2.cloned.1.call-start = ((), (), s32[]{:S(2)}) async-start(), calls=%async_computation | async-start | bytes 13926400 | tf_op jit(solution)/shard_map/all_gather | solution.py:55
  199.4 3.9 copy-start.1
  203.3 225.0 %all-reduce.2.cloned.1.call-start = ((), (), s32[]{:S(2)}) async-start(), calls=%async_computation.1 | async-start | bytes 1310720 | tf_op jit(solution)/shard_map/psum | solution.py:63
Sparse Core Ops, SparseCore 0:
  11.0 175.8 all-gather.1
  207.7 220.6 all-reduce.1
where the time goes:
time: 440 us
  waiting for transfers between devices  398 us (90%)
  matrix products  16.7 us (4%)
  between operations  14.1 us (3%)
  local copies, waits for them, and re-layouts  6.37 us (1%)
  other arithmetic  4.94 us (1%)
    psum x1, waiting for transfers between devices, reduce_whole(): return lax.psum(coeff, 'rep')  219 us
    all_gather x1, waiting for transfers between devices, per_device(): lax.all_gather(out_grad, 'fsdp', axis=0, tiled=True)  178 us
  transfers between devices with their start and end apart: 2, of which 2 were waited for; matrix products, arithmetic and copies ran while one was open for 1% of the time, Pallas kernels for 0%

commit v1 on v0

v1 whole, which is shorter than its diff:
```python
import math

import jax
import jax.numpy as jnp
from jax import lax
from jax.experimental import pallas as pl
from jax.experimental.pallas import tpu as pltpu
from jax.sharding import Mesh, PartitionSpec as P

GROUP = 64
KEEP = 16
BETA = 0.999

REP = ("ylo", "z", "core")
FSDP = ("yhi", "x")


def basis_table(kept):
    freq = kept.astype(jnp.float32)
    points = jnp.arange(GROUP, dtype=jnp.float32) + 0.5
    weight = jnp.where(kept == 0, math.sqrt(1.0 / GROUP), math.sqrt(2.0 / GROUP)).astype(
        jnp.float32
    )
    return weight[None, :] * jnp.cos(math.pi * points[:, None] * freq[None, :] / GROUP)


def block_basis(basis, groups):
    tiled = jnp.tile(basis, (groups, groups))
    row = lax.broadcasted_iota(jnp.int32, tiled.shape, 0) // GROUP
    col = lax.broadcasted_iota(jnp.int32, tiled.shape, 1) // KEEP
    return jnp.where(row == col, tiled, 0.0)


def dot_f32(a, b, dims):
    return lax.dot_general(
        a, b, (dims, ((), ())), precision=lax.Precision.HIGHEST, preferred_element_type=jnp.float32
    )


def product_kernel(
    scale, where_ref, acts_ref, own_ref, pa_ref, pb_ref, ma_ref, mb_ref, fa_ref, fb_ref,
    mom_ref, basis_ref, fresh_ref, keep_ref, send_ref,
):
    yhi = where_ref[0]
    core = where_ref[1]
    depth = own_ref.shape[0]
    half = depth // 2

    def acts(shift, start, size):
        at = lax.rem(yhi + shift, 4) * depth
        block = acts_ref[:, pl.ds(pl.multiple_of(at, depth), depth)]
        return block[:, start : start + size]

    def mul(a, b_ref):
        return jnp.dot(a, b_ref[...], preferred_element_type=jnp.float32)

    grad = mul(acts(0, 0, depth), own_ref)
    grad += jnp.dot(
        acts(3, 0, depth), jnp.concatenate([pa_ref[...], pb_ref[...]], 0),
        preferred_element_type=jnp.float32,
    )
    grad += jnp.dot(
        acts(1, 0, depth), jnp.concatenate([ma_ref[...], mb_ref[...]], 0),
        preferred_element_type=jnp.float32,
    )
    grad += jnp.dot(
        acts(2, 0, depth), jnp.concatenate([fa_ref[...], fb_ref[...]], 0),
        preferred_element_type=jnp.float32,
    )
    moment = BETA * mom_ref[...].astype(jnp.float32) + grad * scale
    basis = basis_ref[...]
    coeff = dot_f32(moment, basis, ((1,), (0,)))
    fresh_ref[...] = (moment - dot_f32(coeff, basis, ((1,), (1,)))).astype(jnp.bfloat16)
    rows = coeff.shape[0] // 2
    low, high = coeff[:rows], coeff[rows:]
    keep_ref[0] = jnp.where(core == 0, low, high)
    send_ref[0] = jnp.where(core == 0, high, low)


def product(scale, where, acts, own, parts, mom, basis):
    feats, toks = acts.shape
    outs = own.shape[1]
    nrow = feats // 4
    coefs = basis.shape[1]
    whole = lambda a: pl.BlockSpec(a.shape, lambda p: (0,) * a.ndim)
    half = jax.ShapeDtypeStruct((4, nrow // 2, coefs), jnp.float32)
    return pl.pallas_call(
        lambda *refs: product_kernel(scale, *refs),
        grid=(4,),
        in_specs=[
            pl.BlockSpec(memory_space=pltpu.SMEM),
            pl.BlockSpec((nrow, toks), lambda p: (p, 0)),
            whole(own),
            *[whole(a) for a in parts],
            pl.BlockSpec((nrow, outs), lambda p: (p, 0)),
            whole(basis),
        ],
        out_specs=[
            pl.BlockSpec((nrow, outs), lambda p: (p, 0)),
            pl.BlockSpec((1, nrow // 2, coefs), lambda p: (p, 0, 0)),
            pl.BlockSpec((1, nrow // 2, coefs), lambda p: (p, 0, 0)),
        ],
        out_shape=[jax.ShapeDtypeStruct((feats, outs), jnp.bfloat16), half, half],
        compiler_params=pltpu.CompilerParams(vmem_limit_bytes=32 * 1024 * 1024),
        cost_estimate=pl.CostEstimate(
            flops=2 * feats * toks * outs + 24 * feats * outs * coefs,
            bytes_accessed=2 * (feats * toks + toks * outs + 2 * feats * outs) + 8 * feats * coefs,
            transcendentals=0,
        ),
    )(where, acts, own, *parts, mom, basis)


def decode_kernel(replicas, total_ref, basis_ref, out_ref):
    mean = total_ref[0] / replicas
    out_ref[...] = dot_f32(mean, basis_ref[...], ((1,), (1,))).astype(jnp.bfloat16)


def decode(replicas, total, basis):
    quarters, rows, coefs = total.shape
    outs = basis.shape[0]
    return pl.pallas_call(
        lambda *refs: decode_kernel(replicas, *refs),
        grid=(quarters,),
        in_specs=[
            pl.BlockSpec((1, rows, coefs), lambda q: (q, 0, 0)),
            pl.BlockSpec(basis.shape, lambda q: (0, 0)),
        ],
        out_specs=pl.BlockSpec((rows, outs), lambda q: (0, q)),
        out_shape=jax.ShapeDtypeStruct((rows, quarters * outs), jnp.bfloat16),
        cost_estimate=pl.CostEstimate(
            flops=12 * quarters * rows * coefs * outs,
            bytes_accessed=4 * quarters * rows * coefs + 2 * quarters * rows * outs,
            transcendentals=0,
        ),
    )(total, basis)


def shifted(x, axis, size, by):
    return lax.ppermute(x, axis, [(i, (i + by) % size) for i in range(size)])


def per_device(attn_out, out_grad, momentum, kept):
    replicas = 32
    scale = 1.0 / math.sqrt(attn_out.shape[0])
    toks, width = out_grad.shape
    half = 2 * toks

    own = lax.all_to_all(out_grad, "x", 1, 0, tiled=True)
    acts = lax.all_gather(attn_out.T, "x", axis=0, tiled=True)
    low, high = own[:half], own[half:]
    from_below_low = shifted(low, "yhi", 4, 1)
    from_above_high = shifted(high, "yhi", 4, -1)
    from_below_high = shifted(high, "yhi", 4, 1)
    from_above_low = shifted(low, "yhi", 4, -1)
    far_low = shifted(from_below_low, "yhi", 4, 1)
    far_high = shifted(from_above_high, "yhi", 4, -1)
    mom = lax.all_to_all(momentum[0], "x", 1, 0, tiled=True)

    basis = block_basis(basis_table(kept), width // 4 // GROUP)
    where = jnp.stack([lax.axis_index("yhi"), lax.axis_index("core")]).astype(jnp.int32)
    parts = (from_below_low, from_below_high, from_above_low, from_above_high, far_low, far_high)
    fresh, keep, send = product(scale, where, acts, own, parts, mom, basis)
    new_momentum = lax.all_to_all(fresh, "x", 0, 1, tiled=True)

    coefs = keep.shape[-1]
    pair = keep + shifted(send, "core", 2, 1)
    pieces = lax.all_to_all(pair.reshape(8, 40, coefs), ("x", "ylo"), 0, 0, tiled=True)
    summed = pieces.reshape(4, 2, 40, coefs).sum(1)
    pieces = lax.all_to_all(summed.reshape(8, 20, coefs), "z", 0, 0, tiled=True)
    summed = pieces.sum(0)
    spread = jnp.broadcast_to(summed[None], (16, 20, coefs))
    spread = lax.all_to_all(spread, ("ylo", "z"), 0, 0, tiled=True)
    spread = lax.all_gather(spread, "core", axis=0)
    total = spread.reshape(2, 2, 4, 2, 20, coefs).transpose(2, 0, 1, 3, 4, 5)
    update = decode(replicas, total.reshape(4, toks, coefs), basis)
    return update, new_momentum[None]


def solution(mesh):
    fine = Mesh(mesh.devices.reshape(2, 8, 2, 4, 4), ("ylo", "z", "core", "yhi", "x"))
    return jax.shard_map(
        per_device,
        mesh=fine,
        in_specs=(P(REP, FSDP), P(REP + FSDP, None), P(REP, FSDP, None), P()),
        out_specs=(P(FSDP, None), P(REP, FSDP, None)),
        check_vma=False,
    )
```

time: 440 us -> 195 us (0.44)
  waiting for transfers between devices: 398 us -> 52.3 us
  blocking collectives: 0 us -> 47.8 us
  starting transfers between devices: 0.04 us -> 45.4 us
  Pallas kernels: 0 us -> 18.1 us
  matrix products: 16.7 us -> 0 us
  local copies, waits for them, and re-layouts: 6.37 us -> 14.1 us
    psum x1 -> x0, waiting for transfers between devices: 219 us -> none  [reduce_whole(): return lax.psum(coeff, 'rep')]
    all_gather x1, waiting for transfers between devices: 178 us -> 0.01 us  [per_device(): acts = lax.all_gather(attn_out.T, 'x', axis=0, tiled=True)]
    all_to_all x0 -> x2, blocking collectives: none -> 41 us  [the longest x1 22.4 us: per_device(): lax.all_to_all(pair.reshape(8, 40, coefs), ('x', 'ylo'), 0, 0, tiled=True)]
    ppermute x0 -> x7, starting transfers between devices: none -> 28.3 us  [shifted(): return lax.ppermute(x, axis, [(i, (i + by) % size) for i in range(size)])]
    ppermute x0 -> x7, waiting for transfers between devices: none -> 28.2 us  [shifted(): return lax.ppermute(x, axis, [(i, (i + by) % size) for i in range(size)])]
    all_to_all x0 -> x4, waiting for transfers between devices: none -> 23.4 us  [the longest x1 9.34 us: per_device(): new_momentum = lax.all_to_all(fresh, 'x', 0, 1, tiled=True)]
    pallas_call x0 -> x2, Pallas kernels: none -> 18.1 us  [the longest x1 12.8 us: product(): pl.pallas_call(lambda *refs: product_kernel(scale, *refs), grid=(4,), in_...]
    all_to_all x0 -> x4, starting transfers between devices: none -> 17.1 us  [the longest x1 5.24 us: per_device(): spread = lax.all_to_all(spread, ('ylo', 'z'), 0, 0, tiled=True)]
  transfers between devices with their start and end apart: 2 -> 12, of which waited for: 2 -> 9; matrix products, arithmetic and copies ran while one was open for 1% -> 6% of each run, Pallas kernels for 0% -> 0%
where the time goes in v1:
time: 195 us; the launch traced here: 194 us
  waiting for transfers between devices  52.3 us (27%)
  blocking collectives  47.8 us (25%)
  starting transfers between devices  45.4 us (23%)
  Pallas kernels  18.1 us (9%)
  between operations  14.2 us (7%)
  local copies, waits for them, and re-layouts  14.1 us (7%)
    ppermute x7, starting transfers between devices, shifted(): return lax.ppermute(x, axis, [(i, (i + by) % size) for i in range(size)])  28.3 us
    ppermute x7, waiting for transfers between devices, shifted(): return lax.ppermute(x, axis, [(i, (i + by) % size) for i in range(size)])  28.2 us
    all_to_all x1, blocking collectives, per_device(): lax.all_to_all(pair.reshape(8, 40, coefs), ('x', 'ylo'), 0, 0, tiled=True)  22.4 us
    all_to_all x1, blocking collectives, per_device(): pieces = lax.all_to_all(summed.reshape(8, 20, coefs), 'z', 0, 0, tiled=True)  18.6 us
    pallas_call x1, Pallas kernels, product(): pl.pallas_call(lambda *refs: product_kernel(scale, *refs), grid=(4,), in_...  12.8 us
    all_to_all x1, waiting for transfers between devices, per_device(): new_momentum = lax.all_to_all(fresh, 'x', 0, 1, tiled=True)  9.34 us
    all_to_all x1, waiting for transfers between devices, per_device(): own = lax.all_to_all(out_grad, 'x', 1, 0, tiled=True)  7.3 us
    all_gather x1, blocking collectives, per_device(): spread = lax.all_gather(spread, 'core', axis=0)  6.82 us
  transfers between devices with their start and end apart: 12, of which 9 were waited for; matrix products, arithmetic and copies ran while one was open for 6% of the time, Pallas kernels for 0%

profile of v1, /device:TPU:1, one launch (start us, length us, event | category | flops | bytes accessed | tf_op | source)
XLA Modules:
  0.0 193.7 jit_solution(17683982630789802871)
XLA Ops:
  7.9 2.1 %copy.31 = bf16[20,4,8,640]{3,2,0,1:T(8,128)(2,1)} copy(bf16[20,4,8,640]{3,2,1,0:T(8,128)(2,1)} %bitcast.33) | data formatting | bytes 1638400 | tf_op jit(solution)/shard_map/all_to_all | solution.py:148
  10.0 4.9 %all-to-all-start = ((bf16[160,4,640]{2,0,1:T(8,128)(2,1)}), bf16[160,4,640]{2,0,1:T(8,128)(2,1)S(1)}, u32[]{:S(2)}, u32[]{:S(2)}) async-start(bf16[160,4,640]{2,0,1:T(8,128)(2,1)} %bitcast.25), calls=%async_computation | async-start | bytes 1638400 | tf_op jit(solution)/shard_map/all_to_all | solution.py:148
  16.1 7.3 %all-to-all-done = bf16[160,4,640]{2,0,1:T(8,128)(2,1)S(1)} async-done(((bf16[160,4,640]{2,0,1:T(8,128)(2,1)}), bf16[160,4,640]{2,0,1:T(8,128)(2,1)S(1)}, u32[]{:S(2)}, u32[]{:S(2)}) %all-to-all-start) | async-done | bytes 819232 | tf_op jit(solution)/shard_map/all_to_all | solution.py:148
  23.4 3.5 %all-to-all-start.1 = ((bf16[160,4,640]{2,0,1:T(8,128)(2,1)}), bf16[160,4,640]{2,0,1:T(8,128)(2,1)S(1)}, u32[]{:S(2)}, u32[]{:S(2)}) async-start(bf16[160,4,640]{2,0,1:T(8,128)(2,1)} %copy.23), calls=%async_computation.1 | async-start | bytes 1638400 | tf_op jit(solution)/shard_map/all_to_all | solution.py:157
  27.9 7.4 %collective-permute-start = (bf16[320,640]{1,0:T(8,128)(2,1)}, bf16[320,640]{1,0:T(8,128)(2,1)S(1)}, u32[]{:S(2)}, u32[]{:S(2)}) collective-permute-start(bf16[320,640]{1,0:T(8,128)(2,1)} %bitcast.5), channel_id=1, source_target_pairs={{0,4},{4,8},{8,12},{12,0},{1,5},{5,9},{9,13},{13,1},{2,6},{6,10},{... | collective-permute-start | bytes 1228808 | tf_op jit(solution)/shard_map/ppermute | solution.py:139
  35.3 3.6 %collective-permute-start.3 = (bf16[320,640]{1,0:T(8,128)(2,1)}, bf16[320,640]{1,0:T(8,128)(2,1)S(1)}, u32[]{:S(2)}, u32[]{:S(2)}) collective-permute-start(bf16[320,640]{1,0:T(8,128)(2,1)} %bitcast.6), channel_id=1, source_target_pairs={{0,12},{4,0},{8,4},{12,8},{1,13},{5,1},{9,5},{13,9},{2,14},{6,2},{... | collective-permute-start | bytes 1228808 | tf_op jit(solution)/shard_map/ppermute | solution.py:139
  39.1 4.3 %collective-permute-start.2 = (bf16[320,640]{1,0:T(8,128)(2,1)}, bf16[320,640]{1,0:T(8,128)(2,1)S(1)}, u32[]{:S(2)}, u32[]{:S(2)}) collective-permute-start(bf16[320,640]{1,0:T(8,128)(2,1)} %bitcast.5), channel_id=1, source_target_pairs={{0,12},{4,0},{8,4},{12,8},{1,13},{5,1},{9,5},{13,9},{2,14},{6,2},{... | collective-permute-start | bytes 1228808 | tf_op jit(solution)/shard_map/ppermute | solution.py:139
  45.3 2.3 %collective-permute-done.refs_3_ = bf16[320,640]{1,0:T(8,128)(2,1)S(1)} collective-permute-done((bf16[320,640]{1,0:T(8,128)(2,1)}, bf16[320,640]{1,0:T(8,128)(2,1)S(1)}, u32[]{:S(2)}, u32[]{:S(2)}) %collective-permute-start) | collective-permute-done | bytes 409632 | tf_op jit(solution)/shard_map/ppermute | solution.py:139
  47.5 5.7 %collective-permute-start.4 = (bf16[320,640]{1,0:T(8,128)(2,1)S(1)}, bf16[320,640]{1,0:T(8,128)(2,1)}, u32[]{:S(2)}, u32[]{:S(2)}) collective-permute-start(bf16[320,640]{1,0:T(8,128)(2,1)S(1)} %collective-permute-done.refs_3_), channel_id=1, source_target_pairs={{0,4},{4,8},{8,12},{12,0},{1,5},{5,9},{9,13},{13,1},{2,6},{6,10},{... | collective-permute-start | bytes 1228808 | tf_op jit(solution)/shard_map/ppermute | solution.py:139
  53.2 15.2 %collective-permute-done.3.refs_6_ = bf16[320,640]{1,0:T(8,128)(2,1)S(1)} collective-permute-done((bf16[320,640]{1,0:T(8,128)(2,1)}, bf16[320,640]{1,0:T(8,128)(2,1)S(1)}, u32[]{:S(2)}, u32[]{:S(2)}) %collective-permute-start.3) | collective-permute-done | bytes 409632 | tf_op jit(solution)/shard_map/ppermute | solution.py:139
  68.4 2.9 %collective-permute-start.5 = (bf16[320,640]{1,0:T(8,128)(2,1)S(1)}, bf16[320,640]{1,0:T(8,128)(2,1)}, u32[]{:S(2)}, u32[]{:S(2)}) collective-permute-start(bf16[320,640]{1,0:T(8,128)(2,1)S(1)} %collective-permute-done.3.refs_6_), channel_id=1, source_target_pairs={{0,12},{4,0},{8,4},{12,8},{1,13},{5,1},{9,5},{13,9},{2,14},{6,2},{... | collective-permute-start | bytes 1228808 | tf_op jit(solution)/shard_map/ppermute | solution.py:139
  77.3 6.2 %collective-permute-done.4.refs_7_ = bf16[320,640]{1,0:T(8,128)(2,1)} collective-permute-done((bf16[320,640]{1,0:T(8,128)(2,1)S(1)}, bf16[320,640]{1,0:T(8,128)(2,1)}, u32[]{:S(2)}, u32[]{:S(2)}) %collective-permute-start.4) | collective-permute-done | bytes 409632 | tf_op jit(solution)/shard_map/ppermute | solution.py:139
  83.5 2.7 %collective-permute-done.5.refs_8_ = bf16[320,640]{1,0:T(8,128)(2,1)} collective-permute-done((bf16[320,640]{1,0:T(8,128)(2,1)S(1)}, bf16[320,640]{1,0:T(8,128)(2,1)}, u32[]{:S(2)}, u32[]{:S(2)}) %collective-permute-start.5) | collective-permute-done | bytes 409632 | tf_op jit(solution)/shard_map/ppermute | solution.py:139
  86.2 1.9 copy-done.1
  88.1 12.8 %shard_map.59 = (bf16[640,640]{1,0:T(8,128)(2,1)}, f32[4,80,160]{2,1,0:T(8,128)S(1)}, f32[4,80,160]{2,1,0:T(8,128)S(1)}) custom-call(s32[2]{0:T(128)S(1)} %pad_add_fusion.refs_0_, bf16[640,2560]{1,0:T(8,128)(2,1)S(1)} %copy-done.1, bf16[640,640]{1,0:T(8,128)(2,1)S(1)} %bitcast.27, bf16[320,640]{1,0:T(8,128)(2,1)S(1)} %collective-permute-done.refs_3_, ...), custom_call_target="tpu_custom_call" | custom-call | flops 3670016000 | bytes 9011200 | tf_op jit(solution)/shard_map/pallas_call | solution.py:87
  100.9 2.5 %collective-permute-start.6 = (f32[4,80,160]{2,1,0:T(8,128)S(1)}, f32[4,80,160]{2,1,0:T(8,128)S(1)}, u32[]{:S(2)}, u32[]{:S(2)}) collective-permute-start(f32[4,80,160]{2,1,0:T(8,128)S(1)} %get-tuple-element.6), channel_id=1, source_target_pairs={{0,16},{16,0},{1,17},{17,1},{2,18},{18,2},{3,19},{19,3},{4,20},{20... | collective-permute-start | bytes 614408 | tf_op jit(solution)/shard_map/ppermute | solution.py:139
  104.7 22.4 %all_to_all.69 = f32[8,40,160]{2,1,0:T(8,128)S(1)} all-to-all(f32[8,40,160]{2,1,0:T(8,128)S(1)} %bitcast.32), channel_id=1, replica_groups=mesh['ylo'=2,'z'=8,'core'=2,'yhi'=4,'x'=4] {'x','ylo'}, dimensions={0} | all-to-all | bytes 409600 | tf_op jit(solution)/shard_map/all_to_all | solution.py:167
  127.2 18.6 %all_to_all.70 = f32[8,20,160]{2,1,0:T(8,128)S(1)} all-to-all(f32[8,20,160]{2,1,0:T(8,128)S(1)} %reshape.84), channel_id=1, replica_groups=mesh['ylo'=2,'z'=8,'core'=2,'yhi'=4,'x'=4] {'z'}, dimensions={0} | all-to-all | bytes 204800 | tf_op jit(solution)/shard_map/all_to_all | solution.py:169
  145.8 3.5 %all-to-all-start.5 = ((bf16[4,160,640]{2,1,0:T(8,128)(2,1)}), bf16[4,160,640]{2,1,0:T(8,128)(2,1)S(1)}, u32[]{:S(2)}, u32[]{:S(2)}) async-start(bf16[4,160,640]{2,1,0:T(8,128)(2,1)} %bitcast.13), calls=%async_computation.5 | async-start | bytes 1638400 | tf_op jit(solution)/shard_map/all_to_all | solution.py:163
  149.3 9.3 %all-to-all-done.5 = bf16[4,160,640]{2,1,0:T(8,128)(2,1)S(1)} async-done(((bf16[4,160,640]{2,1,0:T(8,128)(2,1)}), bf16[4,160,640]{2,1,0:T(8,128)(2,1)S(1)}, u32[]{:S(2)}, u32[]{:S(2)}) %all-to-all-start.5) | async-done | bytes 819232 | tf_op jit(solution)/shard_map/all_to_all | solution.py:163
  159.4 5.2 %all-to-all-start.4 = ((f32[16,20,160]{2,1,0:T(8,128)}), f32[16,20,160]{2,1,0:T(8,128)S(1)}, u32[]{:S(2)}, u32[]{:S(2)}) async-start(f32[16,20,160]{2,1,0:T(8,128)} %broadcast_in_dim.27), calls=%async_computation.4 | async-start | bytes 786432 | tf_op jit(solution)/shard_map/all_to_all | solution.py:172
  166.3 6.8 %all-to-all-done.4 = f32[16,20,160]{2,1,0:T(8,128)S(1)} async-done(((f32[16,20,160]{2,1,0:T(8,128)}), f32[16,20,160]{2,1,0:T(8,128)S(1)}, u32[]{:S(2)}, u32[]{:S(2)}) %all-to-all-start.4) | async-done | bytes 204832 | tf_op jit(solution)/shard_map/all_to_all | solution.py:172
  173.2 6.8 %all-gather = f32[32,20,160]{2,0,1:T(8,128)S(1)} all-gather(f32[16,20,160]{2,0,1:T(8,128)S(1)} %copy.25), channel_id=2, replica_groups=mesh['ylo'=2,'z'=8,'core'=2,'yhi'=4,'x'=4] {'core'}, dimensions={0}, use_global_device_ids=true | all-gather | bytes 614400 | tf_op jit(solution)/shard_map/all_gather | solution.py:173
  181.6 5.3 %shard_map.60 = bf16[160,2560]{1,0:T(8,128)(2,1)} custom-call(f32[4,160,160]{2,1,0:T(8,128)} %copy.27.refs_0_, f32[640,160]{1,0:T(8,128)} %copy-done), custom_call_target="tpu_custom_call" | custom-call | flops 786432000 | bytes 1228800 | tf_op jit(solution)/shard_map/pallas_call | solution.py:121
  (42 shorter events, 16.3 us)
Async XLA Ops:
  7.2 7.7 %copy-start.3 = (s32[16]{0:T(128)S(1)}, s32[16]{0:T(128)}, u32[]{:S(2)}) copy-start(s32[16]{0:T(128)} %param.7) | copy-start | bytes 196
  7.2 7.7 %copy-start.2 = (bf16[1,160,2560]{2,1,0:T(8,128)(2,1)S(1)}, bf16[1,160,2560]{2,1,0:T(8,128)(2,1)}, u32[]{:S(2)}) copy-start(bf16[1,160,2560]{2,1,0:T(8,128)(2,1)} %param.6) | copy-start | bytes 2457604
  7.2 79.0 %all-gather.3.cloned.1.call-start = ((), (), s32[]{:S(2)}) async-start(), calls=%async_computation.6 | async-start | bytes 4096000 | tf_op jit(solution)/shard_map/all_gather | solution.py:149
  10.0 13.4 %all-to-all-start = ((bf16[160,4,640]{2,0,1:T(8,128)(2,1)}), bf16[160,4,640]{2,0,1:T(8,128)(2,1)S(1)}, u32[]{:S(2)}, u32[]{:S(2)}) async-start(bf16[160,4,640]{2,0,1:T(8,128)(2,1)} %bitcast.25), calls=%async_computation | async-start | bytes 1638400 | tf_op jit(solution)/shard_map/all_to_all | solution.py:148
  23.4 53.3 %all-to-all-start.1 = ((bf16[160,4,640]{2,0,1:T(8,128)(2,1)}), bf16[160,4,640]{2,0,1:T(8,128)(2,1)S(1)}, u32[]{:S(2)}, u32[]{:S(2)}) async-start(bf16[160,4,640]{2,0,1:T(8,128)(2,1)} %copy.23), calls=%async_computation.1 | async-start | bytes 1638400 | tf_op jit(solution)/shard_map/all_to_all | solution.py:157
  27.9 19.7 %collective-permute-start = (bf16[320,640]{1,0:T(8,128)(2,1)}, bf16[320,640]{1,0:T(8,128)(2,1)S(1)}, u32[]{:S(2)}, u32[]{:S(2)}) collective-permute-start(bf16[320,640]{1,0:T(8,128)(2,1)} %bitcast.5), channel_id=1, source_target_pairs={{0,4},{4,8},{8,12},{12,0},{1,5},{5,9},{9,13},{13,1},{2,6},{6,10},{... | collective-permute-start | bytes 1228808 | tf_op jit(solution)/shard_map/ppermute | solution.py:139
  35.3 33.1 %collective-permute-start.3 = (bf16[320,640]{1,0:T(8,128)(2,1)}, bf16[320,640]{1,0:T(8,128)(2,1)S(1)}, u32[]{:S(2)}, u32[]{:S(2)}) collective-permute-start(bf16[320,640]{1,0:T(8,128)(2,1)} %bitcast.6), channel_id=1, source_target_pairs={{0,12},{4,0},{8,4},{12,8},{1,13},{5,1},{9,5},{13,9},{2,14},{6,2},{... | collective-permute-start | bytes 1228808 | tf_op jit(solution)/shard_map/ppermute | solution.py:139
  39.1 38.2 %collective-permute-start.2 = (bf16[320,640]{1,0:T(8,128)(2,1)}, bf16[320,640]{1,0:T(8,128)(2,1)S(1)}, u32[]{:S(2)}, u32[]{:S(2)}) collective-permute-start(bf16[320,640]{1,0:T(8,128)(2,1)} %bitcast.5), channel_id=1, source_target_pairs={{0,12},{4,0},{8,4},{12,8},{1,13},{5,1},{9,5},{13,9},{2,14},{6,2},{... | collective-permute-start | bytes 1228808 | tf_op jit(solution)/shard_map/ppermute | solution.py:139
  43.3 34.0 %collective-permute-start.1 = (bf16[320,640]{1,0:T(8,128)(2,1)}, bf16[320,640]{1,0:T(8,128)(2,1)}, u32[]{:S(2)}, u32[]{:S(2)}) collective-permute-start(bf16[320,640]{1,0:T(8,128)(2,1)} %bitcast.6), channel_id=1, source_target_pairs={{0,4},{4,8},{8,12},{12,0},{1,5},{5,9},{9,13},{13,1},{2,6},{6,10},{... | collective-permute-start | bytes 1228808 | tf_op jit(solution)/shard_map/ppermute | solution.py:139
  47.5 36.0 %collective-permute-start.4 = (bf16[320,640]{1,0:T(8,128)(2,1)S(1)}, bf16[320,640]{1,0:T(8,128)(2,1)}, u32[]{:S(2)}, u32[]{:S(2)}) collective-permute-start(bf16[320,640]{1,0:T(8,128)(2,1)S(1)} %collective-permute-done.refs_3_), channel_id=1, source_target_pairs={{0,4},{4,8},{8,12},{12,0},{1,5},{5,9},{9,13},{13,1},{2,6},{6,10},{... | collective-permute-start | bytes 1228808 | tf_op jit(solution)/shard_map/ppermute | solution.py:139
  68.4 17.8 %collective-permute-start.5 = (bf16[320,640]{1,0:T(8,128)(2,1)S(1)}, bf16[320,640]{1,0:T(8,128)(2,1)}, u32[]{:S(2)}, u32[]{:S(2)}) collective-permute-start(bf16[320,640]{1,0:T(8,128)(2,1)S(1)} %collective-permute-done.3.refs_6_), channel_id=1, source_target_pairs={{0,12},{4,0},{8,4},{12,8},{1,13},{5,1},{9,5},{13,9},{2,14},{6,2},{... | collective-permute-start | bytes 1228808 | tf_op jit(solution)/shard_map/ppermute | solution.py:139
  76.7 24.3 %copy-start = (f32[640,160]{1,0:T(8,128)}, f32[640,160]{1,0:T(8,128)S(1)}, u32[]{:S(2)}) copy-start(f32[640,160]{1,0:T(8,128)S(1)} %fusion.refs_10_.refs_1_) | copy-start | bytes 1228804
  86.2 1.9 copy-start.1
  100.9 3.8 %collective-permute-start.6 = (f32[4,80,160]{2,1,0:T(8,128)S(1)}, f32[4,80,160]{2,1,0:T(8,128)S(1)}, u32[]{:S(2)}, u32[]{:S(2)}) collective-permute-start(f32[4,80,160]{2,1,0:T(8,128)S(1)} %get-tuple-element.6), channel_id=1, source_target_pairs={{0,16},{16,0},{1,17},{17,1},{2,18},{18,2},{3,19},{19,3},{4,20},{20... | collective-permute-start | bytes 614408 | tf_op jit(solution)/shard_map/ppermute | solution.py:139
  145.8 12.9 %all-to-all-start.5 = ((bf16[4,160,640]{2,1,0:T(8,128)(2,1)}), bf16[4,160,640]{2,1,0:T(8,128)(2,1)S(1)}, u32[]{:S(2)}, u32[]{:S(2)}) async-start(bf16[4,160,640]{2,1,0:T(8,128)(2,1)} %bitcast.13), calls=%async_computation.5 | async-start | bytes 1638400 | tf_op jit(solution)/shard_map/all_to_all | solution.py:163
  159.4 13.7 %all-to-all-start.4 = ((f32[16,20,160]{2,1,0:T(8,128)}), f32[16,20,160]{2,1,0:T(8,128)S(1)}, u32[]{:S(2)}, u32[]{:S(2)}) async-start(f32[16,20,160]{2,1,0:T(8,128)} %broadcast_in_dim.27), calls=%async_computation.4 | async-start | bytes 786432 | tf_op jit(solution)/shard_map/all_to_all | solution.py:172
Sparse Core Ops, SparseCore 0:
  10.1 56.5 all-gather.2

commit v2 on v0

v2 whole, which is shorter than its diff:
```python
import math

import jax
import jax.numpy as jnp
from jax import lax
from jax.experimental import pallas as pl
from jax.experimental.pallas import tpu as pltpu
from jax.sharding import Mesh, PartitionSpec as P

GROUP = 64
KEEP = 16
BETA = 0.999
SIDE = 4
STEPS = 2
LANES = 128

REP = ("ylo", "z", "core")
FSDP = ("yhi", "x")

SMEM = pl.BlockSpec(memory_space=pltpu.SMEM)
VMEM = pl.BlockSpec(memory_space=pltpu.VMEM)
HBM = pl.BlockSpec(memory_space=pltpu.HBM)


def room(mebibytes):
    return pltpu.CompilerParams(vmem_limit_bytes=mebibytes * 1024 * 1024)


def basis_table(kept):
    freq = kept.astype(jnp.float32)
    points = jnp.arange(GROUP, dtype=jnp.float32) + 0.5
    weight = jnp.where(kept == 0, math.sqrt(1.0 / GROUP), math.sqrt(2.0 / GROUP)).astype(
        jnp.float32
    )
    return weight[None, :] * jnp.cos(math.pi * points[:, None] * freq[None, :] / GROUP)


def cost(flops, *arrays):
    return pl.CostEstimate(
        flops=flops, bytes_accessed=sum(a.size * a.dtype.itemsize for a in arrays), transcendentals=0
    )


def two_parts(x):
    high = x.astype(jnp.bfloat16)
    return high, (x - high.astype(jnp.float32)).astype(jnp.bfloat16)


def dot_parts(a, b, dims):
    def one(x, y):
        return lax.dot_general(x, y, (dims, ((), ())), preferred_element_type=jnp.float32)

    return one(a[0], b[0]) + (one(a[0], b[1]) + one(a[1], b[0]))


def quarter_kernel(where_ref, grad_ref, out_ref):
    width = out_ref.shape[1]
    at = where_ref[0] * width
    out_ref[...] = grad_ref[:, pl.ds(pl.multiple_of(at, width), width)]


def quarter(where, whole):
    rows, width = whole.shape
    out = jax.ShapeDtypeStruct((rows, width // SIDE), whole.dtype)
    return pl.pallas_call(
        quarter_kernel,
        in_specs=[SMEM, VMEM],
        out_specs=VMEM,
        out_shape=out,
        compiler_params=room(4),
        cost_estimate=cost(0, out, out),
    )(where, whole)


def pack_kernel(whole_ref, out_ref):
    width = out_ref.shape[2]
    for q in range(SIDE):
        out_ref[q] = whole_ref[:, q * width : (q + 1) * width]


def pack(whole, weight=1):
    rows, width = whole.shape
    out = jax.ShapeDtypeStruct((SIDE, rows, width // SIDE), whole.dtype)
    return pl.pallas_call(
        pack_kernel,
        in_specs=[VMEM],
        out_specs=VMEM,
        out_shape=out,
        compiler_params=room(4),
        cost_estimate=cost(0, *[out] * weight),
    )(whole)


def others_kernel(where_ref, all_ref, out_ref):
    rows = all_ref.shape[1]
    for n in range(SIDE - 1):
        out_ref[n * rows : (n + 1) * rows] = all_ref[lax.rem(where_ref[0] + n + 1, SIDE)]


def others(where, every):
    _, toks, width = every.shape
    return pl.pallas_call(
        others_kernel,
        in_specs=[SMEM, VMEM],
        out_specs=VMEM,
        out_shape=jax.ShapeDtypeStruct(((SIDE - 1) * toks, width), every.dtype),
        compiler_params=room(4),
        cost_estimate=cost(0, every, every),
    )(where, every)


def rows_in_order(where_ref, piece_refs, block, sems):
    each = block.shape[0] // SIDE
    copies = []
    row = 0
    for piece_ref in piece_refs:
        start = row
        while row < start + piece_ref.shape[0]:
            n, skip = divmod(row, each)
            size = min(each - skip, start + piece_ref.shape[0] - row)
            at = pl.multiple_of(lax.rem(where_ref[0] + n, SIDE) * each + skip, each // 2)
            copies.append(
                pltpu.make_async_copy(
                    piece_ref.at[pl.ds(row - start, size)], block.at[pl.ds(at, size)], sems.at[len(copies)]
                )
            )
            row += size
    return copies


def acts_columns(where_ref, shift, acts_ref, depth):
    at = lax.rem(where_ref[1] + shift, SIDE) * depth
    return acts_ref.at[:, pl.ds(pl.multiple_of(at, depth), depth)]


def near_kernel(scale, where_ref, acts_ref, mom_ref, table_ref, *rest):
    pieces, rest = rest[:6], rest[6:]
    part_ref, coeff_ref, high_ref, low_ref, grad_block, sems = rest
    depth = grad_block.shape[0] // 3

    @pl.when(pl.program_id(0) == 0)
    def _():
        copies = []
        for n in range(3):
            block = grad_block.at[n * depth : (n + 1) * depth]
            copies += rows_in_order(where_ref, pieces[2 * n : 2 * n + 2], block, sems.at[n])
        for copy in copies:
            copy.start()
        rows, coefs = high_ref.shape
        table = jnp.concatenate([table_ref[...]] * (rows // GROUP), 0)
        row = lax.broadcasted_iota(jnp.int32, (rows, coefs), 0) // GROUP
        col = lax.broadcasted_iota(jnp.int32, (rows, coefs), 1) // KEEP
        high_ref[...], low_ref[...] = two_parts(jnp.where(row == col, table, 0.0))
        for copy in copies:
            copy.wait()

    total = None
    for n, shift in enumerate((0, 3, 1)):
        at = pl.multiple_of(lax.rem(where_ref[1] + shift, SIDE) * depth, depth)
        term = jnp.dot(
            acts_ref[:, pl.ds(at, depth)], grad_block[n * depth : (n + 1) * depth],
            preferred_element_type=jnp.float32,
        )
        total = term if total is None else total + term
    part = BETA * mom_ref[...].astype(jnp.float32) + total * scale
    part_ref[...] = part
    coeff_ref[...] = dot_parts(two_parts(part), (high_ref[...], low_ref[...]), ((1,), (0,)))


def near(scale, where, acts, mom, table, pieces, weight=1):
    feats, toks = acts.shape
    rows = feats // STEPS
    outs = pieces[0].shape[1]
    coefs = table.shape[1]
    part = jax.ShapeDtypeStruct((feats, outs), jnp.float32)
    coeff = jax.ShapeDtypeStruct((feats, coefs), jnp.float32)
    basis = jax.ShapeDtypeStruct((outs, coefs), jnp.bfloat16)
    some = pl.BlockSpec((rows, outs), lambda p, w: (p, 0))
    whole = pl.BlockSpec(basis.shape, lambda p, w: (0, 0))
    return pl.pallas_call(
        lambda *refs: near_kernel(scale, *refs),
        grid_spec=pltpu.PrefetchScalarGridSpec(
            num_scalar_prefetch=1,
            grid=(STEPS,),
            in_specs=[
                pl.BlockSpec((rows, toks), lambda p, w: (p, 0)),
                some,
                pl.BlockSpec(table.shape, lambda p, w: (0, 0)),
                *[HBM] * len(pieces),
            ],
            out_specs=[some, pl.BlockSpec((rows, coefs), lambda p, w: (p, 0)), whole, whole],
            scratch_shapes=[
                pltpu.VMEM((3 * toks // SIDE, outs), jnp.bfloat16),
                pltpu.SemaphoreType.DMA((3, SIDE)),
            ],
        ),
        out_shape=[part, coeff, basis, basis],
        compiler_params=room(60),
        cost_estimate=cost(weight * 3 * feats * toks * outs // 2, acts, part, *pieces),
    )(where, acts, mom, table, *pieces)


def packed(coeff, rows):
    wide = coeff.shape[1] - LANES
    rest = [coeff[n : n + 8, LANES:] for n in range(0, coeff.shape[0], 8)]
    rest += [jnp.zeros_like(rest[0])] * (-len(rest) % (LANES // wide))
    tiles = [
        jnp.concatenate(rest[n : n + LANES // wide], 1) for n in range(0, len(rest), LANES // wide)
    ]
    blank = jnp.zeros((rows - coeff.shape[0] - 8 * len(tiles), LANES), coeff.dtype)
    return jnp.concatenate([coeff[:, :LANES], *tiles, blank], 0)


def unpacked(tiles, rows, coefs):
    wide = coefs - LANES
    rest = []
    for n in range(rows // 8):
        row, lane = rows + 8 * (n // (LANES // wide)), wide * (n % (LANES // wide))
        rest.append(tiles[row : row + 8, lane : lane + wide])
    return jnp.concatenate([tiles[:rows], jnp.concatenate(rest, 0)], 1)


def far_kernel(
    scale, where_ref, acts_ref, near_ref, high_ref, low_ref, p0_ref, p1_ref, p2_ref, p3_ref,
    coeff_ref, packed_ref, acts_block, grad_block, sems,
):
    depth = grad_block.shape[0]
    copies = rows_in_order(where_ref, (p0_ref, p1_ref, p2_ref, p3_ref), grad_block, sems)
    last = pltpu.make_async_copy(
        acts_columns(where_ref, 2, acts_ref, depth), acts_block, sems.at[6]
    )
    for copy in [*copies, last]:
        copy.start()
    for copy in copies:
        copy.wait()

    def dot(a, b):
        return jnp.dot(a, b, preferred_element_type=jnp.float32)

    grad = grad_block[...]
    high, low = two_parts(dot(grad, high_ref[...]) + dot(grad, low_ref[...]))
    last.wait()
    acts = acts_block[...]
    coeff = near_ref[...] + (dot(acts, high) + dot(acts, low)) * scale
    coeff_ref[...] = coeff
    count, rows, _ = packed_ref.shape
    each = coeff.shape[0] // count
    for n in range(count):
        packed_ref[n] = packed(coeff[n * each : (n + 1) * each], rows)


def far(scale, where, acts, coeff, high, low, pieces):
    outs, coefs = high.shape
    feats = acts.shape[0]
    depth = acts.shape[1] // SIDE
    out = jax.ShapeDtypeStruct((16, 64, LANES), jnp.float32)
    return pl.pallas_call(
        lambda *refs: far_kernel(scale, *refs),
        in_specs=[SMEM, HBM] + [VMEM] * 3 + [HBM] * len(pieces),
        out_specs=[VMEM] * 2,
        out_shape=[jax.ShapeDtypeStruct(coeff.shape, coeff.dtype), out],
        scratch_shapes=[
            pltpu.VMEM((feats, depth), jnp.bfloat16),
            pltpu.VMEM((depth, outs), jnp.bfloat16),
            pltpu.SemaphoreType.DMA((8,)),
        ],
        compiler_params=room(14),
        cost_estimate=cost(4 * coefs * depth * (feats + outs), acts, coeff, out, *pieces),
    )(where, acts, coeff, high, low, *pieces)


def residual_kernel(
    scale, where_ref, acts_ref, part_ref, coeff_ref, high_ref, low_ref, p0_ref, p1_ref, p2_ref, p3_ref,
    *refs,
):
    outs, (acts_block, grad_block, part_block, sems) = refs[:SIDE], refs[SIDE:]
    x = where_ref[0]
    depth = grad_block.shape[0]
    copies = rows_in_order(where_ref, (p0_ref, p1_ref, p2_ref, p3_ref), grad_block, sems)
    copies.append(
        pltpu.make_async_copy(acts_columns(where_ref, 2, acts_ref, depth), acts_block, sems.at[6])
    )
    copies.append(pltpu.make_async_copy(part_ref, part_block, sems.at[7]))
    for copy in copies:
        copy.start()
    basis = (high_ref[...], low_ref[...])
    kept = dot_parts(two_parts(coeff_ref[...]), basis, ((1,), (1,)))
    for copy in copies:
        copy.wait()
    term = jnp.dot(acts_block[...], grad_block[...], preferred_element_type=jnp.float32)
    part_block[...] = (part_block[...] + term * scale) - kept
    rows = outs[0].shape[0]
    for shift, out_ref in enumerate(outs):
        at = pl.multiple_of(lax.rem(x + shift, SIDE) * rows, rows)
        out_ref[...] = part_block[pl.ds(at, rows), :].astype(jnp.bfloat16)


def residual(scale, where, acts, part, coeff, high, low, pieces):
    feats, outs = part.shape
    depth = acts.shape[1] // SIDE
    fresh = jax.ShapeDtypeStruct((feats // SIDE, outs), jnp.bfloat16)
    return pl.pallas_call(
        lambda *refs: residual_kernel(scale, *refs),
        in_specs=[SMEM] + [HBM] * 2 + [VMEM] * 3 + [HBM] * len(pieces),
        out_specs=[VMEM] * SIDE,
        out_shape=[fresh] * SIDE,
        scratch_shapes=[
            pltpu.VMEM((feats, depth), jnp.bfloat16),
            pltpu.VMEM((depth, outs), jnp.bfloat16),
            pltpu.VMEM(part.shape, part.dtype),
            pltpu.SemaphoreType.DMA((8,)),
        ],
        compiler_params=room(60),
        cost_estimate=cost(feats * outs * (2 * depth + 960), part, coeff, *[fresh] * SIDE),
    )(where, acts, part, coeff, high, low, *pieces)


def finish_kernel(replicas, where_ref, total_ref, high_ref, low_ref, *refs):
    pieces, (update_ref, fresh_ref) = refs[:SIDE], refs[SIDE:]
    x = where_ref[0]
    rows, width = pieces[0].shape
    coefs = high_ref.shape[1]
    basis = (high_ref[...], low_ref[...])
    for q, piece_ref in enumerate(pieces):
        at = pl.multiple_of(lax.rem(x + SIDE - q, SIDE) * width, width)
        fresh_ref[:, pl.ds(at, width)] = piece_ref[...]
        quarters = []
        for ylo in range(2):
            for core in range(2):
                tiles = jnp.concatenate([total_ref[core, ylo, q, 0], total_ref[core, ylo, q, 1]], 0)
                quarters.append(unpacked(tiles, rows // 4, coefs))
        mean = two_parts(jnp.concatenate(quarters, 0) / replicas)
        update_ref[:, q * width : (q + 1) * width] = dot_parts(mean, basis, ((1,), (1,))).astype(
            jnp.bfloat16
        )


def finish(replicas, where, total, high, low, pieces):
    rows, width = pieces[0].shape
    out = jax.ShapeDtypeStruct((rows, SIDE * width), jnp.bfloat16)
    return pl.pallas_call(
        lambda *refs: finish_kernel(replicas, *refs),
        in_specs=[SMEM] + [VMEM] * (3 + SIDE),
        out_specs=[VMEM] * 2,
        out_shape=[out, out],
        compiler_params=room(8),
        cost_estimate=cost(6 * total.size * width, total, out, out, out),
    )(where, total, high, low, *pieces)


def shifted(x, axis, by):
    return lax.ppermute(x, axis, [(i, (i + by) % SIDE) for i in range(SIDE)])


def per_device(attn_out, out_grad, momentum, kept):
    replicas = 32
    scale = 1.0 / math.sqrt(attn_out.shape[0])
    toks, width = out_grad.shape
    where = jnp.stack([lax.axis_index("x"), lax.axis_index("yhi")]).astype(jnp.int32)

    acts = lax.all_gather(attn_out.T, "x", axis=0, tiled=True)
    first = quarter(where, out_grad)
    up, down = [shifted(first, "yhi", 1)], [shifted(first, "yhi", -1)]
    every = lax.all_to_all(pack(out_grad), "x", 0, 0, tiled=True)
    every, up[0], down[0] = lax.optimization_barrier((every, up[0], down[0]))
    rest = others(where, every)
    stored, rest = lax.optimization_barrier((momentum[0], rest))
    mom = lax.all_to_all(pack(stored, 60), "x", 0, 0, tiled=True).reshape(SIDE * toks, width // SIDE)
    own = [first, rest]
    up.append(shifted(rest, "yhi", 1))
    down.append(shifted(rest, "yhi", -1))
    over = []
    for above, below in zip(up, down):
        middle = above.shape[0] // 2
        over.append(shifted(above[:middle], "yhi", 1))
        over.append(shifted(below[middle:], "yhi", -1))

    table = basis_table(jnp.tile(kept, width // SIDE // GROUP))
    part, coeff, high, low = near(scale, where, acts, mom, table, own + up + down, 20)
    coeff, pieces = far(scale, where, acts, coeff, high, low, over)
    fresh = residual(scale, where, acts, part, coeff, high, low, over)

    tile = pieces.shape[1:]
    pieces = lax.all_to_all(pieces, ("x", "ylo", "core"), 0, 0, tiled=True)
    summed = pieces.reshape(4, 4, *tile).sum(1)
    tile = (tile[0] // 2, tile[1])
    summed, *fresh = lax.optimization_barrier((summed, *fresh))
    pieces = lax.all_to_all(summed.reshape(8, *tile), "z", 0, 0, tiled=True)
    summed = pieces.sum(0)
    spread = jnp.broadcast_to(summed[None], (16, *tile))
    spread = lax.all_to_all(spread, ("ylo", "z"), 0, 0, tiled=True)
    total = lax.all_gather(spread, "core", axis=0).reshape(2, 2, 4, 2, *tile)
    fresh = [fresh[0]] + [shifted(fresh[s], "x", s) for s in (1, 2, 3)]
    update, new_momentum = finish(
        replicas, where, total, high, low, fresh
    )
    return update, new_momentum[None]


def solution(mesh):
    fine = Mesh(mesh.devices.reshape(2, 8, 2, 4, 4), ("ylo", "z", "core", "yhi", "x"))
    return jax.shard_map(
        per_device,
        mesh=fine,
        in_specs=(P(REP, FSDP), P(REP + FSDP, None), P(REP, FSDP, None), P()),
        out_specs=(P(FSDP, None), P(REP, FSDP, None)),
        check_vma=False,
    )
```

time: 440 us -> 162 us (0.37)
  the two profiles are of different devices: /device:TPU:1 before, /device:TPU:8 now
where the time goes in v2:
time: 162 us; the launch traced here: 161 us
  starting transfers between devices  68.9 us (43%)
  Pallas kernels  26.6 us (16%)
  waiting for transfers between devices  20.3 us (13%)
  blocking collectives  19.5 us (12%)
  between operations  14.4 us (9%)
  local copies, waits for them, and re-layouts  10.1 us (6%)
    ppermute x11, starting transfers between devices, shifted(): return lax.ppermute(x, axis, [(i, (i + by) % SIDE) for i in range(SIDE)])  50.6 us
    all_to_all x1, blocking collectives, per_device(): pieces = lax.all_to_all(summed.reshape(8, *tile), 'z', 0, 0, tiled=True)  17.3 us
    ppermute x11, waiting for transfers between devices, shifted(): return lax.ppermute(x, axis, [(i, (i + by) % SIDE) for i in range(SIDE)])  15.5 us
    pallas_call x1, Pallas kernels, near(): pl.pallas_call(lambda *refs: near_kernel(scale, *refs), grid_spec=pltpu.P...  9.65 us
    unnamed x46, local copies, waits for them, and re-layouts  6.82 us
    pallas_call x1, Pallas kernels, residual(): pl.pallas_call(lambda *refs: residual_kernel(scale, *refs), in_specs=[SME...  5.66 us
    pallas_call x1, Pallas kernels, far(): pl.pallas_call(lambda *refs: far_kernel(scale, *refs), in_specs=[SMEM, HB...  5.21 us
    all_to_all x1, starting transfers between devices, per_device(): pieces = lax.all_to_all(pieces, ('x', 'ylo', 'core'), 0, 0, tiled=True)  5.15 us
  transfers between devices with their start and end apart: 16, of which 5 were waited for; matrix products, arithmetic and copies ran while one was open for 2% of the time, Pallas kernels for 11%

profile of v2, /device:TPU:8, one launch (start us, length us, event | category | flops | bytes accessed | tf_op | source)
XLA Modules:
  0.0 160.9 jit_solution(8085452023731547)
XLA Ops:
  10.0 4.3 %all-to-all-start = ((bf16[4,160,640]{2,1,0:T(8,128)(2,1)}), bf16[4,160,640]{2,1,0:T(8,128)(2,1)S(1)}, u32[]{:S(2)}, u32[]{:S(2)}) async-start(bf16[4,160,640]{2,1,0:T(8,128)(2,1)} %shard_map.59), calls=%async_computation | async-start | bytes 1638400 | tf_op jit(solution)/shard_map/all_to_all | solution.py:364
  15.0 4.5 %collective-permute-start = (bf16[160,640]{1,0:T(8,128)(2,1)S(1)}, bf16[160,640]{1,0:T(8,128)(2,1)S(1)}, u32[]{:S(2)}, u32[]{:S(2)}) collective-permute-start(bf16[160,640]{1,0:T(8,128)(2,1)S(1)} %shard_map.60.refs_4_), channel_id=1, source_target_pairs={{0,4},{4,8},{8,12},{12,0},{1,5},{5,9},{9,13},{13,1},{2,6},{6,10},{... | collective-permute-start | bytes 614408 | tf_op jit(solution)/shard_map/ppermute | solution.py:352
  19.5 3.5 %collective-permute-start.1 = (bf16[160,640]{1,0:T(8,128)(2,1)S(1)}, bf16[160,640]{1,0:T(8,128)(2,1)S(1)}, u32[]{:S(2)}, u32[]{:S(2)}) collective-permute-start(bf16[160,640]{1,0:T(8,128)(2,1)S(1)} %shard_map.60.refs_4_), channel_id=1, source_target_pairs={{0,12},{4,0},{8,4},{12,8},{1,13},{5,1},{9,5},{13,9},{2,14},{6,2},{... | collective-permute-start | bytes 614408 | tf_op jit(solution)/shard_map/ppermute | solution.py:352
  22.9 5.8 %collective-permute-done.refs_6_ = bf16[160,640]{1,0:T(8,128)(2,1)S(1)} collective-permute-done((bf16[160,640]{1,0:T(8,128)(2,1)S(1)}, bf16[160,640]{1,0:T(8,128)(2,1)S(1)}, u32[]{:S(2)}, u32[]{:S(2)}) %collective-permute-start) | collective-permute-done | bytes 204832 | tf_op jit(solution)/shard_map/ppermute | solution.py:352
  30.4 9.1 %collective-permute-start.2 = (bf16[480,640]{1,0:T(8,128)(2,1)S(1)}, bf16[480,640]{1,0:T(8,128)(2,1)S(1)}, u32[]{:S(2)}, u32[]{:S(2)}) collective-permute-start(bf16[480,640]{1,0:T(8,128)(2,1)S(1)} %shard_map.61.refs_5_), channel_id=1, source_target_pairs={{0,4},{4,8},{8,12},{12,0},{1,5},{5,9},{9,13},{13,1},{2,6},{6,10},{... | collective-permute-start | bytes 1843208 | tf_op jit(solution)/shard_map/ppermute | solution.py:352
  39.4 1.9 %collective-permute-start.3 = (bf16[480,640]{1,0:T(8,128)(2,1)S(1)}, bf16[480,640]{1,0:T(8,128)(2,1)}, u32[]{:S(2)}, u32[]{:S(2)}) collective-permute-start(bf16[480,640]{1,0:T(8,128)(2,1)S(1)} %shard_map.61.refs_5_), channel_id=1, source_target_pairs={{0,12},{4,0},{8,4},{12,8},{1,13},{5,1},{9,5},{13,9},{2,14},{6,2},{... | collective-permute-start | bytes 1843208 | tf_op jit(solution)/shard_map/ppermute | solution.py:352
  42.3 4.5 %all-to-all-start.1 = ((bf16[4,160,640]{2,1,0:T(8,128)(2,1)}), bf16[4,160,640]{2,1,0:T(8,128)(2,1)S(1)}, u32[]{:S(2)}, u32[]{:S(2)}) async-start(bf16[4,160,640]{2,1,0:T(8,128)(2,1)} %shard_map.62), calls=%async_computation.1 | async-start | bytes 1638400 | tf_op jit(solution)/shard_map/all_to_all | solution.py:368
  48.0 4.8 %collective-permute-start.4 = (bf16[80,640]{1,0:T(8,128)(2,1)S(1)}, bf16[80,640]{1,0:T(8,128)(2,1)S(1)}, u32[]{:S(2)}, u32[]{:S(2)}) collective-permute-start(bf16[80,640]{1,0:T(8,128)(2,1)S(1)} %slice.12), channel_id=1, source_target_pairs={{0,4},{4,8},{8,12},{12,0},{1,5},{5,9},{9,13},{13,1},{2,6},{6,10},{... | collective-permute-start | bytes 307208 | tf_op jit(solution)/shard_map/ppermute | solution.py:352
  53.5 3.1 %collective-permute-start.5 = (bf16[80,640]{1,0:T(8,128)(2,1)}, bf16[80,640]{1,0:T(8,128)(2,1)S(1)}, u32[]{:S(2)}, u32[]{:S(2)}) collective-permute-start(bf16[80,640]{1,0:T(8,128)(2,1)} %slice.13), channel_id=1, source_target_pairs={{0,12},{4,0},{8,4},{12,8},{1,13},{5,1},{9,5},{13,9},{2,14},{6,2},{... | collective-permute-start | bytes 307208 | tf_op jit(solution)/shard_map/ppermute | solution.py:352
  56.7 13.2 %collective-permute-start.6 = (bf16[240,640]{1,0:T(8,128)(2,1)S(1)}, bf16[240,640]{1,0:T(8,128)(2,1)}, u32[]{:S(2)}, u32[]{:S(2)}) collective-permute-start(bf16[240,640]{1,0:T(8,128)(2,1)S(1)} %slice.16), channel_id=1, source_target_pairs={{0,4},{4,8},{8,12},{12,0},{1,5},{5,9},{9,13},{13,1},{2,6},{6,10},{... | collective-permute-start | bytes 921608 | tf_op jit(solution)/shard_map/ppermute | solution.py:352
  74.5 9.7 %shard_map.63 = (f32[640,640]{1,0:T(8,128)}, f32[640,160]{1,0:T(8,128)}, bf16[640,160]{1,0:T(8,128)(2,1)}, bf16[640,160]{1,0:T(8,128)(2,1)}) custom-call(s32[2]{0:T(128)} %copy-done.15, bf16[640,2560]{1,0:T(8,128)(2,1)} %all-gather.3.cloned.1.call-done.refs_1_, bf16[640,640]{1,0:T(8,128)(2,1)} %bitcast.13, f32[64,160]{1,0:T(8,128)} %cosine_multiply_fusion.refs_3_, ...), custom_call_target="tpu_custom_call" | custom-call | flops 31457280000 | bytes 7372800 | tf_op jit(solution)/shard_map/pallas_call | solution.py:180
  84.2 3.5 %collective-permute-done.7.refs_8_.refs_9_ = bf16[240,640]{1,0:T(8,128)(2,1)} collective-permute-done((bf16[240,640]{1,0:T(8,128)(2,1)}, bf16[240,640]{1,0:T(8,128)(2,1)}, u32[]{:S(2)}, u32[]{:S(2)}) %collective-permute-start.7) | collective-permute-done | bytes 307232 | tf_op jit(solution)/shard_map/ppermute | solution.py:352
  90.8 5.2 %shard_map.64 = (f32[640,160]{1,0:T(8,128)S(1)}, f32[16,64,128]{2,1,0:T(8,128)}) custom-call(s32[2]{0:T(128)S(1)} %copy-done.16, bf16[640,2560]{1,0:T(8,128)(2,1)S(1)} %copy-done, f32[640,160]{1,0:T(8,128)S(1)} %copy-done.9, bf16[640,160]{1,0:T(8,128)(2,1)S(1)} %copy-done.3, bf16[640,160]{1,0:T(8,128)(2,1)S(1)} %copy-done.5, ...), custom_call_target="tpu_custom_call" | custom-call | flops 524288000 | bytes 5029888 | tf_op jit(solution)/shard_map/pallas_call | solution.py:257
  96.8 5.2 %all-to-all-start.2 = ((f32[16,64,128]{2,1,0:T(8,128)}), f32[16,64,128]{2,1,0:T(8,128)S(1)}, u32[]{:S(2)}, u32[]{:S(2)}) async-start(f32[16,64,128]{2,1,0:T(8,128)} %get-tuple-element.32), calls=%async_computation.2 | async-start | bytes 1048576 | tf_op jit(solution)/shard_map/all_to_all | solution.py:384
  102.0 5.7 %shard_map.65 = (bf16[160,640]{1,0:T(8,128)(2,1)}, bf16[160,640]{1,0:T(8,128)(2,1)}, bf16[160,640]{1,0:T(8,128)(2,1)}, bf16[160,640]{1,0:T(8,128)(2,1)}) custom-call(s32[2]{0:T(128)} %copy-done.15, bf16[640,2560]{1,0:T(8,128)(2,1)} %all-gather.3.cloned.1.call-done.refs_1_, f32[640,640]{1,0:T(8,128)} %get-tuple-element.33.refs_2_, f32[640,160]{1,0:T(8,128)} %copy-done.8, ...), custom_call_target="tpu_custom_call" | custom-call | flops 917504000 | bytes 2867200 | tf_op jit(solution)/shard_map/pallas_call | solution.py:302
  107.7 4.0 %all-to-all-done.2 = f32[16,64,128]{2,1,0:T(8,128)S(1)} async-done(((f32[16,64,128]{2,1,0:T(8,128)}), f32[16,64,128]{2,1,0:T(8,128)S(1)}, u32[]{:S(2)}, u32[]{:S(2)}) %all-to-all-start.2) | async-done | bytes 524320 | tf_op jit(solution)/shard_map/all_to_all | solution.py:384
  111.7 17.3 %all_to_all.25 = f32[8,32,128]{2,1,0:T(8,128)S(1)} all-to-all(f32[8,32,128]{2,1,0:T(8,128)S(1)} %bitcast.14), channel_id=1, replica_groups=mesh['ylo'=2,'z'=8,'core'=2,'yhi'=4,'x'=4] {'z'}, dimensions={0} | all-to-all | bytes 262144 | tf_op jit(solution)/shard_map/all_to_all | solution.py:388
  129.8 4.3 %all-to-all-start.4 = ((f32[16,32,128]{2,1,0:T(8,128)}), f32[16,32,128]{2,1,0:T(8,128)S(1)}, u32[]{:S(2)}, u32[]{:S(2)}) async-start(f32[16,32,128]{2,1,0:T(8,128)} %broadcast_in_dim.22), calls=%async_computation.4 | async-start | bytes 524288 | tf_op jit(solution)/shard_map/all_to_all | solution.py:391
  134.1 2.7 %collective-permute-start.10 = (bf16[160,640]{1,0:T(8,128)(2,1)}, bf16[160,640]{1,0:T(8,128)(2,1)S(1)}, u32[]{:S(2)}, u32[]{:S(2)}) collective-permute-start(bf16[160,640]{1,0:T(8,128)(2,1)} %get-tuple-element.43), channel_id=1, source_target_pairs={{0,3},{1,0},{2,1},{3,2},{4,7},{5,4},{6,5},{7,6},{8,11},{9,8},{10,9... | collective-permute-start | bytes 614408 | tf_op jit(solution)/shard_map/ppermute | solution.py:352
  136.8 3.1 %collective-permute-start.8 = (bf16[160,640]{1,0:T(8,128)(2,1)}, bf16[160,640]{1,0:T(8,128)(2,1)S(1)}, u32[]{:S(2)}, u32[]{:S(2)}) collective-permute-start(bf16[160,640]{1,0:T(8,128)(2,1)} %get-tuple-element.41), channel_id=1, source_target_pairs={{0,1},{1,2},{2,3},{3,0},{4,5},{5,6},{6,7},{7,4},{8,9},{9,10},{10,1... | collective-permute-start | bytes 614408 | tf_op jit(solution)/shard_map/ppermute | solution.py:352
  139.9 2.8 %collective-permute-start.9 = (bf16[160,640]{1,0:T(8,128)(2,1)}, bf16[160,640]{1,0:T(8,128)(2,1)S(1)}, u32[]{:S(2)}, u32[]{:S(2)}) collective-permute-start(bf16[160,640]{1,0:T(8,128)(2,1)} %get-tuple-element.42), channel_id=1, source_target_pairs={{0,2},{1,3},{2,0},{3,1},{4,6},{5,7},{6,4},{7,5},{8,10},{9,11},{10,... | collective-permute-start | bytes 614408 | tf_op jit(solution)/shard_map/ppermute | solution.py:352
  142.7 2.2 %all-gather = f32[32,32,128]{2,1,0:T(8,128)S(1)} all-gather(f32[16,32,128]{2,1,0:T(8,128)S(1)} %all-to-all-done.4), channel_id=2, replica_groups=mesh['ylo'=2,'z'=8,'core'=2,'yhi'=4,'x'=4] {'core'}, dimensions={0}, use_global_device_ids=true | all-gather | bytes 786432 | tf_op jit(solution)/shard_map/all_gather | solution.py:392
  144.9 5.2 %collective-permute-done.8.refs_5_ = bf16[160,640]{1,0:T(8,128)(2,1)S(1)} collective-permute-done((bf16[160,640]{1,0:T(8,128)(2,1)}, bf16[160,640]{1,0:T(8,128)(2,1)S(1)}, u32[]{:S(2)}, u32[]{:S(2)}) %collective-permute-start.8) | collective-permute-done | bytes 204832 | tf_op jit(solution)/shard_map/ppermute | solution.py:352
  151.0 3.0 %shard_map.66 = (bf16[160,2560]{1,0:T(8,128)(2,1)}, bf16[160,2560]{1,0:T(8,128)(2,1)}) custom-call(s32[2]{0:T(128)S(1)} %copy-done.17, f32[2,2,4,2,32,128]{5,4,3,2,1,0:T(8,128)S(1)} %bitcast.10, bf16[640,160]{1,0:T(8,128)(2,1)S(1)} %copy-done.4, bf16[640,160]{1,0:T(8,128)(2,1)S(1)} %copy-done.6, bf16[160,640]{1,0:T(8,128)(2,1)S(1)} %copy-done.14, ...), custom_call_target="tpu_custom_call" | custom-call | flops 503316480 | bytes 2981888 | tf_op jit(solution)/shard_map/pallas_call | solution.py:341
  (81 shorter events, 18.0 us)
Async XLA Ops:
  7.2 66.5 %all-gather.3.cloned.1.call-start = ((), (), s32[]{:S(2)}) async-start(), calls=%async_computation.5 | async-start | bytes 4096000 | tf_op jit(solution)/shard_map/all_gather | solution.py:361
  10.0 19.7 %all-to-all-start = ((bf16[4,160,640]{2,1,0:T(8,128)(2,1)}), bf16[4,160,640]{2,1,0:T(8,128)(2,1)S(1)}, u32[]{:S(2)}, u32[]{:S(2)}) async-start(bf16[4,160,640]{2,1,0:T(8,128)(2,1)} %shard_map.59), calls=%async_computation | async-start | bytes 1638400 | tf_op jit(solution)/shard_map/all_to_all | solution.py:364
  14.3 32.6 %copy-start.22 = (s32[16]{0:T(128)S(1)}, s32[16]{0:T(128)}, u32[]{:S(2)}) copy-start(s32[16]{0:T(128)} %param.7) | copy-start | bytes 196
  14.4 42.3 %copy-start.15 = (s32[2]{0:T(128)}, s32[2]{0:T(128)S(1)}, u32[]{:S(2)}) copy-start(s32[2]{0:T(128)S(1)} %pad_add_fusion.where_ref.refs_0_) | copy-start | bytes 28
  15.0 59.5 %copy-start.13 = (bf16[160,640]{1,0:T(8,128)(2,1)}, bf16[160,640]{1,0:T(8,128)(2,1)S(1)}, u32[]{:S(2)}) copy-start(bf16[160,640]{1,0:T(8,128)(2,1)S(1)} %shard_map.60.refs_4_) | copy-start | bytes 614404
  15.0 13.8 %collective-permute-start = (bf16[160,640]{1,0:T(8,128)(2,1)S(1)}, bf16[160,640]{1,0:T(8,128)(2,1)S(1)}, u32[]{:S(2)}, u32[]{:S(2)}) collective-permute-start(bf16[160,640]{1,0:T(8,128)(2,1)S(1)} %shard_map.60.refs_4_), channel_id=1, source_target_pairs={{0,4},{4,8},{8,12},{12,0},{1,5},{5,9},{9,13},{13,1},{2,6},{6,10},{... | collective-permute-start | bytes 614408 | tf_op jit(solution)/shard_map/ppermute | solution.py:352
  19.5 10.3 %collective-permute-start.1 = (bf16[160,640]{1,0:T(8,128)(2,1)S(1)}, bf16[160,640]{1,0:T(8,128)(2,1)S(1)}, u32[]{:S(2)}, u32[]{:S(2)}) collective-permute-start(bf16[160,640]{1,0:T(8,128)(2,1)S(1)} %shard_map.60.refs_4_), channel_id=1, source_target_pairs={{0,12},{4,0},{8,4},{12,8},{1,13},{5,1},{9,5},{13,9},{2,14},{6,2},{... | collective-permute-start | bytes 614408 | tf_op jit(solution)/shard_map/ppermute | solution.py:352
  29.8 43.9 %copy-start.21 = (bf16[160,640]{1,0:T(8,128)(2,1)}, bf16[160,640]{1,0:T(8,128)(2,1)S(1)}, u32[]{:S(2)}) copy-start(bf16[160,640]{1,0:T(8,128)(2,1)S(1)} %collective-permute-done.1.refs_8_) | copy-start | bytes 614404
  30.4 43.3 %copy-start.10 = (bf16[480,640]{1,0:T(8,128)(2,1)}, bf16[480,640]{1,0:T(8,128)(2,1)S(1)}, u32[]{:S(2)}) copy-start(bf16[480,640]{1,0:T(8,128)(2,1)S(1)} %shard_map.61.refs_5_) | copy-start | bytes 1843204
  30.4 26.3 %collective-permute-start.2 = (bf16[480,640]{1,0:T(8,128)(2,1)S(1)}, bf16[480,640]{1,0:T(8,128)(2,1)S(1)}, u32[]{:S(2)}, u32[]{:S(2)}) collective-permute-start(bf16[480,640]{1,0:T(8,128)(2,1)S(1)} %shard_map.61.refs_5_), channel_id=1, source_target_pairs={{0,4},{4,8},{8,12},{12,0},{1,5},{5,9},{9,13},{13,1},{2,6},{6,10},{... | collective-permute-start | bytes 1843208 | tf_op jit(solution)/shard_map/ppermute | solution.py:352
  39.4 30.5 %collective-permute-start.3 = (bf16[480,640]{1,0:T(8,128)(2,1)S(1)}, bf16[480,640]{1,0:T(8,128)(2,1)}, u32[]{:S(2)}, u32[]{:S(2)}) collective-permute-start(bf16[480,640]{1,0:T(8,128)(2,1)S(1)} %shard_map.61.refs_5_), channel_id=1, source_target_pairs={{0,12},{4,0},{8,4},{12,8},{1,13},{5,1},{9,5},{13,9},{2,14},{6,2},{... | collective-permute-start | bytes 1843208 | tf_op jit(solution)/shard_map/ppermute | solution.py:352
  42.3 31.2 %all-to-all-start.1 = ((bf16[4,160,640]{2,1,0:T(8,128)(2,1)}), bf16[4,160,640]{2,1,0:T(8,128)(2,1)S(1)}, u32[]{:S(2)}, u32[]{:S(2)}) async-start(bf16[4,160,640]{2,1,0:T(8,128)(2,1)} %shard_map.62), calls=%async_computation.1 | async-start | bytes 1638400 | tf_op jit(solution)/shard_map/all_to_all | solution.py:368
  48.0 36.2 %collective-permute-start.4 = (bf16[80,640]{1,0:T(8,128)(2,1)S(1)}, bf16[80,640]{1,0:T(8,128)(2,1)S(1)}, u32[]{:S(2)}, u32[]{:S(2)}) collective-permute-start(bf16[80,640]{1,0:T(8,128)(2,1)S(1)} %slice.12), channel_id=1, source_target_pairs={{0,4},{4,8},{8,12},{12,0},{1,5},{5,9},{9,13},{13,1},{2,6},{6,10},{... | collective-permute-start | bytes 307208 | tf_op jit(solution)/shard_map/ppermute | solution.py:352
  53.5 30.7 %collective-permute-start.5 = (bf16[80,640]{1,0:T(8,128)(2,1)}, bf16[80,640]{1,0:T(8,128)(2,1)S(1)}, u32[]{:S(2)}, u32[]{:S(2)}) collective-permute-start(bf16[80,640]{1,0:T(8,128)(2,1)} %slice.13), channel_id=1, source_target_pairs={{0,12},{4,0},{8,4},{12,8},{1,13},{5,1},{9,5},{13,9},{2,14},{6,2},{... | collective-permute-start | bytes 307208 | tf_op jit(solution)/shard_map/ppermute | solution.py:352
  56.7 27.5 %collective-permute-start.6 = (bf16[240,640]{1,0:T(8,128)(2,1)S(1)}, bf16[240,640]{1,0:T(8,128)(2,1)}, u32[]{:S(2)}, u32[]{:S(2)}) collective-permute-start(bf16[240,640]{1,0:T(8,128)(2,1)S(1)} %slice.16), channel_id=1, source_target_pairs={{0,4},{4,8},{8,12},{12,0},{1,5},{5,9},{9,13},{13,1},{2,6},{6,10},{... | collective-permute-start | bytes 921608 | tf_op jit(solution)/shard_map/ppermute | solution.py:352
  71.7 16.1 %collective-permute-start.7 = (bf16[240,640]{1,0:T(8,128)(2,1)}, bf16[240,640]{1,0:T(8,128)(2,1)}, u32[]{:S(2)}, u32[]{:S(2)}) collective-permute-start(bf16[240,640]{1,0:T(8,128)(2,1)} %slice.17), channel_id=1, source_target_pairs={{0,12},{4,0},{8,4},{12,8},{1,13},{5,1},{9,5},{13,9},{2,14},{6,2},{... | collective-permute-start | bytes 921608 | tf_op jit(solution)/shard_map/ppermute | solution.py:352
  96.8 14.9 %all-to-all-start.2 = ((f32[16,64,128]{2,1,0:T(8,128)}), f32[16,64,128]{2,1,0:T(8,128)S(1)}, u32[]{:S(2)}, u32[]{:S(2)}) async-start(f32[16,64,128]{2,1,0:T(8,128)} %get-tuple-element.32), calls=%async_computation.2 | async-start | bytes 1048576 | tf_op jit(solution)/shard_map/all_to_all | solution.py:384
  102.0 48.1 %copy-start.4 = (bf16[640,160]{1,0:T(8,128)(2,1)S(1)}, bf16[640,160]{1,0:T(8,128)(2,1)}, u32[]{:S(2)}) copy-start(bf16[640,160]{1,0:T(8,128)(2,1)} %get-tuple-element.30.refs_3_.refs_4_.refs_2_) | copy-start | bytes 614404
  102.0 48.1 %copy-start.6 = (bf16[640,160]{1,0:T(8,128)(2,1)S(1)}, bf16[640,160]{1,0:T(8,128)(2,1)}, u32[]{:S(2)}) copy-start(bf16[640,160]{1,0:T(8,128)(2,1)} %get-tuple-element.31.refs_4_.refs_5_.refs_3_) | copy-start | bytes 614404
  102.0 48.1 %copy-start.17 = (s32[2]{0:T(128)S(1)}, s32[2]{0:T(128)}, u32[]{:S(2)}) copy-start(s32[2]{0:T(128)} %copy-done.15) | copy-start | bytes 28
  129.8 12.9 %all-to-all-start.4 = ((f32[16,32,128]{2,1,0:T(8,128)}), f32[16,32,128]{2,1,0:T(8,128)S(1)}, u32[]{:S(2)}, u32[]{:S(2)}) async-start(f32[16,32,128]{2,1,0:T(8,128)} %broadcast_in_dim.22), calls=%async_computation.4 | async-start | bytes 524288 | tf_op jit(solution)/shard_map/all_to_all | solution.py:391
  134.1 10.8 %collective-permute-start.10 = (bf16[160,640]{1,0:T(8,128)(2,1)}, bf16[160,640]{1,0:T(8,128)(2,1)S(1)}, u32[]{:S(2)}, u32[]{:S(2)}) collective-permute-start(bf16[160,640]{1,0:T(8,128)(2,1)} %get-tuple-element.43), channel_id=1, source_target_pairs={{0,3},{1,0},{2,1},{3,2},{4,7},{5,4},{6,5},{7,6},{8,11},{9,8},{10,9... | collective-permute-start | bytes 614408 | tf_op jit(solution)/shard_map/ppermute | solution.py:352
  136.8 13.2 %collective-permute-start.8 = (bf16[160,640]{1,0:T(8,128)(2,1)}, bf16[160,640]{1,0:T(8,128)(2,1)S(1)}, u32[]{:S(2)}, u32[]{:S(2)}) collective-permute-start(bf16[160,640]{1,0:T(8,128)(2,1)} %get-tuple-element.41), channel_id=1, source_target_pairs={{0,1},{1,2},{2,3},{3,0},{4,5},{5,6},{6,7},{7,4},{8,9},{9,10},{10,1... | collective-permute-start | bytes 614408 | tf_op jit(solution)/shard_map/ppermute | solution.py:352
  139.9 10.1 %collective-permute-start.9 = (bf16[160,640]{1,0:T(8,128)(2,1)}, bf16[160,640]{1,0:T(8,128)(2,1)S(1)}, u32[]{:S(2)}, u32[]{:S(2)}) collective-permute-start(bf16[160,640]{1,0:T(8,128)(2,1)} %get-tuple-element.42), channel_id=1, source_target_pairs={{0,2},{1,3},{2,0},{3,1},{4,6},{5,7},{6,4},{7,5},{8,10},{9,11},{10,... | collective-permute-start | bytes 614408 | tf_op jit(solution)/shard_map/ppermute | solution.py:352
  (15 other events, 153.4 us)
Sparse Core Ops, SparseCore 0:
  10.1 59.2 all-gather.2

commit v3 on v2

--- a/solution.py
+++ b/solution.py
@@ -53,10 +53,13 @@
     return one(a[0], b[0]) + (one(a[0], b[1]) + one(a[1], b[0]))
 
 
-def quarter_kernel(where_ref, grad_ref, out_ref):
-    width = out_ref.shape[1]
-    at = where_ref[0] * width
-    out_ref[...] = grad_ref[:, pl.ds(pl.multiple_of(at, width), width)]
+def quarter_kernel(where_ref, grad_ref, up_ref, down_ref):
+    rows, width = up_ref.shape
+    half = rows // 2
+    at = pl.multiple_of(where_ref[0] * width, width)
+    up_ref[...] = grad_ref[:, pl.ds(at, width)]
+    down_ref[:half] = grad_ref[half:, pl.ds(at, width)]
+    down_ref[half:] = grad_ref[:half, pl.ds(at, width)]
 
 
 def quarter(where, whole):
@@ -65,8 +68,8 @@
     return pl.pallas_call(
         quarter_kernel,
         in_specs=[SMEM, VMEM],
-        out_specs=VMEM,
-        out_shape=out,
+        out_specs=[VMEM] * 2,
+        out_shape=[out] * 2,
         compiler_params=room(4),
         cost_estimate=cost(0, out, out),
     )(where, whole)
@@ -91,22 +94,33 @@
     )(whole)
 
 
-def others_kernel(where_ref, all_ref, out_ref):
+def others_kernel(where_ref, all_ref, up_ref, down_ref):
     rows = all_ref.shape[1]
-    for n in range(SIDE - 1):
-        out_ref[n * rows : (n + 1) * rows] = all_ref[lax.rem(where_ref[0] + n + 1, SIDE)]
+    half = rows // 2
+    one, two, three = [lax.rem(where_ref[0] + n, SIDE) for n in (1, 2, 3)]
+    up_ref[:rows] = down_ref[rows + half : 2 * rows + half] = all_ref[one]
+    up_ref[rows : 2 * rows] = all_ref[two]
+    up_ref[2 * rows :] = down_ref[half : rows + half] = all_ref[three]
+    down_ref[:half] = all_ref[two, half:]
+    down_ref[2 * rows + half :] = all_ref[two, :half]
 
 
 def others(where, every):
     _, toks, width = every.shape
+    out = jax.ShapeDtypeStruct(((SIDE - 1) * toks, width), every.dtype)
     return pl.pallas_call(
         others_kernel,
         in_specs=[SMEM, VMEM],
-        out_specs=VMEM,
-        out_shape=jax.ShapeDtypeStruct(((SIDE - 1) * toks, width), every.dtype),
-        compiler_params=room(4),
+        out_specs=[VMEM] * 2,
+        out_shape=[out] * 2,
+        compiler_params=room(8),
         cost_estimate=cost(0, every, every),
     )(where, every)
+
+
+def halves_swapped(ref):
+    half = ref.shape[0] // 2
+    return [ref.at[half : 2 * half], ref.at[:half]]
 
 
 def rows_in_order(where_ref, piece_refs, block, sems):
@@ -121,7 +135,7 @@
             at = pl.multiple_of(lax.rem(where_ref[0] + n, SIDE) * each + skip, each // 2)
             copies.append(
                 pltpu.make_async_copy(
-                    piece_ref.at[pl.ds(row - start, size)], block.at[pl.ds(at, size)], sems.at[len(copies)]
+                    piece_ref.at[row - start : row - start + size], block.at[pl.ds(at, size)], sems.at[len(copies)]
                 )
             )
             row += size
@@ -141,9 +155,11 @@
     @pl.when(pl.program_id(0) == 0)
     def _():
         copies = []
-        for n in range(3):
+        own, up, down = pieces[:2], pieces[2:4], pieces[4:]
+        down = [*halves_swapped(down[0]), *halves_swapped(down[1])]
+        for n, refs in enumerate((own, up, down)):
             block = grad_block.at[n * depth : (n + 1) * depth]
-            copies += rows_in_order(where_ref, pieces[2 * n : 2 * n + 2], block, sems.at[n])
+            copies += rows_in_order(where_ref, refs, block, sems.at[n])
         for copy in copies:
             copy.start()
         rows, coefs = high_ref.shape
@@ -191,7 +207,7 @@
             out_specs=[some, pl.BlockSpec((rows, coefs), lambda p, w: (p, 0)), whole, whole],
             scratch_shapes=[
                 pltpu.VMEM((3 * toks // SIDE, outs), jnp.bfloat16),
-                pltpu.SemaphoreType.DMA((3, SIDE)),
+                pltpu.SemaphoreType.DMA((3, 6)),
             ],
         ),
         out_shape=[part, coeff, basis, basis],
@@ -222,14 +238,19 @@
 
 def far_kernel(
     scale, where_ref, acts_ref, near_ref, high_ref, low_ref, p0_ref, p1_ref, p2_ref, p3_ref,
-    coeff_ref, packed_ref, acts_block, grad_block, sems,
+    packed_ref, acts_block, grad_block, near_block, high_block, low_block, sems,
 ):
     depth = grad_block.shape[0]
     copies = rows_in_order(where_ref, (p0_ref, p1_ref, p2_ref, p3_ref), grad_block, sems)
-    last = pltpu.make_async_copy(
-        acts_columns(where_ref, 2, acts_ref, depth), acts_block, sems.at[6]
-    )
-    for copy in [*copies, last]:
+    copies.append(pltpu.make_async_copy(high_ref, high_block, sems.at[8]))
+    copies.append(pltpu.make_async_copy(low_ref, low_block, sems.at[9]))
+    last = [
+        pltpu.make_async_copy(
+            acts_columns(where_ref, 2, acts_ref, depth), acts_block, sems.at[6]
+        ),
+        pltpu.make_async_copy(near_ref, near_block, sems.at[7]),
+    ]
+    for copy in copies + last:
         copy.start()
     for copy in copies:
         copy.wait()
@@ -238,11 +259,11 @@
         return jnp.dot(a, b, preferred_element_type=jnp.float32)
 
     grad = grad_block[...]
-    high, low = two_parts(dot(grad, high_ref[...]) + dot(grad, low_ref[...]))
-    last.wait()
+    high, low = two_parts(dot(grad, high_block[...]) + dot(grad, low_block[...]))
+    for copy in last:
+        copy.wait()
     acts = acts_block[...]
-    coeff = near_ref[...] + (dot(acts, high) + dot(acts, low)) * scale
-    coeff_ref[...] = coeff
+    coeff = near_block[...] + (dot(acts, high) + dot(acts, low)) * scale
     count, rows, _ = packed_ref.shape
     each = coeff.shape[0] // count
     for n in range(count):
@@ -256,21 +277,24 @@
     out = jax.ShapeDtypeStruct((16, 64, LANES), jnp.float32)
     return pl.pallas_call(
         lambda *refs: far_kernel(scale, *refs),
-        in_specs=[SMEM, HBM] + [VMEM] * 3 + [HBM] * len(pieces),
-        out_specs=[VMEM] * 2,
-        out_shape=[jax.ShapeDtypeStruct(coeff.shape, coeff.dtype), out],
+        in_specs=[SMEM] + [HBM] * (4 + len(pieces)),
+        out_specs=VMEM,
+        out_shape=out,
         scratch_shapes=[
             pltpu.VMEM((feats, depth), jnp.bfloat16),
             pltpu.VMEM((depth, outs), jnp.bfloat16),
-            pltpu.SemaphoreType.DMA((8,)),
+            pltpu.VMEM(coeff.shape, coeff.dtype),
+            pltpu.VMEM(high.shape, high.dtype),
+            pltpu.VMEM(low.shape, low.dtype),
+            pltpu.SemaphoreType.DMA((10,)),
         ],
-        compiler_params=room(14),
+        compiler_params=room(60),
         cost_estimate=cost(4 * coefs * depth * (feats + outs), acts, coeff, out, *pieces),
     )(where, acts, coeff, high, low, *pieces)
 
 
 def residual_kernel(
-    scale, where_ref, acts_ref, part_ref, coeff_ref, high_ref, low_ref, p0_ref, p1_ref, p2_ref, p3_ref,
+    scale, where_ref, acts_ref, part_ref, packed_ref, high_ref, low_ref, p0_ref, p1_ref, p2_ref, p3_ref,
     *refs,
 ):
     outs, (acts_block, grad_block, part_block, sems) = refs[:SIDE], refs[SIDE:]
@@ -284,7 +308,10 @@
     for copy in copies:
         copy.start()
     basis = (high_ref[...], low_ref[...])
-    kept = dot_parts(two_parts(coeff_ref[...]), basis, ((1,), (1,)))
+    count = packed_ref.shape[0]
+    each, coefs = part_block.shape[0] // count, high_ref.shape[1]
+    coeff = jnp.concatenate([unpacked(packed_ref[n], each, coefs) for n in range(count)], 0)
+    kept = dot_parts(two_parts(coeff), basis, ((1,), (1,)))
     for copy in copies:
         copy.wait()
     term = jnp.dot(acts_block[...], grad_block[...], preferred_element_type=jnp.float32)
@@ -315,15 +342,11 @@
     )(where, acts, part, coeff, high, low, *pieces)
 
 
-def finish_kernel(replicas, where_ref, total_ref, high_ref, low_ref, *refs):
-    pieces, (update_ref, fresh_ref) = refs[:SIDE], refs[SIDE:]
-    x = where_ref[0]
-    rows, width = pieces[0].shape
-    coefs = high_ref.shape[1]
+def decode_kernel(replicas, total_ref, high_ref, low_ref, update_ref):
+    rows = update_ref.shape[0]
+    width, coefs = high_ref.shape
     basis = (high_ref[...], low_ref[...])
-    for q, piece_ref in enumerate(pieces):
-        at = pl.multiple_of(lax.rem(x + SIDE - q, SIDE) * width, width)
-        fresh_ref[:, pl.ds(at, width)] = piece_ref[...]
+    for q in range(SIDE):
         quarters = []
         for ylo in range(2):
             for core in range(2):
@@ -335,17 +358,37 @@
         )
 
 
-def finish(replicas, where, total, high, low, pieces):
+def decode(replicas, rows, total, high, low):
+    out = jax.ShapeDtypeStruct((rows, SIDE * high.shape[0]), jnp.bfloat16)
+    return pl.pallas_call(
+        lambda *refs: decode_kernel(replicas, *refs),
+        in_specs=[VMEM] * 3,
+        out_specs=VMEM,
+        out_shape=out,
+        compiler_params=room(8),
+        cost_estimate=cost(6 * total.size * high.shape[0], total, out),
+    )(total, high, low)
+
+
+def columns_kernel(where_ref, *refs):
+    *pieces, out_ref = refs
+    width = pieces[0].shape[1]
+    for n, piece_ref in enumerate(pieces):
+        at = lax.rem(where_ref[0] + SIDE - n, SIDE) * width
+        out_ref[:, pl.ds(pl.multiple_of(at, width), width)] = piece_ref[...]
+
+
+def columns(where, pieces):
     rows, width = pieces[0].shape
-    out = jax.ShapeDtypeStruct((rows, SIDE * width), jnp.bfloat16)
-    return pl.pallas_call(
-        lambda *refs: finish_kernel(replicas, *refs),
-        in_specs=[SMEM] + [VMEM] * (3 + SIDE),
-        out_specs=[VMEM] * 2,
-        out_shape=[out, out],
-        compiler_params=room(8),
-        cost_estimate=cost(6 * total.size * width, total, out, out, out),
-    )(where, total, high, low, *pieces)
+    out = jax.ShapeDtypeStruct((rows, SIDE * width), pieces[0].dtype)
+    return pl.pallas_call(
+        columns_kernel,
+        in_specs=[SMEM] + [VMEM] * SIDE,
+        out_specs=VMEM,
+        out_shape=out,
+        compiler_params=room(4),
+        cost_estimate=cost(0, out, out),
+    )(where, *pieces)
 
 
 def shifted(x, axis, by):
@@ -359,26 +402,26 @@
     where = jnp.stack([lax.axis_index("x"), lax.axis_index("yhi")]).astype(jnp.int32)
 
     acts = lax.all_gather(attn_out.T, "x", axis=0, tiled=True)
-    first = quarter(where, out_grad)
-    up, down = [shifted(first, "yhi", 1)], [shifted(first, "yhi", -1)]
+    first, swapped = quarter(where, out_grad)
+    up, down = [shifted(first, "yhi", 1)], [shifted(swapped, "yhi", -1)]
     every = lax.all_to_all(pack(out_grad), "x", 0, 0, tiled=True)
     every, up[0], down[0] = lax.optimization_barrier((every, up[0], down[0]))
-    rest = others(where, every)
-    stored, rest = lax.optimization_barrier((momentum[0], rest))
+    rest, swapped = others(where, every)
+    stored, rest, swapped = lax.optimization_barrier((momentum[0], rest, swapped))
     mom = lax.all_to_all(pack(stored, 60), "x", 0, 0, tiled=True).reshape(SIDE * toks, width // SIDE)
     own = [first, rest]
     up.append(shifted(rest, "yhi", 1))
-    down.append(shifted(rest, "yhi", -1))
+    down.append(shifted(swapped, "yhi", -1))
     over = []
     for above, below in zip(up, down):
         middle = above.shape[0] // 2
         over.append(shifted(above[:middle], "yhi", 1))
-        over.append(shifted(below[middle:], "yhi", -1))
+        over.append(shifted(below[:middle], "yhi", -1))
 
     table = basis_table(jnp.tile(kept, width // SIDE // GROUP))
     part, coeff, high, low = near(scale, where, acts, mom, table, own + up + down, 20)
-    coeff, pieces = far(scale, where, acts, coeff, high, low, over)
-    fresh = residual(scale, where, acts, part, coeff, high, low, over)
+    pieces = far(scale, where, acts, coeff, high, low, over)
+    fresh = residual(scale, where, acts, part, pieces, high, low, over)
 
     tile = pieces.shape[1:]
     pieces = lax.all_to_all(pieces, ("x", "ylo", "core"), 0, 0, tiled=True)
@@ -391,9 +434,9 @@
     spread = lax.all_to_all(spread, ("ylo", "z"), 0, 0, tiled=True)
     total = lax.all_gather(spread, "core", axis=0).reshape(2, 2, 4, 2, *tile)
     fresh = [fresh[0]] + [shifted(fresh[s], "x", s) for s in (1, 2, 3)]
-    update, new_momentum = finish(
-        replicas, where, total, high, low, fresh
-    )
+    update = decode(replicas, toks, total, high, low)
+    total, *fresh = lax.optimization_barrier((total, *fresh))
+    new_momentum = columns(where, fresh)
     return update, new_momentum[None]
 
 

time: 162 us -> 157 us (0.969)
  the two profiles are of different devices: /device:TPU:8 before, /device:TPU:1 now
where the time goes in v3:
time: 157 us; the launch traced here: 154 us
  starting transfers between devices  59.2 us (38%)
  Pallas kernels  27.4 us (17%)
  waiting for transfers between devices  24.6 us (16%)
  blocking collectives  20.6 us (13%)
  between operations  14.4 us (9%)
  local copies, waits for them, and re-layouts  6.43 us (4%)
    ppermute x11, starting transfers between devices, shifted(): return lax.ppermute(x, axis, [(i, (i + by) % SIDE) for i in range(SIDE)])  37.6 us
    ppermute x11, waiting for transfers between devices, shifted(): return lax.ppermute(x, axis, [(i, (i + by) % SIDE) for i in range(SIDE)])  19.8 us
    all_to_all x1, blocking collectives, per_device(): pieces = lax.all_to_all(summed.reshape(8, *tile), 'z', 0, 0, tiled=True)  15.5 us
    pallas_call x1, Pallas kernels, near(): pl.pallas_call(lambda *refs: near_kernel(scale, *refs), grid_spec=pltpu.P...  9.41 us
    all_to_all x1, starting transfers between devices, per_device(): pieces = lax.all_to_all(pieces, ('x', 'ylo', 'core'), 0, 0, tiled=True)  8.84 us
    pallas_call x1, Pallas kernels, residual(): pl.pallas_call(lambda *refs: residual_kernel(scale, *refs), in_specs=[SME...  5.69 us
    pallas_call x1, Pallas kernels, far(): pl.pallas_call(lambda *refs: far_kernel(scale, *refs), in_specs=[SMEM] +...  5.39 us
    all_gather x1, blocking collectives, per_device(): total = lax.all_gather(spread, 'core', axis=0).reshape(2, 2, 4, 2, *tile)  5.05 us
  transfers between devices with their start and end apart: 16, of which 5 were waited for; matrix products, arithmetic and copies ran while one was open for 2% of the time, Pallas kernels for 13%

profile of v3, /device:TPU:1, one launch (start us, length us, event | category | flops | bytes accessed | tf_op | source)
XLA Modules:
  0.0 153.6 jit_solution(2778482282079855163)
XLA Ops:
  10.0 5.0 %all-to-all-start = ((bf16[4,160,640]{2,1,0:T(8,128)(2,1)}), bf16[4,160,640]{2,1,0:T(8,128)(2,1)S(1)}, u32[]{:S(2)}, u32[]{:S(2)}) async-start(bf16[4,160,640]{2,1,0:T(8,128)(2,1)} %shard_map.59), calls=%async_computation | async-start | bytes 1638400 | tf_op jit(solution)/shard_map/all_to_all | solution.py:407
  15.7 4.2 %collective-permute-start = (bf16[160,640]{1,0:T(8,128)(2,1)S(1)}, bf16[160,640]{1,0:T(8,128)(2,1)S(1)}, u32[]{:S(2)}, u32[]{:S(2)}) collective-permute-start(bf16[160,640]{1,0:T(8,128)(2,1)S(1)} %get-tuple-element.29.refs_4_), channel_id=1, source_target_pairs={{0,4},{4,8},{8,12},{12,0},{1,5},{5,9},{9,13},{13,1},{2,6},{6,10},{... | collective-permute-start | bytes 614408 | tf_op jit(solution)/shard_map/ppermute | solution.py:395
  19.9 3.6 %collective-permute-start.1 = (bf16[160,640]{1,0:T(8,128)(2,1)S(1)}, bf16[160,640]{1,0:T(8,128)(2,1)S(1)}, u32[]{:S(2)}, u32[]{:S(2)}) collective-permute-start(bf16[160,640]{1,0:T(8,128)(2,1)S(1)} %get-tuple-element.30), channel_id=1, source_target_pairs={{0,12},{4,0},{8,4},{12,8},{1,13},{5,1},{9,5},{13,9},{2,14},{6,2},{... | collective-permute-start | bytes 614408 | tf_op jit(solution)/shard_map/ppermute | solution.py:395
  25.6 9.5 %collective-permute-done.1.refs_8_ = bf16[160,640]{1,0:T(8,128)(2,1)S(1)} collective-permute-done((bf16[160,640]{1,0:T(8,128)(2,1)S(1)}, bf16[160,640]{1,0:T(8,128)(2,1)S(1)}, u32[]{:S(2)}, u32[]{:S(2)}) %collective-permute-start.1) | collective-permute-done | bytes 204832 | tf_op jit(solution)/shard_map/ppermute | solution.py:395
  35.8 4.0 %collective-permute-start.2 = (bf16[480,640]{1,0:T(8,128)(2,1)S(1)}, bf16[480,640]{1,0:T(8,128)(2,1)}, u32[]{:S(2)}, u32[]{:S(2)}) collective-permute-start(bf16[480,640]{1,0:T(8,128)(2,1)S(1)} %get-tuple-element.35.refs_5_), channel_id=1, source_target_pairs={{0,4},{4,8},{8,12},{12,0},{1,5},{5,9},{9,13},{13,1},{2,6},{6,10},{... | collective-permute-start | bytes 1843208 | tf_op jit(solution)/shard_map/ppermute | solution.py:395
  39.8 3.4 %collective-permute-start.3 = (bf16[480,640]{1,0:T(8,128)(2,1)S(1)}, bf16[480,640]{1,0:T(8,128)(2,1)}, u32[]{:S(2)}, u32[]{:S(2)}) collective-permute-start(bf16[480,640]{1,0:T(8,128)(2,1)S(1)} %get-tuple-element.38), channel_id=1, source_target_pairs={{0,12},{4,0},{8,4},{12,8},{1,13},{5,1},{9,5},{13,9},{2,14},{6,2},{... | collective-permute-start | bytes 1843208 | tf_op jit(solution)/shard_map/ppermute | solution.py:395
  44.2 4.2 %all-to-all-start.1 = ((bf16[4,160,640]{2,1,0:T(8,128)(2,1)}), bf16[4,160,640]{2,1,0:T(8,128)(2,1)S(1)}, u32[]{:S(2)}, u32[]{:S(2)}) async-start(bf16[4,160,640]{2,1,0:T(8,128)(2,1)} %shard_map.62), calls=%async_computation.1 | async-start | bytes 1638400 | tf_op jit(solution)/shard_map/all_to_all | solution.py:411
  49.5 2.8 %collective-permute-start.4 = (bf16[80,640]{1,0:T(8,128)(2,1)S(1)}, bf16[80,640]{1,0:T(8,128)(2,1)S(1)}, u32[]{:S(2)}, u32[]{:S(2)}) collective-permute-start(bf16[80,640]{1,0:T(8,128)(2,1)S(1)} %slice.12), channel_id=1, source_target_pairs={{0,4},{4,8},{8,12},{12,0},{1,5},{5,9},{9,13},{13,1},{2,6},{6,10},{... | collective-permute-start | bytes 307208 | tf_op jit(solution)/shard_map/ppermute | solution.py:395
  53.0 4.6 %collective-permute-start.5 = (bf16[80,640]{1,0:T(8,128)(2,1)}, bf16[80,640]{1,0:T(8,128)(2,1)S(1)}, u32[]{:S(2)}, u32[]{:S(2)}) collective-permute-start(bf16[80,640]{1,0:T(8,128)(2,1)} %slice.13), channel_id=1, source_target_pairs={{0,12},{4,0},{8,4},{12,8},{1,13},{5,1},{9,5},{13,9},{2,14},{6,2},{... | collective-permute-start | bytes 307208 | tf_op jit(solution)/shard_map/ppermute | solution.py:395
  57.6 7.8 %collective-permute-done.2.refs_7_ = bf16[480,640]{1,0:T(8,128)(2,1)} collective-permute-done((bf16[480,640]{1,0:T(8,128)(2,1)S(1)}, bf16[480,640]{1,0:T(8,128)(2,1)}, u32[]{:S(2)}, u32[]{:S(2)}) %collective-permute-start.2) | collective-permute-done | bytes 614432 | tf_op jit(solution)/shard_map/ppermute | solution.py:395
  66.4 3.1 %collective-permute-start.6 = (bf16[240,640]{1,0:T(8,128)(2,1)S(1)}, bf16[240,640]{1,0:T(8,128)(2,1)S(1)}, u32[]{:S(2)}, u32[]{:S(2)}) collective-permute-start(bf16[240,640]{1,0:T(8,128)(2,1)S(1)} %slice.16), channel_id=1, source_target_pairs={{0,4},{4,8},{8,12},{12,0},{1,5},{5,9},{9,13},{13,1},{2,6},{6,10},{... | collective-permute-start | bytes 921608 | tf_op jit(solution)/shard_map/ppermute | solution.py:395
  70.9 3.9 %collective-permute-start.7 = (bf16[240,640]{1,0:T(8,128)(2,1)S(1)}, bf16[240,640]{1,0:T(8,128)(2,1)S(1)}, u32[]{:S(2)}, u32[]{:S(2)}) collective-permute-start(bf16[240,640]{1,0:T(8,128)(2,1)S(1)} %slice.17), channel_id=1, source_target_pairs={{0,12},{4,0},{8,4},{12,8},{1,13},{5,1},{9,5},{13,9},{2,14},{6,2},{... | collective-permute-start | bytes 921608 | tf_op jit(solution)/shard_map/ppermute | solution.py:395
  75.7 9.4 %shard_map.63 = (f32[640,640]{1,0:T(8,128)}, f32[640,160]{1,0:T(8,128)}, bf16[640,160]{1,0:T(8,128)(2,1)}, bf16[640,160]{1,0:T(8,128)(2,1)}) custom-call(s32[2]{0:T(128)} %copy-done.6, bf16[640,2560]{1,0:T(8,128)(2,1)} %all-gather.3.cloned.1.call-done.refs_1_, bf16[640,640]{1,0:T(8,128)(2,1)} %bitcast.13, f32[64,160]{1,0:T(8,128)} %cosine_multiply_fusion.refs_3_, ...), custom_call_target="tpu_custom_call" | custom-call | flops 31457280000 | bytes 7372800 | tf_op jit(solution)/shard_map/pallas_call | solution.py:196
  86.1 5.4 %shard_map.64.refs_3_ = f32[16,64,128]{2,1,0:T(8,128)} custom-call(s32[2]{0:T(128)} %copy-done.6, bf16[640,2560]{1,0:T(8,128)(2,1)} %all-gather.3.cloned.1.call-done.refs_1_, f32[640,160]{1,0:T(8,128)} %get-tuple-element.39.refs_2_, bf16[640,160]{1,0:T(8,128)(2,1)} %get-tuple-element.40.refs_3_.refs_4_.refs_1_, ...), custom_call_target="tpu_custom_call" | custom-call | flops 524288000 | bytes 5029888 | tf_op jit(solution)/shard_map/pallas_call | solution.py:278
  91.5 8.8 %all-to-all-start.2 = ((f32[16,64,128]{2,1,0:T(8,128)}), f32[16,64,128]{2,1,0:T(8,128)S(1)}, u32[]{:S(2)}, u32[]{:S(2)}) async-start(f32[16,64,128]{2,1,0:T(8,128)} %shard_map.64.refs_3_), calls=%async_computation.2 | async-start | bytes 1048576 | tf_op jit(solution)/shard_map/all_to_all | solution.py:427
  100.3 5.7 %shard_map.65 = (bf16[160,640]{1,0:T(8,128)(2,1)}, bf16[160,640]{1,0:T(8,128)(2,1)}, bf16[160,640]{1,0:T(8,128)(2,1)}, bf16[160,640]{1,0:T(8,128)(2,1)}) custom-call(s32[2]{0:T(128)} %copy-done.6, bf16[640,2560]{1,0:T(8,128)(2,1)} %all-gather.3.cloned.1.call-done.refs_1_, f32[640,640]{1,0:T(8,128)} %get-tuple-element.42.refs_2_, ...), custom_call_target="tpu_custom_call" | custom-call | flops 917504000 | bytes 2981888 | tf_op jit(solution)/shard_map/pallas_call | solution.py:329
  106.0 4.1 %all-to-all-done.2 = f32[16,64,128]{2,1,0:T(8,128)S(1)} async-done(((f32[16,64,128]{2,1,0:T(8,128)}), f32[16,64,128]{2,1,0:T(8,128)S(1)}, u32[]{:S(2)}, u32[]{:S(2)}) %all-to-all-start.2) | async-done | bytes 524320 | tf_op jit(solution)/shard_map/all_to_all | solution.py:427
  110.1 15.5 %all_to_all.25 = f32[8,32,128]{2,1,0:T(8,128)S(1)} all-to-all(f32[8,32,128]{2,1,0:T(8,128)S(1)} %bitcast.15), channel_id=1, replica_groups=mesh['ylo'=2,'z'=8,'core'=2,'yhi'=4,'x'=4] {'z'}, dimensions={0} | all-to-all | bytes 262144 | tf_op jit(solution)/shard_map/all_to_all | solution.py:431
  126.4 3.5 %all-to-all-start.4 = ((f32[16,32,128]{2,1,0:T(8,128)}), f32[16,32,128]{2,1,0:T(8,128)S(1)}, u32[]{:S(2)}, u32[]{:S(2)}) async-start(f32[16,32,128]{2,1,0:T(8,128)} %broadcast_in_dim.22), calls=%async_computation.4 | async-start | bytes 524288 | tf_op jit(solution)/shard_map/all_to_all | solution.py:434
  129.9 2.5 %collective-permute-start.10 = (bf16[160,640]{1,0:T(8,128)(2,1)}, bf16[160,640]{1,0:T(8,128)(2,1)S(1)}, u32[]{:S(2)}, u32[]{:S(2)}) collective-permute-start(bf16[160,640]{1,0:T(8,128)(2,1)} %get-tuple-element.51), channel_id=1, source_target_pairs={{0,3},{1,0},{2,1},{3,2},{4,7},{5,4},{6,5},{7,6},{8,11},{9,8},{10,9... | collective-permute-start | bytes 614408 | tf_op jit(solution)/shard_map/ppermute | solution.py:395
  132.4 2.8 %collective-permute-start.8 = (bf16[160,640]{1,0:T(8,128)(2,1)}, bf16[160,640]{1,0:T(8,128)(2,1)S(1)}, u32[]{:S(2)}, u32[]{:S(2)}) collective-permute-start(bf16[160,640]{1,0:T(8,128)(2,1)} %get-tuple-element.49), channel_id=1, source_target_pairs={{0,1},{1,2},{2,3},{3,0},{4,5},{5,6},{6,7},{7,4},{8,9},{9,10},{10,1... | collective-permute-start | bytes 614408 | tf_op jit(solution)/shard_map/ppermute | solution.py:395
  135.2 2.7 %collective-permute-start.9 = (bf16[160,640]{1,0:T(8,128)(2,1)}, bf16[160,640]{1,0:T(8,128)(2,1)S(1)}, u32[]{:S(2)}, u32[]{:S(2)}) collective-permute-start(bf16[160,640]{1,0:T(8,128)(2,1)} %get-tuple-element.50), channel_id=1, source_target_pairs={{0,2},{1,3},{2,0},{3,1},{4,6},{5,7},{6,4},{7,5},{8,10},{9,11},{10,... | collective-permute-start | bytes 614408 | tf_op jit(solution)/shard_map/ppermute | solution.py:395
  138.0 5.1 %all-gather = f32[32,32,128]{2,1,0:T(8,128)S(1)} all-gather(f32[16,32,128]{2,1,0:T(8,128)S(1)} %all-to-all-done.4), channel_id=2, replica_groups=mesh['ylo'=2,'z'=8,'core'=2,'yhi'=4,'x'=4] {'core'}, dimensions={0}, use_global_device_ids=true | all-gather | bytes 786432 | tf_op jit(solution)/shard_map/all_gather | solution.py:435
  143.0 2.2 %shard_map.66 = bf16[160,2560]{1,0:T(8,128)(2,1)} custom-call(f32[2,2,4,2,32,128]{5,4,3,2,1,0:T(8,128)S(1)} %bitcast.10, bf16[640,160]{1,0:T(8,128)(2,1)S(1)} %copy-done.2, bf16[640,160]{1,0:T(8,128)(2,1)S(1)} %copy-done.3), custom_call_target="tpu_custom_call" | custom-call | flops 503316480 | bytes 1343488 | tf_op jit(solution)/shard_map/pallas_call | solution.py:363
  (72 shorter events, 15.4 us)
Async XLA Ops:
  7.2 67.7 %all-gather.3.cloned.1.call-start = ((), (), s32[]{:S(2)}) async-start(), calls=%async_computation.5 | async-start | bytes 4096000 | tf_op jit(solution)/shard_map/all_gather | solution.py:404
  10.0 25.1 %all-to-all-start = ((bf16[4,160,640]{2,1,0:T(8,128)(2,1)}), bf16[4,160,640]{2,1,0:T(8,128)(2,1)S(1)}, u32[]{:S(2)}, u32[]{:S(2)}) async-start(bf16[4,160,640]{2,1,0:T(8,128)(2,1)} %shard_map.59), calls=%async_computation | async-start | bytes 1638400 | tf_op jit(solution)/shard_map/all_to_all | solution.py:407
  15.1 55.8 %copy-start.6 = (s32[2]{0:T(128)}, s32[2]{0:T(128)S(1)}, u32[]{:S(2)}) copy-start(s32[2]{0:T(128)S(1)} %pad_add_fusion.where_ref.refs_0_) | copy-start | bytes 28
  15.7 59.2 %copy-start.9 = (bf16[160,640]{1,0:T(8,128)(2,1)}, bf16[160,640]{1,0:T(8,128)(2,1)S(1)}, u32[]{:S(2)}) copy-start(bf16[160,640]{1,0:T(8,128)(2,1)S(1)} %get-tuple-element.29.refs_4_) | copy-start | bytes 614404
  15.7 10.0 %collective-permute-start = (bf16[160,640]{1,0:T(8,128)(2,1)S(1)}, bf16[160,640]{1,0:T(8,128)(2,1)S(1)}, u32[]{:S(2)}, u32[]{:S(2)}) collective-permute-start(bf16[160,640]{1,0:T(8,128)(2,1)S(1)} %get-tuple-element.29.refs_4_), channel_id=1, source_target_pairs={{0,4},{4,8},{8,12},{12,0},{1,5},{5,9},{9,13},{13,1},{2,6},{6,10},{... | collective-permute-start | bytes 614408 | tf_op jit(solution)/shard_map/ppermute | solution.py:395
  19.9 15.2 %collective-permute-start.1 = (bf16[160,640]{1,0:T(8,128)(2,1)S(1)}, bf16[160,640]{1,0:T(8,128)(2,1)S(1)}, u32[]{:S(2)}, u32[]{:S(2)}) collective-permute-start(bf16[160,640]{1,0:T(8,128)(2,1)S(1)} %get-tuple-element.30), channel_id=1, source_target_pairs={{0,12},{4,0},{8,4},{12,8},{1,13},{5,1},{9,5},{13,9},{2,14},{6,2},{... | collective-permute-start | bytes 614408 | tf_op jit(solution)/shard_map/ppermute | solution.py:395
  25.6 39.8 %copy-start.15 = (bf16[160,640]{1,0:T(8,128)(2,1)}, bf16[160,640]{1,0:T(8,128)(2,1)S(1)}, u32[]{:S(2)}) copy-start(bf16[160,640]{1,0:T(8,128)(2,1)S(1)} %collective-permute-done.refs_6_) | copy-start | bytes 614404
  35.8 39.1 %copy-start.8 = (bf16[480,640]{1,0:T(8,128)(2,1)}, bf16[480,640]{1,0:T(8,128)(2,1)S(1)}, u32[]{:S(2)}) copy-start(bf16[480,640]{1,0:T(8,128)(2,1)S(1)} %get-tuple-element.35.refs_5_) | copy-start | bytes 1843204
  35.8 29.6 %collective-permute-start.2 = (bf16[480,640]{1,0:T(8,128)(2,1)S(1)}, bf16[480,640]{1,0:T(8,128)(2,1)}, u32[]{:S(2)}, u32[]{:S(2)}) collective-permute-start(bf16[480,640]{1,0:T(8,128)(2,1)S(1)} %get-tuple-element.35.refs_5_), channel_id=1, source_target_pairs={{0,4},{4,8},{8,12},{12,0},{1,5},{5,9},{9,13},{13,1},{2,6},{6,10},{... | collective-permute-start | bytes 1843208 | tf_op jit(solution)/shard_map/ppermute | solution.py:395
  39.8 30.1 %collective-permute-start.3 = (bf16[480,640]{1,0:T(8,128)(2,1)S(1)}, bf16[480,640]{1,0:T(8,128)(2,1)}, u32[]{:S(2)}, u32[]{:S(2)}) collective-permute-start(bf16[480,640]{1,0:T(8,128)(2,1)S(1)} %get-tuple-element.38), channel_id=1, source_target_pairs={{0,12},{4,0},{8,4},{12,8},{1,13},{5,1},{9,5},{13,9},{2,14},{6,2},{... | collective-permute-start | bytes 1843208 | tf_op jit(solution)/shard_map/ppermute | solution.py:395
  44.2 30.6 %all-to-all-start.1 = ((bf16[4,160,640]{2,1,0:T(8,128)(2,1)}), bf16[4,160,640]{2,1,0:T(8,128)(2,1)S(1)}, u32[]{:S(2)}, u32[]{:S(2)}) async-start(bf16[4,160,640]{2,1,0:T(8,128)(2,1)} %shard_map.62), calls=%async_computation.1 | async-start | bytes 1638400 | tf_op jit(solution)/shard_map/all_to_all | solution.py:411
  49.5 35.6 %collective-permute-start.4 = (bf16[80,640]{1,0:T(8,128)(2,1)S(1)}, bf16[80,640]{1,0:T(8,128)(2,1)S(1)}, u32[]{:S(2)}, u32[]{:S(2)}) collective-permute-start(bf16[80,640]{1,0:T(8,128)(2,1)S(1)} %slice.12), channel_id=1, source_target_pairs={{0,4},{4,8},{8,12},{12,0},{1,5},{5,9},{9,13},{13,1},{2,6},{6,10},{... | collective-permute-start | bytes 307208 | tf_op jit(solution)/shard_map/ppermute | solution.py:395
  53.0 32.1 %collective-permute-start.5 = (bf16[80,640]{1,0:T(8,128)(2,1)}, bf16[80,640]{1,0:T(8,128)(2,1)S(1)}, u32[]{:S(2)}, u32[]{:S(2)}) collective-permute-start(bf16[80,640]{1,0:T(8,128)(2,1)} %slice.13), channel_id=1, source_target_pairs={{0,12},{4,0},{8,4},{12,8},{1,13},{5,1},{9,5},{13,9},{2,14},{6,2},{... | collective-permute-start | bytes 307208 | tf_op jit(solution)/shard_map/ppermute | solution.py:395
  66.4 18.8 %collective-permute-start.6 = (bf16[240,640]{1,0:T(8,128)(2,1)S(1)}, bf16[240,640]{1,0:T(8,128)(2,1)S(1)}, u32[]{:S(2)}, u32[]{:S(2)}) collective-permute-start(bf16[240,640]{1,0:T(8,128)(2,1)S(1)} %slice.16), channel_id=1, source_target_pairs={{0,4},{4,8},{8,12},{12,0},{1,5},{5,9},{9,13},{13,1},{2,6},{6,10},{... | collective-permute-start | bytes 921608 | tf_op jit(solution)/shard_map/ppermute | solution.py:395
  70.9 14.3 %collective-permute-start.7 = (bf16[240,640]{1,0:T(8,128)(2,1)S(1)}, bf16[240,640]{1,0:T(8,128)(2,1)S(1)}, u32[]{:S(2)}, u32[]{:S(2)}) collective-permute-start(bf16[240,640]{1,0:T(8,128)(2,1)S(1)} %slice.17), channel_id=1, source_target_pairs={{0,12},{4,0},{8,4},{12,8},{1,13},{5,1},{9,5},{13,9},{2,14},{6,2},{... | collective-permute-start | bytes 921608 | tf_op jit(solution)/shard_map/ppermute | solution.py:395
  91.5 18.6 %all-to-all-start.2 = ((f32[16,64,128]{2,1,0:T(8,128)}), f32[16,64,128]{2,1,0:T(8,128)S(1)}, u32[]{:S(2)}, u32[]{:S(2)}) async-start(f32[16,64,128]{2,1,0:T(8,128)} %shard_map.64.refs_3_), calls=%async_computation.2 | async-start | bytes 1048576 | tf_op jit(solution)/shard_map/all_to_all | solution.py:427
  100.3 42.7 %copy-start.2 = (bf16[640,160]{1,0:T(8,128)(2,1)S(1)}, bf16[640,160]{1,0:T(8,128)(2,1)}, u32[]{:S(2)}) copy-start(bf16[640,160]{1,0:T(8,128)(2,1)} %get-tuple-element.40.refs_3_.refs_4_.refs_1_) | copy-start | bytes 614404
  100.3 42.7 %copy-start.3 = (bf16[640,160]{1,0:T(8,128)(2,1)S(1)}, bf16[640,160]{1,0:T(8,128)(2,1)}, u32[]{:S(2)}) copy-start(bf16[640,160]{1,0:T(8,128)(2,1)} %get-tuple-element.41.refs_4_.refs_5_.refs_2_) | copy-start | bytes 614404
  106.0 39.2 %copy-start.5 = (bf16[160,640]{1,0:T(8,128)(2,1)S(1)}, bf16[160,640]{1,0:T(8,128)(2,1)}, u32[]{:S(2)}) copy-start(bf16[160,640]{1,0:T(8,128)(2,1)} %get-tuple-element.52.refs_0_) | copy-start | bytes 614404
  106.0 39.2 %copy-start.7 = (s32[2]{0:T(128)S(1)}, s32[2]{0:T(128)}, u32[]{:S(2)}) copy-start(s32[2]{0:T(128)} %copy-done.6) | copy-start | bytes 28
  126.4 11.5 %all-to-all-start.4 = ((f32[16,32,128]{2,1,0:T(8,128)}), f32[16,32,128]{2,1,0:T(8,128)S(1)}, u32[]{:S(2)}, u32[]{:S(2)}) async-start(f32[16,32,128]{2,1,0:T(8,128)} %broadcast_in_dim.22), calls=%async_computation.4 | async-start | bytes 524288 | tf_op jit(solution)/shard_map/all_to_all | solution.py:434
  129.9 15.3 %collective-permute-start.10 = (bf16[160,640]{1,0:T(8,128)(2,1)}, bf16[160,640]{1,0:T(8,128)(2,1)S(1)}, u32[]{:S(2)}, u32[]{:S(2)}) collective-permute-start(bf16[160,640]{1,0:T(8,128)(2,1)} %get-tuple-element.51), channel_id=1, source_target_pairs={{0,3},{1,0},{2,1},{3,2},{4,7},{5,4},{6,5},{7,6},{8,11},{9,8},{10,9... | collective-permute-start | bytes 614408 | tf_op jit(solution)/shard_map/ppermute | solution.py:395
  132.4 12.8 %collective-permute-start.8 = (bf16[160,640]{1,0:T(8,128)(2,1)}, bf16[160,640]{1,0:T(8,128)(2,1)S(1)}, u32[]{:S(2)}, u32[]{:S(2)}) collective-permute-start(bf16[160,640]{1,0:T(8,128)(2,1)} %get-tuple-element.49), channel_id=1, source_target_pairs={{0,1},{1,2},{2,3},{3,0},{4,5},{5,6},{6,7},{7,4},{8,9},{9,10},{10,1... | collective-permute-start | bytes 614408 | tf_op jit(solution)/shard_map/ppermute | solution.py:395
  135.2 10.0 %collective-permute-start.9 = (bf16[160,640]{1,0:T(8,128)(2,1)}, bf16[160,640]{1,0:T(8,128)(2,1)S(1)}, u32[]{:S(2)}, u32[]{:S(2)}) collective-permute-start(bf16[160,640]{1,0:T(8,128)(2,1)} %get-tuple-element.50), channel_id=1, source_target_pairs={{0,2},{1,3},{2,0},{3,1},{4,6},{5,7},{6,4},{7,5},{8,10},{9,11},{10,... | collective-permute-start | bytes 614408 | tf_op jit(solution)/shard_map/ppermute | solution.py:395
  (10 other events, 107.9 us)
Sparse Core Ops, SparseCore 0:
  10.1 59.2 all-gather.2

commit v4 on v3

--- a/solution.py
+++ b/solution.py
@@ -171,7 +171,8 @@
             copy.wait()
 
     total = None
-    for n, shift in enumerate((0, 3, 1)):
+    ylo = where_ref[2]
+    for n, shift in enumerate((0, 3 - 2 * ylo, 1 + 2 * ylo)):
         at = pl.multiple_of(lax.rem(where_ref[1] + shift, SIDE) * depth, depth)
         term = jnp.dot(
             acts_ref[:, pl.ds(at, depth)], grad_block[n * depth : (n + 1) * depth],
@@ -391,6 +392,13 @@
     )(where, *pieces)
 
 
+def y_shifted(x, by):
+    pairs = []
+    for ylo, step in ((0, by), (1, -by)):
+        pairs += [(SIDE * ylo + i, SIDE * ylo + (i + step) % SIDE) for i in range(SIDE)]
+    return lax.ppermute(x, ("ylo", "yhi"), pairs)
+
+
 def shifted(x, axis, by):
     return lax.ppermute(x, axis, [(i, (i + by) % SIDE) for i in range(SIDE)])
 
@@ -399,24 +407,24 @@
     replicas = 32
     scale = 1.0 / math.sqrt(attn_out.shape[0])
     toks, width = out_grad.shape
-    where = jnp.stack([lax.axis_index("x"), lax.axis_index("yhi")]).astype(jnp.int32)
+    where = jnp.stack([lax.axis_index(name) for name in ("x", "yhi", "ylo")]).astype(jnp.int32)
 
     acts = lax.all_gather(attn_out.T, "x", axis=0, tiled=True)
     first, swapped = quarter(where, out_grad)
-    up, down = [shifted(first, "yhi", 1)], [shifted(swapped, "yhi", -1)]
+    up, down = [y_shifted(first, 1)], [y_shifted(swapped, -1)]
     every = lax.all_to_all(pack(out_grad), "x", 0, 0, tiled=True)
     every, up[0], down[0] = lax.optimization_barrier((every, up[0], down[0]))
     rest, swapped = others(where, every)
     stored, rest, swapped = lax.optimization_barrier((momentum[0], rest, swapped))
     mom = lax.all_to_all(pack(stored, 60), "x", 0, 0, tiled=True).reshape(SIDE * toks, width // SIDE)
     own = [first, rest]
-    up.append(shifted(rest, "yhi", 1))
-    down.append(shifted(swapped, "yhi", -1))
+    up.append(y_shifted(rest, 1))
+    down.append(y_shifted(swapped, -1))
     over = []
     for above, below in zip(up, down):
         middle = above.shape[0] // 2
-        over.append(shifted(above[:middle], "yhi", 1))
-        over.append(shifted(below[:middle], "yhi", -1))
+        over.append(y_shifted(above[:middle], 1))
+        over.append(y_shifted(below[:middle], -1))
 
     table = basis_table(jnp.tile(kept, width // SIDE // GROUP))
     part, coeff, high, low = near(scale, where, acts, mom, table, own + up + down, 20)

time: 157 us -> 156 us (level)
  starting transfers between devices: 59.2 us -> 57.3 us
    ppermute x0 -> x8, starting transfers between devices: none -> 31.4 us  [y_shifted(): return lax.ppermute(x, ('ylo', 'yhi'), pairs)]
    ppermute x11 -> x3, starting transfers between devices: 37.6 us -> 7.98 us  [shifted(): return lax.ppermute(x, axis, [(i, (i + by) % SIDE) for i in range(SIDE)])]
    ppermute x11 -> x3, waiting for transfers between devices: 19.8 us -> 0.01 us  [shifted(): return lax.ppermute(x, axis, [(i, (i + by) % SIDE) for i in range(SIDE)])]
    ppermute x0 -> x8, waiting for transfers between devices: none -> 19.4 us  [y_shifted(): return lax.ppermute(x, ('ylo', 'yhi'), pairs)]
    all_to_all x1, starting transfers between devices: 8.84 us -> 5.41 us  [per_device(): pieces = lax.all_to_all(pieces, ('x', 'ylo', 'core'), 0, 0, tiled=True)]
    unnamed x36 -> x38, local copies, waits for them, and re-layouts: 2.89 us -> 3.42 us
where the time goes in v4:
time: 156 us; the launch traced here: 153 us
  starting transfers between devices  57.3 us (37%)
  Pallas kernels  27.3 us (18%)
  waiting for transfers between devices  24.2 us (16%)
  blocking collectives  21.9 us (14%)
  between operations  14.4 us (9%)
  local copies, waits for them, and re-layouts  6.33 us (4%)
    ppermute x8, starting transfers between devices, y_shifted(): return lax.ppermute(x, ('ylo', 'yhi'), pairs)  31.4 us
    ppermute x8, waiting for transfers between devices, y_shifted(): return lax.ppermute(x, ('ylo', 'yhi'), pairs)  19.4 us
    all_to_all x1, blocking collectives, per_device(): pieces = lax.all_to_all(summed.reshape(8, *tile), 'z', 0, 0, tiled=True)  16.8 us
    pallas_call x1, Pallas kernels, near(): pl.pallas_call(lambda *refs: near_kernel(scale, *refs), grid_spec=pltpu.P...  9.39 us
    ppermute x3, starting transfers between devices, shifted(): return lax.ppermute(x, axis, [(i, (i + by) % SIDE) for i in range(SIDE)])  7.98 us
    pallas_call x1, Pallas kernels, residual(): pl.pallas_call(lambda *refs: residual_kernel(scale, *refs), in_specs=[SME...  5.68 us
    all_to_all x1, starting transfers between devices, per_device(): pieces = lax.all_to_all(pieces, ('x', 'ylo', 'core'), 0, 0, tiled=True)  5.41 us
    pallas_call x1, Pallas kernels, far(): pl.pallas_call(lambda *refs: far_kernel(scale, *refs), in_specs=[SMEM] +...  5.39 us
  transfers between devices with their start and end apart: 16, of which 5 were waited for; matrix products, arithmetic and copies ran while one was open for 2% of the time, Pallas kernels for 13%

profile of v4, /device:TPU:1, one launch (start us, length us, event | category | flops | bytes accessed | tf_op | source)
XLA Modules:
  0.0 152.6 jit_solution(558414467632703090)
XLA Ops:
  10.0 5.0 %all-to-all-start = ((bf16[4,160,640]{2,1,0:T(8,128)(2,1)}), bf16[4,160,640]{2,1,0:T(8,128)(2,1)S(1)}, u32[]{:S(2)}, u32[]{:S(2)}) async-start(bf16[4,160,640]{2,1,0:T(8,128)(2,1)} %shard_map.59), calls=%async_computation | async-start | bytes 1638400 | tf_op jit(solution)/shard_map/all_to_all | solution.py:415
  15.7 4.2 %collective-permute-start = (bf16[160,640]{1,0:T(8,128)(2,1)S(1)}, bf16[160,640]{1,0:T(8,128)(2,1)S(1)}, u32[]{:S(2)}, u32[]{:S(2)}) collective-permute-start(bf16[160,640]{1,0:T(8,128)(2,1)S(1)} %get-tuple-element.29.refs_4_), channel_id=1, source_target_pairs={{0,4},{4,8},{8,12},{12,0},{256,268},{260,256},{264,260},{268,264},... | collective-permute-start | bytes 614408 | tf_op jit(solution)/shard_map/ppermute | solution.py:399
  19.9 3.6 %collective-permute-start.1 = (bf16[160,640]{1,0:T(8,128)(2,1)S(1)}, bf16[160,640]{1,0:T(8,128)(2,1)S(1)}, u32[]{:S(2)}, u32[]{:S(2)}) collective-permute-start(bf16[160,640]{1,0:T(8,128)(2,1)S(1)} %get-tuple-element.30), channel_id=1, source_target_pairs={{0,12},{4,0},{8,4},{12,8},{256,260},{260,264},{264,268},{268,256},... | collective-permute-start | bytes 614408 | tf_op jit(solution)/shard_map/ppermute | solution.py:399
  24.7 4.1 %collective-permute-done.1.refs_8_ = bf16[160,640]{1,0:T(8,128)(2,1)S(1)} collective-permute-done((bf16[160,640]{1,0:T(8,128)(2,1)S(1)}, bf16[160,640]{1,0:T(8,128)(2,1)S(1)}, u32[]{:S(2)}, u32[]{:S(2)}) %collective-permute-start.1) | collective-permute-done | bytes 204832 | tf_op jit(solution)/shard_map/ppermute | solution.py:399
  30.2 6.1 %collective-permute-start.2 = (bf16[480,640]{1,0:T(8,128)(2,1)S(1)}, bf16[480,640]{1,0:T(8,128)(2,1)}, u32[]{:S(2)}, u32[]{:S(2)}) collective-permute-start(bf16[480,640]{1,0:T(8,128)(2,1)S(1)} %get-tuple-element.35.refs_5_), channel_id=1, source_target_pairs={{0,4},{4,8},{8,12},{12,0},{256,268},{260,256},{264,260},{268,264},... | collective-permute-start | bytes 1843208 | tf_op jit(solution)/shard_map/ppermute | solution.py:399
  39.2 4.0 %all-to-all-start.1 = ((bf16[4,160,640]{2,1,0:T(8,128)(2,1)}), bf16[4,160,640]{2,1,0:T(8,128)(2,1)S(1)}, u32[]{:S(2)}, u32[]{:S(2)}) async-start(bf16[4,160,640]{2,1,0:T(8,128)(2,1)} %shard_map.62), calls=%async_computation.1 | async-start | bytes 1638400 | tf_op jit(solution)/shard_map/all_to_all | solution.py:419
  44.3 4.3 %collective-permute-start.4 = (bf16[80,640]{1,0:T(8,128)(2,1)S(1)}, bf16[80,640]{1,0:T(8,128)(2,1)S(1)}, u32[]{:S(2)}, u32[]{:S(2)}) collective-permute-start(bf16[80,640]{1,0:T(8,128)(2,1)S(1)} %slice.12), channel_id=1, source_target_pairs={{0,4},{4,8},{8,12},{12,0},{256,268},{260,256},{264,260},{268,264},... | collective-permute-start | bytes 307208 | tf_op jit(solution)/shard_map/ppermute | solution.py:399
  48.6 3.1 %collective-permute-start.5 = (bf16[80,640]{1,0:T(8,128)(2,1)S(1)}, bf16[80,640]{1,0:T(8,128)(2,1)S(1)}, u32[]{:S(2)}, u32[]{:S(2)}) collective-permute-start(bf16[80,640]{1,0:T(8,128)(2,1)S(1)} %slice.13), channel_id=1, source_target_pairs={{0,12},{4,0},{8,4},{12,8},{256,260},{260,264},{264,268},{268,256},... | collective-permute-start | bytes 307208 | tf_op jit(solution)/shard_map/ppermute | solution.py:399
  52.7 3.7 %collective-permute-start.6 = (bf16[240,640]{1,0:T(8,128)(2,1)S(1)}, bf16[240,640]{1,0:T(8,128)(2,1)S(1)}, u32[]{:S(2)}, u32[]{:S(2)}) collective-permute-start(bf16[240,640]{1,0:T(8,128)(2,1)S(1)} %slice.16), channel_id=1, source_target_pairs={{0,4},{4,8},{8,12},{12,0},{256,268},{260,256},{264,260},{268,264},... | collective-permute-start | bytes 921608 | tf_op jit(solution)/shard_map/ppermute | solution.py:399
  56.4 11.8 %collective-permute-done.3.refs_9_ = bf16[480,640]{1,0:T(8,128)(2,1)} collective-permute-done((bf16[480,640]{1,0:T(8,128)(2,1)S(1)}, bf16[480,640]{1,0:T(8,128)(2,1)}, u32[]{:S(2)}, u32[]{:S(2)}) %collective-permute-start.3) | collective-permute-done | bytes 614432 | tf_op jit(solution)/shard_map/ppermute | solution.py:399
  69.3 4.5 %collective-permute-start.7 = (bf16[240,640]{1,0:T(8,128)(2,1)S(1)}, bf16[240,640]{1,0:T(8,128)(2,1)S(1)}, u32[]{:S(2)}, u32[]{:S(2)}) collective-permute-start(bf16[240,640]{1,0:T(8,128)(2,1)S(1)} %slice.17), channel_id=1, source_target_pairs={{0,12},{4,0},{8,4},{12,8},{256,260},{260,264},{264,268},{268,256},... | collective-permute-start | bytes 921608 | tf_op jit(solution)/shard_map/ppermute | solution.py:399
  74.7 9.4 %shard_map.63 = (f32[640,640]{1,0:T(8,128)}, f32[640,160]{1,0:T(8,128)}, bf16[640,160]{1,0:T(8,128)(2,1)}, bf16[640,160]{1,0:T(8,128)(2,1)}) custom-call(s32[3]{0:T(128)} %copy-done.6, bf16[640,2560]{1,0:T(8,128)(2,1)} %all-gather.3.cloned.1.call-done.refs_1_, bf16[640,640]{1,0:T(8,128)(2,1)} %bitcast.14, f32[64,160]{1,0:T(8,128)} %cosine_multiply_fusion.refs_3_, ...), custom_call_target="tpu_custom_call" | custom-call | flops 31457280000 | bytes 7372800 | tf_op jit(solution)/shard_map/pallas_call | solution.py:197
  84.1 2.3 %collective-permute-done.7.refs_8_.refs_9_ = bf16[240,640]{1,0:T(8,128)(2,1)S(1)} collective-permute-done((bf16[240,640]{1,0:T(8,128)(2,1)S(1)}, bf16[240,640]{1,0:T(8,128)(2,1)S(1)}, u32[]{:S(2)}, u32[]{:S(2)}) %collective-permute-start.7) | collective-permute-done | bytes 307232 | tf_op jit(solution)/shard_map/ppermute | solution.py:399
  87.1 5.4 %shard_map.64.refs_3_ = f32[16,64,128]{2,1,0:T(8,128)} custom-call(s32[3]{0:T(128)} %copy-done.6, bf16[640,2560]{1,0:T(8,128)(2,1)} %all-gather.3.cloned.1.call-done.refs_1_, f32[640,160]{1,0:T(8,128)} %get-tuple-element.39.refs_2_, bf16[640,160]{1,0:T(8,128)(2,1)} %get-tuple-element.40.refs_3_.refs_4_.refs_1_, ...), custom_call_target="tpu_custom_call" | custom-call | flops 524288000 | bytes 5029888 | tf_op jit(solution)/shard_map/pallas_call | solution.py:279
  92.5 5.4 %all-to-all-start.2 = ((f32[16,64,128]{2,1,0:T(8,128)}), f32[16,64,128]{2,1,0:T(8,128)S(1)}, u32[]{:S(2)}, u32[]{:S(2)}) async-start(f32[16,64,128]{2,1,0:T(8,128)} %shard_map.64.refs_3_), calls=%async_computation.2 | async-start | bytes 1048576 | tf_op jit(solution)/shard_map/all_to_all | solution.py:435
  98.0 5.7 %shard_map.65 = (bf16[160,640]{1,0:T(8,128)(2,1)}, bf16[160,640]{1,0:T(8,128)(2,1)}, bf16[160,640]{1,0:T(8,128)(2,1)}, bf16[160,640]{1,0:T(8,128)(2,1)}) custom-call(s32[3]{0:T(128)} %copy-done.6, bf16[640,2560]{1,0:T(8,128)(2,1)} %all-gather.3.cloned.1.call-done.refs_1_, f32[640,640]{1,0:T(8,128)} %get-tuple-element.42.refs_2_, ...), custom_call_target="tpu_custom_call" | custom-call | flops 917504000 | bytes 2981888 | tf_op jit(solution)/shard_map/pallas_call | solution.py:330
  103.7 4.1 %all-to-all-done.2 = f32[16,64,128]{2,1,0:T(8,128)S(1)} async-done(((f32[16,64,128]{2,1,0:T(8,128)}), f32[16,64,128]{2,1,0:T(8,128)S(1)}, u32[]{:S(2)}, u32[]{:S(2)}) %all-to-all-start.2) | async-done | bytes 524320 | tf_op jit(solution)/shard_map/all_to_all | solution.py:435
  107.8 16.8 %all_to_all.25 = f32[8,32,128]{2,1,0:T(8,128)S(1)} all-to-all(f32[8,32,128]{2,1,0:T(8,128)S(1)} %bitcast.16), channel_id=1, replica_groups=mesh['ylo'=2,'z'=8,'core'=2,'yhi'=4,'x'=4] {'z'}, dimensions={0} | all-to-all | bytes 262144 | tf_op jit(solution)/shard_map/all_to_all | solution.py:439
  125.4 3.5 %all-to-all-start.4 = ((f32[16,32,128]{2,1,0:T(8,128)}), f32[16,32,128]{2,1,0:T(8,128)S(1)}, u32[]{:S(2)}, u32[]{:S(2)}) async-start(f32[16,32,128]{2,1,0:T(8,128)} %broadcast_in_dim.22), calls=%async_computation.4 | async-start | bytes 524288 | tf_op jit(solution)/shard_map/all_to_all | solution.py:442
  128.9 2.5 %collective-permute-start.10 = (bf16[160,640]{1,0:T(8,128)(2,1)}, bf16[160,640]{1,0:T(8,128)(2,1)S(1)}, u32[]{:S(2)}, u32[]{:S(2)}) collective-permute-start(bf16[160,640]{1,0:T(8,128)(2,1)} %get-tuple-element.51), channel_id=1, source_target_pairs={{0,3},{1,0},{2,1},{3,2},{4,7},{5,4},{6,5},{7,6},{8,11},{9,8},{10,9... | collective-permute-start | bytes 614408 | tf_op jit(solution)/shard_map/ppermute | solution.py:403
  131.4 2.8 %collective-permute-start.8 = (bf16[160,640]{1,0:T(8,128)(2,1)}, bf16[160,640]{1,0:T(8,128)(2,1)S(1)}, u32[]{:S(2)}, u32[]{:S(2)}) collective-permute-start(bf16[160,640]{1,0:T(8,128)(2,1)} %get-tuple-element.49), channel_id=1, source_target_pairs={{0,1},{1,2},{2,3},{3,0},{4,5},{5,6},{6,7},{7,4},{8,9},{9,10},{10,1... | collective-permute-start | bytes 614408 | tf_op jit(solution)/shard_map/ppermute | solution.py:403
  134.2 2.7 %collective-permute-start.9 = (bf16[160,640]{1,0:T(8,128)(2,1)}, bf16[160,640]{1,0:T(8,128)(2,1)S(1)}, u32[]{:S(2)}, u32[]{:S(2)}) collective-permute-start(bf16[160,640]{1,0:T(8,128)(2,1)} %get-tuple-element.50), channel_id=1, source_target_pairs={{0,2},{1,3},{2,0},{3,1},{4,6},{5,7},{6,4},{7,5},{8,10},{9,11},{10,... | collective-permute-start | bytes 614408 | tf_op jit(solution)/shard_map/ppermute | solution.py:403
  136.9 5.1 %all-gather = f32[32,32,128]{2,1,0:T(8,128)S(1)} all-gather(f32[16,32,128]{2,1,0:T(8,128)S(1)} %all-to-all-done.4), channel_id=2, replica_groups=mesh['ylo'=2,'z'=8,'core'=2,'yhi'=4,'x'=4] {'core'}, dimensions={0}, use_global_device_ids=true | all-gather | bytes 786432 | tf_op jit(solution)/shard_map/all_gather | solution.py:443
  142.0 2.2 %shard_map.66 = bf16[160,2560]{1,0:T(8,128)(2,1)} custom-call(f32[2,2,4,2,32,128]{5,4,3,2,1,0:T(8,128)S(1)} %bitcast.11, bf16[640,160]{1,0:T(8,128)(2,1)S(1)} %copy-done.2, bf16[640,160]{1,0:T(8,128)(2,1)S(1)} %copy-done.3), custom_call_target="tpu_custom_call" | custom-call | flops 503316480 | bytes 1343488 | tf_op jit(solution)/shard_map/pallas_call | solution.py:364
  (74 shorter events, 15.9 us)
Async XLA Ops:
  7.2 66.6 %all-gather.3.cloned.1.call-start = ((), (), s32[]{:S(2)}) async-start(), calls=%async_computation.5 | async-start | bytes 4096000 | tf_op jit(solution)/shard_map/all_gather | solution.py:412
  10.0 19.5 %all-to-all-start = ((bf16[4,160,640]{2,1,0:T(8,128)(2,1)}), bf16[4,160,640]{2,1,0:T(8,128)(2,1)S(1)}, u32[]{:S(2)}, u32[]{:S(2)}) async-start(bf16[4,160,640]{2,1,0:T(8,128)(2,1)} %shard_map.59), calls=%async_computation | async-start | bytes 1638400 | tf_op jit(solution)/shard_map/all_to_all | solution.py:415
  15.1 54.2 %copy-start.6 = (s32[3]{0:T(128)}, s32[3]{0:T(128)S(1)}, u32[]{:S(2)}) copy-start(s32[3]{0:T(128)S(1)} %pad_add_fusion.where_ref.refs_0_) | copy-start | bytes 40
  15.7 58.2 %copy-start.9 = (bf16[160,640]{1,0:T(8,128)(2,1)}, bf16[160,640]{1,0:T(8,128)(2,1)S(1)}, u32[]{:S(2)}) copy-start(bf16[160,640]{1,0:T(8,128)(2,1)S(1)} %get-tuple-element.29.refs_4_) | copy-start | bytes 614404
  15.7 9.0 %collective-permute-start = (bf16[160,640]{1,0:T(8,128)(2,1)S(1)}, bf16[160,640]{1,0:T(8,128)(2,1)S(1)}, u32[]{:S(2)}, u32[]{:S(2)}) collective-permute-start(bf16[160,640]{1,0:T(8,128)(2,1)S(1)} %get-tuple-element.29.refs_4_), channel_id=1, source_target_pairs={{0,4},{4,8},{8,12},{12,0},{256,268},{260,256},{264,260},{268,264},... | collective-permute-start | bytes 614408 | tf_op jit(solution)/shard_map/ppermute | solution.py:399
  19.9 8.9 %collective-permute-start.1 = (bf16[160,640]{1,0:T(8,128)(2,1)S(1)}, bf16[160,640]{1,0:T(8,128)(2,1)S(1)}, u32[]{:S(2)}, u32[]{:S(2)}) collective-permute-start(bf16[160,640]{1,0:T(8,128)(2,1)S(1)} %get-tuple-element.30), channel_id=1, source_target_pairs={{0,12},{4,0},{8,4},{12,8},{256,260},{260,264},{264,268},{268,256},... | collective-permute-start | bytes 614408 | tf_op jit(solution)/shard_map/ppermute | solution.py:399
  24.7 49.1 %copy-start.15 = (bf16[160,640]{1,0:T(8,128)(2,1)}, bf16[160,640]{1,0:T(8,128)(2,1)S(1)}, u32[]{:S(2)}) copy-start(bf16[160,640]{1,0:T(8,128)(2,1)S(1)} %collective-permute-done.refs_6_) | copy-start | bytes 614404
  30.2 43.7 %copy-start.8 = (bf16[480,640]{1,0:T(8,128)(2,1)}, bf16[480,640]{1,0:T(8,128)(2,1)S(1)}, u32[]{:S(2)}) copy-start(bf16[480,640]{1,0:T(8,128)(2,1)S(1)} %get-tuple-element.35.refs_5_) | copy-start | bytes 1843204
  30.2 21.5 %collective-permute-start.2 = (bf16[480,640]{1,0:T(8,128)(2,1)S(1)}, bf16[480,640]{1,0:T(8,128)(2,1)}, u32[]{:S(2)}, u32[]{:S(2)}) collective-permute-start(bf16[480,640]{1,0:T(8,128)(2,1)S(1)} %get-tuple-element.35.refs_5_), channel_id=1, source_target_pairs={{0,4},{4,8},{8,12},{12,0},{256,268},{260,256},{264,260},{268,264},... | collective-permute-start | bytes 1843208 | tf_op jit(solution)/shard_map/ppermute | solution.py:399
  36.3 32.0 %collective-permute-start.3 = (bf16[480,640]{1,0:T(8,128)(2,1)S(1)}, bf16[480,640]{1,0:T(8,128)(2,1)}, u32[]{:S(2)}, u32[]{:S(2)}) collective-permute-start(bf16[480,640]{1,0:T(8,128)(2,1)S(1)} %get-tuple-element.38), channel_id=1, source_target_pairs={{0,12},{4,0},{8,4},{12,8},{256,260},{260,264},{264,268},{268,256},... | collective-permute-start | bytes 1843208 | tf_op jit(solution)/shard_map/ppermute | solution.py:399
  39.2 34.6 %all-to-all-start.1 = ((bf16[4,160,640]{2,1,0:T(8,128)(2,1)}), bf16[4,160,640]{2,1,0:T(8,128)(2,1)S(1)}, u32[]{:S(2)}, u32[]{:S(2)}) async-start(bf16[4,160,640]{2,1,0:T(8,128)(2,1)} %shard_map.62), calls=%async_computation.1 | async-start | bytes 1638400 | tf_op jit(solution)/shard_map/all_to_all | solution.py:419
  44.3 39.8 %collective-permute-start.4 = (bf16[80,640]{1,0:T(8,128)(2,1)S(1)}, bf16[80,640]{1,0:T(8,128)(2,1)S(1)}, u32[]{:S(2)}, u32[]{:S(2)}) collective-permute-start(bf16[80,640]{1,0:T(8,128)(2,1)S(1)} %slice.12), channel_id=1, source_target_pairs={{0,4},{4,8},{8,12},{12,0},{256,268},{260,256},{264,260},{268,264},... | collective-permute-start | bytes 307208 | tf_op jit(solution)/shard_map/ppermute | solution.py:399
  48.6 35.5 %collective-permute-start.5 = (bf16[80,640]{1,0:T(8,128)(2,1)S(1)}, bf16[80,640]{1,0:T(8,128)(2,1)S(1)}, u32[]{:S(2)}, u32[]{:S(2)}) collective-permute-start(bf16[80,640]{1,0:T(8,128)(2,1)S(1)} %slice.13), channel_id=1, source_target_pairs={{0,12},{4,0},{8,4},{12,8},{256,260},{260,264},{264,268},{268,256},... | collective-permute-start | bytes 307208 | tf_op jit(solution)/shard_map/ppermute | solution.py:399
  52.7 31.4 %collective-permute-start.6 = (bf16[240,640]{1,0:T(8,128)(2,1)S(1)}, bf16[240,640]{1,0:T(8,128)(2,1)S(1)}, u32[]{:S(2)}, u32[]{:S(2)}) collective-permute-start(bf16[240,640]{1,0:T(8,128)(2,1)S(1)} %slice.16), channel_id=1, source_target_pairs={{0,4},{4,8},{8,12},{12,0},{256,268},{260,256},{264,260},{268,264},... | collective-permute-start | bytes 921608 | tf_op jit(solution)/shard_map/ppermute | solution.py:399
  69.3 17.2 %collective-permute-start.7 = (bf16[240,640]{1,0:T(8,128)(2,1)S(1)}, bf16[240,640]{1,0:T(8,128)(2,1)S(1)}, u32[]{:S(2)}, u32[]{:S(2)}) collective-permute-start(bf16[240,640]{1,0:T(8,128)(2,1)S(1)} %slice.17), channel_id=1, source_target_pairs={{0,12},{4,0},{8,4},{12,8},{256,260},{260,264},{264,268},{268,256},... | collective-permute-start | bytes 921608 | tf_op jit(solution)/shard_map/ppermute | solution.py:399
  92.5 15.2 %all-to-all-start.2 = ((f32[16,64,128]{2,1,0:T(8,128)}), f32[16,64,128]{2,1,0:T(8,128)S(1)}, u32[]{:S(2)}, u32[]{:S(2)}) async-start(f32[16,64,128]{2,1,0:T(8,128)} %shard_map.64.refs_3_), calls=%async_computation.2 | async-start | bytes 1048576 | tf_op jit(solution)/shard_map/all_to_all | solution.py:435
  97.9 44.0 %copy-start.2 = (bf16[640,160]{1,0:T(8,128)(2,1)S(1)}, bf16[640,160]{1,0:T(8,128)(2,1)}, u32[]{:S(2)}) copy-start(bf16[640,160]{1,0:T(8,128)(2,1)} %get-tuple-element.40.refs_3_.refs_4_.refs_1_) | copy-start | bytes 614404
  98.0 44.0 %copy-start.3 = (bf16[640,160]{1,0:T(8,128)(2,1)S(1)}, bf16[640,160]{1,0:T(8,128)(2,1)}, u32[]{:S(2)}) copy-start(bf16[640,160]{1,0:T(8,128)(2,1)} %get-tuple-element.41.refs_4_.refs_5_.refs_2_) | copy-start | bytes 614404
  103.7 40.6 %copy-start.5 = (bf16[160,640]{1,0:T(8,128)(2,1)S(1)}, bf16[160,640]{1,0:T(8,128)(2,1)}, u32[]{:S(2)}) copy-start(bf16[160,640]{1,0:T(8,128)(2,1)} %get-tuple-element.52.refs_0_) | copy-start | bytes 614404
  103.7 40.6 %copy-start.7 = (s32[3]{0:T(128)S(1)}, s32[3]{0:T(128)}, u32[]{:S(2)}) copy-start(s32[3]{0:T(128)} %copy-done.6) | copy-start | bytes 40
  125.4 11.5 %all-to-all-start.4 = ((f32[16,32,128]{2,1,0:T(8,128)}), f32[16,32,128]{2,1,0:T(8,128)S(1)}, u32[]{:S(2)}, u32[]{:S(2)}) async-start(f32[16,32,128]{2,1,0:T(8,128)} %broadcast_in_dim.22), calls=%async_computation.4 | async-start | bytes 524288 | tf_op jit(solution)/shard_map/all_to_all | solution.py:442
  128.9 15.3 %collective-permute-start.10 = (bf16[160,640]{1,0:T(8,128)(2,1)}, bf16[160,640]{1,0:T(8,128)(2,1)S(1)}, u32[]{:S(2)}, u32[]{:S(2)}) collective-permute-start(bf16[160,640]{1,0:T(8,128)(2,1)} %get-tuple-element.51), channel_id=1, source_target_pairs={{0,3},{1,0},{2,1},{3,2},{4,7},{5,4},{6,5},{7,6},{8,11},{9,8},{10,9... | collective-permute-start | bytes 614408 | tf_op jit(solution)/shard_map/ppermute | solution.py:403
  131.4 12.8 %collective-permute-start.8 = (bf16[160,640]{1,0:T(8,128)(2,1)}, bf16[160,640]{1,0:T(8,128)(2,1)S(1)}, u32[]{:S(2)}, u32[]{:S(2)}) collective-permute-start(bf16[160,640]{1,0:T(8,128)(2,1)} %get-tuple-element.49), channel_id=1, source_target_pairs={{0,1},{1,2},{2,3},{3,0},{4,5},{5,6},{6,7},{7,4},{8,9},{9,10},{10,1... | collective-permute-start | bytes 614408 | tf_op jit(solution)/shard_map/ppermute | solution.py:403
  134.2 10.0 %collective-permute-start.9 = (bf16[160,640]{1,0:T(8,128)(2,1)}, bf16[160,640]{1,0:T(8,128)(2,1)S(1)}, u32[]{:S(2)}, u32[]{:S(2)}) collective-permute-start(bf16[160,640]{1,0:T(8,128)(2,1)} %get-tuple-element.50), channel_id=1, source_target_pairs={{0,2},{1,3},{2,0},{3,1},{4,6},{5,7},{6,4},{7,5},{8,10},{9,11},{10,... | collective-permute-start | bytes 614408 | tf_op jit(solution)/shard_map/ppermute | solution.py:403
  (11 other events, 99.0 us)
Sparse Core Ops, SparseCore 0:
  10.1 60.0 all-gather.2

commit v5 on v4

--- a/solution.py
+++ b/solution.py
@@ -11,7 +11,6 @@
 KEEP = 16
 BETA = 0.999
 SIDE = 4
-STEPS = 2
 LANES = 128
 
 REP = ("ylo", "z", "core")
@@ -91,6 +90,36 @@
         out_shape=out,
         compiler_params=room(4),
         cost_estimate=cost(0, *[out] * weight),
+    )(whole)
+
+
+def pack_through_kernel(whole_ref, out_ref, block, sems):
+    width = out_ref.shape[2]
+    reads, writes = [], []
+    for q in range(SIDE):
+        span = slice(q * width, (q + 1) * width)
+        reads.append(pltpu.make_async_copy(whole_ref.at[:, span], block.at[q], sems.at[0, q]))
+        writes.append(pltpu.make_async_copy(block.at[q], out_ref.at[q], sems.at[1, q]))
+    for copy in reads:
+        copy.start()
+    for read, write in zip(reads, writes):
+        read.wait()
+        write.start()
+    for copy in writes:
+        copy.wait()
+
+
+def pack_through(whole):
+    rows, width = whole.shape
+    out = jax.ShapeDtypeStruct((SIDE, rows, width // SIDE), whole.dtype)
+    return pl.pallas_call(
+        pack_through_kernel,
+        in_specs=[HBM],
+        out_specs=HBM,
+        out_shape=out,
+        scratch_shapes=[pltpu.VMEM(out.shape, out.dtype), pltpu.SemaphoreType.DMA((2, SIDE))],
+        compiler_params=room(60),
+        cost_estimate=cost(0, out, out),
     )(whole)
 
 
@@ -149,69 +178,61 @@
 
 def near_kernel(scale, where_ref, acts_ref, mom_ref, table_ref, *rest):
     pieces, rest = rest[:6], rest[6:]
-    part_ref, coeff_ref, high_ref, low_ref, grad_block, sems = rest
-    depth = grad_block.shape[0] // 3
-
-    @pl.when(pl.program_id(0) == 0)
-    def _():
-        copies = []
-        own, up, down = pieces[:2], pieces[2:4], pieces[4:]
-        down = [*halves_swapped(down[0]), *halves_swapped(down[1])]
-        for n, refs in enumerate((own, up, down)):
-            block = grad_block.at[n * depth : (n + 1) * depth]
-            copies += rows_in_order(where_ref, refs, block, sems.at[n])
+    part_ref, coeff_ref, high_ref, low_ref, acts_blocks, grad_blocks, mom_block, part_block, sems = rest
+    depth = grad_blocks.shape[1]
+    own, up, down = pieces[:2], pieces[2:4], pieces[4:]
+    down = [*halves_swapped(down[0]), *halves_swapped(down[1])]
+    ylo = where_ref[2]
+    blocks = []
+    for n, (shift, refs) in enumerate(zip((0, 3 - 2 * ylo, 1 + 2 * ylo), (own, up, down))):
+        columns = acts_columns(where_ref, shift, acts_ref, depth)
+        copies = rows_in_order(where_ref, refs, grad_blocks.at[n], sems.at[n])
+        copies.append(pltpu.make_async_copy(columns, acts_blocks.at[n], sems.at[n, 6]))
+        blocks.append(copies)
+    blocks[2].append(pltpu.make_async_copy(mom_ref, mom_block, sems.at[0, 7]))
+    for copies in blocks:
         for copy in copies:
             copy.start()
-        rows, coefs = high_ref.shape
-        table = jnp.concatenate([table_ref[...]] * (rows // GROUP), 0)
-        row = lax.broadcasted_iota(jnp.int32, (rows, coefs), 0) // GROUP
-        col = lax.broadcasted_iota(jnp.int32, (rows, coefs), 1) // KEEP
-        high_ref[...], low_ref[...] = two_parts(jnp.where(row == col, table, 0.0))
+    rows, coefs = high_ref.shape
+    table = jnp.concatenate([table_ref[...]] * (rows // GROUP), 0)
+    row = lax.broadcasted_iota(jnp.int32, (rows, coefs), 0) // GROUP
+    col = lax.broadcasted_iota(jnp.int32, (rows, coefs), 1) // KEEP
+    high, low = two_parts(jnp.where(row == col, table, 0.0))
+    high_ref[...], low_ref[...] = high, low
+    total = None
+    for n, copies in enumerate(blocks):
         for copy in copies:
             copy.wait()
-
-    total = None
-    ylo = where_ref[2]
-    for n, shift in enumerate((0, 3 - 2 * ylo, 1 + 2 * ylo)):
-        at = pl.multiple_of(lax.rem(where_ref[1] + shift, SIDE) * depth, depth)
-        term = jnp.dot(
-            acts_ref[:, pl.ds(at, depth)], grad_block[n * depth : (n + 1) * depth],
-            preferred_element_type=jnp.float32,
-        )
+        term = jnp.dot(acts_blocks[n], grad_blocks[n], preferred_element_type=jnp.float32)
         total = term if total is None else total + term
-    part = BETA * mom_ref[...].astype(jnp.float32) + total * scale
-    part_ref[...] = part
-    coeff_ref[...] = dot_parts(two_parts(part), (high_ref[...], low_ref[...]), ((1,), (0,)))
+    part = BETA * mom_block[...].astype(jnp.float32) + total * scale
+    part_block[...] = part
+    out = pltpu.make_async_copy(part_block, part_ref, sems.at[1, 7])
+    out.start()
+    coeff_ref[...] = dot_parts(two_parts(part), (high, low), ((1,), (0,)))
+    out.wait()
 
 
 def near(scale, where, acts, mom, table, pieces, weight=1):
     feats, toks = acts.shape
-    rows = feats // STEPS
+    depth = toks // SIDE
     outs = pieces[0].shape[1]
     coefs = table.shape[1]
     part = jax.ShapeDtypeStruct((feats, outs), jnp.float32)
     coeff = jax.ShapeDtypeStruct((feats, coefs), jnp.float32)
     basis = jax.ShapeDtypeStruct((outs, coefs), jnp.bfloat16)
-    some = pl.BlockSpec((rows, outs), lambda p, w: (p, 0))
-    whole = pl.BlockSpec(basis.shape, lambda p, w: (0, 0))
     return pl.pallas_call(
         lambda *refs: near_kernel(scale, *refs),
-        grid_spec=pltpu.PrefetchScalarGridSpec(
-            num_scalar_prefetch=1,
-            grid=(STEPS,),
-            in_specs=[
-                pl.BlockSpec((rows, toks), lambda p, w: (p, 0)),
-                some,
-                pl.BlockSpec(table.shape, lambda p, w: (0, 0)),
-                *[HBM] * len(pieces),
-            ],
-            out_specs=[some, pl.BlockSpec((rows, coefs), lambda p, w: (p, 0)), whole, whole],
-            scratch_shapes=[
-                pltpu.VMEM((3 * toks // SIDE, outs), jnp.bfloat16),
-                pltpu.SemaphoreType.DMA((3, 6)),
-            ],
-        ),
+        in_specs=[SMEM, HBM, HBM, VMEM] + [HBM] * len(pieces),
+        out_specs=[HBM] + [VMEM] * 3,
         out_shape=[part, coeff, basis, basis],
+        scratch_shapes=[
+            pltpu.VMEM((3, feats, depth), jnp.bfloat16),
+            pltpu.VMEM((3, depth, outs), jnp.bfloat16),
+            pltpu.VMEM(mom.shape, mom.dtype),
+            pltpu.VMEM(part.shape, part.dtype),
+            pltpu.SemaphoreType.DMA((3, 8)),
+        ],
         compiler_params=room(60),
         cost_estimate=cost(weight * 3 * feats * toks * outs // 2, acts, part, *pieces),
     )(where, acts, mom, table, *pieces)
@@ -289,7 +310,7 @@
             pltpu.VMEM(low.shape, low.dtype),
             pltpu.SemaphoreType.DMA((10,)),
         ],
-        compiler_params=room(60),
+        compiler_params=room(58),
         cost_estimate=cost(4 * coefs * depth * (feats + outs), acts, coeff, out, *pieces),
     )(where, acts, coeff, high, low, *pieces)
 
@@ -412,7 +433,7 @@
     acts = lax.all_gather(attn_out.T, "x", axis=0, tiled=True)
     first, swapped = quarter(where, out_grad)
     up, down = [y_shifted(first, 1)], [y_shifted(swapped, -1)]
-    every = lax.all_to_all(pack(out_grad), "x", 0, 0, tiled=True)
+    every = lax.all_to_all(pack_through(out_grad), "x", 0, 0, tiled=True)
     every, up[0], down[0] = lax.optimization_barrier((every, up[0], down[0]))
     rest, swapped = others(where, every)
     stored, rest, swapped = lax.optimization_barrier((momentum[0], rest, swapped))

time: 156 us -> 155 us (level)
    pallas_call x1 -> x2, Pallas kernels: 9.39 us -> 10.7 us  [the longest x1 8.73 us: near(): pl.pallas_call(lambda *refs: near_kernel(scale, *refs), in_specs=[SMEM, H...]
    unnamed x38 -> x36, local copies, waits for them, and re-layouts: 3.42 us -> 2.28 us
  transfers between devices with their start and end apart: 16 -> 16, of which waited for: 5 -> 5; matrix products, arithmetic and copies ran while one was open for 2% -> 2% of each run, Pallas kernels for 13% -> 14%
where the time goes in v5:
time: 155 us; the launch traced here: 152 us
  starting transfers between devices  56.6 us (37%)
  Pallas kernels  27.7 us (18%)
  waiting for transfers between devices  24.9 us (16%)
  blocking collectives  22 us (14%)
  between operations  14.4 us (9%)
  local copies, waits for them, and re-layouts  5.19 us (3%)
    ppermute x8, starting transfers between devices, y_shifted(): return lax.ppermute(x, ('ylo', 'yhi'), pairs)  31.4 us
    ppermute x8, waiting for transfers between devices, y_shifted(): return lax.ppermute(x, ('ylo', 'yhi'), pairs)  20.1 us
    all_to_all x1, blocking collectives, per_device(): pieces = lax.all_to_all(summed.reshape(8, *tile), 'z', 0, 0, tiled=True)  16.9 us
    pallas_call x1, Pallas kernels, near(): pl.pallas_call(lambda *refs: near_kernel(scale, *refs), in_specs=[SMEM, H...  8.73 us
    ppermute x3, starting transfers between devices, shifted(): return lax.ppermute(x, axis, [(i, (i + by) % SIDE) for i in range(SIDE)])  7.98 us
    pallas_call x1, Pallas kernels, residual(): pl.pallas_call(lambda *refs: residual_kernel(scale, *refs), in_specs=[SME...  5.68 us
    pallas_call x1, Pallas kernels, far(): pl.pallas_call(lambda *refs: far_kernel(scale, *refs), in_specs=[SMEM] +...  5.39 us
    all_gather x1, blocking collectives, per_device(): total = lax.all_gather(spread, 'core', axis=0).reshape(2, 2, 4, 2, *tile)  5.05 us
  transfers between devices with their start and end apart: 16, of which 5 were waited for; matrix products, arithmetic and copies ran while one was open for 2% of the time, Pallas kernels for 14%

profile of v5, /device:TPU:1, one launch (start us, length us, event | category | flops | bytes accessed | tf_op | source)
XLA Modules:
  0.0 151.8 jit_solution(8643482518813025461)
XLA Ops:
  9.9 4.9 %all-to-all-start = ((bf16[4,160,640]{2,1,0:T(8,128)(2,1)}), bf16[4,160,640]{2,1,0:T(8,128)(2,1)S(1)}, u32[]{:S(2)}, u32[]{:S(2)}) async-start(bf16[4,160,640]{2,1,0:T(8,128)(2,1)} %shard_map.59), calls=%async_computation | async-start | bytes 1638400 | tf_op jit(solution)/shard_map/all_to_all | solution.py:436
  15.5 4.2 %collective-permute-start = (bf16[160,640]{1,0:T(8,128)(2,1)S(1)}, bf16[160,640]{1,0:T(8,128)(2,1)S(1)}, u32[]{:S(2)}, u32[]{:S(2)}) collective-permute-start(bf16[160,640]{1,0:T(8,128)(2,1)S(1)} %get-tuple-element.29.refs_4_), channel_id=1, source_target_pairs={{0,4},{4,8},{8,12},{12,0},{256,268},{260,256},{264,260},{268,264},... | collective-permute-start | bytes 614408 | tf_op jit(solution)/shard_map/ppermute | solution.py:420
  19.7 3.6 %collective-permute-start.1 = (bf16[160,640]{1,0:T(8,128)(2,1)S(1)}, bf16[160,640]{1,0:T(8,128)(2,1)S(1)}, u32[]{:S(2)}, u32[]{:S(2)}) collective-permute-start(bf16[160,640]{1,0:T(8,128)(2,1)S(1)} %get-tuple-element.30), channel_id=1, source_target_pairs={{0,12},{4,0},{8,4},{12,8},{256,260},{260,264},{264,268},{268,256},... | collective-permute-start | bytes 614408 | tf_op jit(solution)/shard_map/ppermute | solution.py:420
  24.5 4.1 %collective-permute-done.1.refs_8_ = bf16[160,640]{1,0:T(8,128)(2,1)S(1)} collective-permute-done((bf16[160,640]{1,0:T(8,128)(2,1)S(1)}, bf16[160,640]{1,0:T(8,128)(2,1)S(1)}, u32[]{:S(2)}, u32[]{:S(2)}) %collective-permute-start.1) | collective-permute-done | bytes 204832 | tf_op jit(solution)/shard_map/ppermute | solution.py:420
  30.0 6.1 %collective-permute-start.2 = (bf16[480,640]{1,0:T(8,128)(2,1)S(1)}, bf16[480,640]{1,0:T(8,128)(2,1)}, u32[]{:S(2)}, u32[]{:S(2)}) collective-permute-start(bf16[480,640]{1,0:T(8,128)(2,1)S(1)} %get-tuple-element.35.refs_5_), channel_id=1, source_target_pairs={{0,4},{4,8},{8,12},{12,0},{256,268},{260,256},{264,260},{268,264},... | collective-permute-start | bytes 1843208 | tf_op jit(solution)/shard_map/ppermute | solution.py:420
  39.0 4.0 %all-to-all-start.1 = ((bf16[4,160,640]{2,1,0:T(8,128)(2,1)}), bf16[4,160,640]{2,1,0:T(8,128)(2,1)S(1)}, u32[]{:S(2)}, u32[]{:S(2)}) async-start(bf16[4,160,640]{2,1,0:T(8,128)(2,1)} %shard_map.62), calls=%async_computation.1 | async-start | bytes 1638400 | tf_op jit(solution)/shard_map/all_to_all | solution.py:440
  44.1 4.3 %collective-permute-start.4 = (bf16[80,640]{1,0:T(8,128)(2,1)S(1)}, bf16[80,640]{1,0:T(8,128)(2,1)S(1)}, u32[]{:S(2)}, u32[]{:S(2)}) collective-permute-start(bf16[80,640]{1,0:T(8,128)(2,1)S(1)} %slice.12), channel_id=1, source_target_pairs={{0,4},{4,8},{8,12},{12,0},{256,268},{260,256},{264,260},{268,264},... | collective-permute-start | bytes 307208 | tf_op jit(solution)/shard_map/ppermute | solution.py:420
  48.4 3.1 %collective-permute-start.5 = (bf16[80,640]{1,0:T(8,128)(2,1)S(1)}, bf16[80,640]{1,0:T(8,128)(2,1)S(1)}, u32[]{:S(2)}, u32[]{:S(2)}) collective-permute-start(bf16[80,640]{1,0:T(8,128)(2,1)S(1)} %slice.13), channel_id=1, source_target_pairs={{0,12},{4,0},{8,4},{12,8},{256,260},{260,264},{264,268},{268,256},... | collective-permute-start | bytes 307208 | tf_op jit(solution)/shard_map/ppermute | solution.py:420
  52.5 3.7 %collective-permute-start.6 = (bf16[240,640]{1,0:T(8,128)(2,1)S(1)}, bf16[240,640]{1,0:T(8,128)(2,1)S(1)}, u32[]{:S(2)}, u32[]{:S(2)}) collective-permute-start(bf16[240,640]{1,0:T(8,128)(2,1)S(1)} %slice.16), channel_id=1, source_target_pairs={{0,4},{4,8},{8,12},{12,0},{256,268},{260,256},{264,260},{268,264},... | collective-permute-start | bytes 921608 | tf_op jit(solution)/shard_map/ppermute | solution.py:420
  56.2 11.8 %collective-permute-done.3.refs_9_ = bf16[480,640]{1,0:T(8,128)(2,1)} collective-permute-done((bf16[480,640]{1,0:T(8,128)(2,1)S(1)}, bf16[480,640]{1,0:T(8,128)(2,1)}, u32[]{:S(2)}, u32[]{:S(2)}) %collective-permute-start.3) | collective-permute-done | bytes 614432 | tf_op jit(solution)/shard_map/ppermute | solution.py:420
  69.1 4.5 %collective-permute-start.7 = (bf16[240,640]{1,0:T(8,128)(2,1)S(1)}, bf16[240,640]{1,0:T(8,128)(2,1)S(1)}, u32[]{:S(2)}, u32[]{:S(2)}) collective-permute-start(bf16[240,640]{1,0:T(8,128)(2,1)S(1)} %slice.17), channel_id=1, source_target_pairs={{0,12},{4,0},{8,4},{12,8},{256,260},{260,264},{264,268},{268,256},... | collective-permute-start | bytes 921608 | tf_op jit(solution)/shard_map/ppermute | solution.py:420
  74.5 8.7 %shard_map.63 = (f32[640,640]{1,0:T(8,128)}, f32[640,160]{1,0:T(8,128)}, bf16[640,160]{1,0:T(8,128)(2,1)}, bf16[640,160]{1,0:T(8,128)(2,1)}) custom-call(s32[3]{0:T(128)} %copy-done.5, bf16[640,2560]{1,0:T(8,128)(2,1)} %all-gather.3.cloned.1.call-done.refs_1_, bf16[640,640]{1,0:T(8,128)(2,1)} %bitcast.14, f32[64,160]{1,0:T(8,128)} %cosine_multiply_fusion.refs_3_, ...), custom_call_target="tpu_custom_call" | custom-call | flops 31457280000 | bytes 7372800 | tf_op jit(solution)/shard_map/pallas_call | solution.py:224
  83.3 2.9 %collective-permute-done.7.refs_8_.refs_9_ = bf16[240,640]{1,0:T(8,128)(2,1)S(1)} collective-permute-done((bf16[240,640]{1,0:T(8,128)(2,1)S(1)}, bf16[240,640]{1,0:T(8,128)(2,1)S(1)}, u32[]{:S(2)}, u32[]{:S(2)}) %collective-permute-start.7) | collective-permute-done | bytes 307232 | tf_op jit(solution)/shard_map/ppermute | solution.py:420
  86.9 5.4 %shard_map.64.refs_3_ = f32[16,64,128]{2,1,0:T(8,128)} custom-call(s32[3]{0:T(128)} %copy-done.5, bf16[640,2560]{1,0:T(8,128)(2,1)} %all-gather.3.cloned.1.call-done.refs_1_, f32[640,160]{1,0:T(8,128)} %get-tuple-element.39.refs_2_, bf16[640,160]{1,0:T(8,128)(2,1)} %get-tuple-element.40.refs_3_.refs_4_.refs_1_, ...), custom_call_target="tpu_custom_call" | custom-call | flops 524288000 | bytes 5029888 | tf_op jit(solution)/shard_map/pallas_call | solution.py:300
  92.3 4.8 %all-to-all-start.2 = ((f32[16,64,128]{2,1,0:T(8,128)}), f32[16,64,128]{2,1,0:T(8,128)S(1)}, u32[]{:S(2)}, u32[]{:S(2)}) async-start(f32[16,64,128]{2,1,0:T(8,128)} %shard_map.64.refs_3_), calls=%async_computation.2 | async-start | bytes 1048576 | tf_op jit(solution)/shard_map/all_to_all | solution.py:456
  97.1 5.7 %shard_map.65 = (bf16[160,640]{1,0:T(8,128)(2,1)}, bf16[160,640]{1,0:T(8,128)(2,1)}, bf16[160,640]{1,0:T(8,128)(2,1)}, bf16[160,640]{1,0:T(8,128)(2,1)}) custom-call(s32[3]{0:T(128)} %copy-done.5, bf16[640,2560]{1,0:T(8,128)(2,1)} %all-gather.3.cloned.1.call-done.refs_1_, f32[640,640]{1,0:T(8,128)} %get-tuple-element.42.refs_2_, ...), custom_call_target="tpu_custom_call" | custom-call | flops 917504000 | bytes 2981888 | tf_op jit(solution)/shard_map/pallas_call | solution.py:351
  102.8 4.1 %all-to-all-done.2 = f32[16,64,128]{2,1,0:T(8,128)S(1)} async-done(((f32[16,64,128]{2,1,0:T(8,128)}), f32[16,64,128]{2,1,0:T(8,128)S(1)}, u32[]{:S(2)}, u32[]{:S(2)}) %all-to-all-start.2) | async-done | bytes 524320 | tf_op jit(solution)/shard_map/all_to_all | solution.py:456
  106.9 16.9 %all_to_all.25 = f32[8,32,128]{2,1,0:T(8,128)S(1)} all-to-all(f32[8,32,128]{2,1,0:T(8,128)S(1)} %bitcast.16), channel_id=1, replica_groups=mesh['ylo'=2,'z'=8,'core'=2,'yhi'=4,'x'=4] {'z'}, dimensions={0} | all-to-all | bytes 262144 | tf_op jit(solution)/shard_map/all_to_all | solution.py:460
  124.6 3.5 %all-to-all-start.4 = ((f32[16,32,128]{2,1,0:T(8,128)}), f32[16,32,128]{2,1,0:T(8,128)S(1)}, u32[]{:S(2)}, u32[]{:S(2)}) async-start(f32[16,32,128]{2,1,0:T(8,128)} %broadcast_in_dim.22), calls=%async_computation.4 | async-start | bytes 524288 | tf_op jit(solution)/shard_map/all_to_all | solution.py:463
  128.1 2.5 %collective-permute-start.10 = (bf16[160,640]{1,0:T(8,128)(2,1)}, bf16[160,640]{1,0:T(8,128)(2,1)S(1)}, u32[]{:S(2)}, u32[]{:S(2)}) collective-permute-start(bf16[160,640]{1,0:T(8,128)(2,1)} %get-tuple-element.51), channel_id=1, source_target_pairs={{0,3},{1,0},{2,1},{3,2},{4,7},{5,4},{6,5},{7,6},{8,11},{9,8},{10,9... | collective-permute-start | bytes 614408 | tf_op jit(solution)/shard_map/ppermute | solution.py:424
  130.6 2.8 %collective-permute-start.8 = (bf16[160,640]{1,0:T(8,128)(2,1)}, bf16[160,640]{1,0:T(8,128)(2,1)S(1)}, u32[]{:S(2)}, u32[]{:S(2)}) collective-permute-start(bf16[160,640]{1,0:T(8,128)(2,1)} %get-tuple-element.49), channel_id=1, source_target_pairs={{0,1},{1,2},{2,3},{3,0},{4,5},{5,6},{6,7},{7,4},{8,9},{9,10},{10,1... | collective-permute-start | bytes 614408 | tf_op jit(solution)/shard_map/ppermute | solution.py:424
  133.4 2.7 %collective-permute-start.9 = (bf16[160,640]{1,0:T(8,128)(2,1)}, bf16[160,640]{1,0:T(8,128)(2,1)S(1)}, u32[]{:S(2)}, u32[]{:S(2)}) collective-permute-start(bf16[160,640]{1,0:T(8,128)(2,1)} %get-tuple-element.50), channel_id=1, source_target_pairs={{0,2},{1,3},{2,0},{3,1},{4,6},{5,7},{6,4},{7,5},{8,10},{9,11},{10,... | collective-permute-start | bytes 614408 | tf_op jit(solution)/shard_map/ppermute | solution.py:424
  136.1 5.1 %all-gather = f32[32,32,128]{2,1,0:T(8,128)S(1)} all-gather(f32[16,32,128]{2,1,0:T(8,128)S(1)} %all-to-all-done.4), channel_id=2, replica_groups=mesh['ylo'=2,'z'=8,'core'=2,'yhi'=4,'x'=4] {'core'}, dimensions={0}, use_global_device_ids=true | all-gather | bytes 786432 | tf_op jit(solution)/shard_map/all_gather | solution.py:464
  141.2 2.2 %shard_map.66 = bf16[160,2560]{1,0:T(8,128)(2,1)} custom-call(f32[2,2,4,2,32,128]{5,4,3,2,1,0:T(8,128)S(1)} %bitcast.11, bf16[640,160]{1,0:T(8,128)(2,1)S(1)} %copy-done.1, bf16[640,160]{1,0:T(8,128)(2,1)S(1)} %copy-done.2), custom_call_target="tpu_custom_call" | custom-call | flops 503316480 | bytes 1343488 | tf_op jit(solution)/shard_map/pallas_call | solution.py:385
  (72 shorter events, 15.8 us)
Async XLA Ops:
  7.2 66.4 %all-gather.3.cloned.1.call-start = ((), (), s32[]{:S(2)}) async-start(), calls=%async_computation.5 | async-start | bytes 4096000 | tf_op jit(solution)/shard_map/all_gather | solution.py:433
  9.9 19.4 %all-to-all-start = ((bf16[4,160,640]{2,1,0:T(8,128)(2,1)}), bf16[4,160,640]{2,1,0:T(8,128)(2,1)S(1)}, u32[]{:S(2)}, u32[]{:S(2)}) async-start(bf16[4,160,640]{2,1,0:T(8,128)(2,1)} %shard_map.59), calls=%async_computation | async-start | bytes 1638400 | tf_op jit(solution)/shard_map/all_to_all | solution.py:436
  14.9 54.2 %copy-start.5 = (s32[3]{0:T(128)}, s32[3]{0:T(128)S(1)}, u32[]{:S(2)}) copy-start(s32[3]{0:T(128)S(1)} %pad_add_fusion.where_ref.refs_0_) | copy-start | bytes 40
  15.4 58.2 %copy-start.8 = (bf16[160,640]{1,0:T(8,128)(2,1)}, bf16[160,640]{1,0:T(8,128)(2,1)S(1)}, u32[]{:S(2)}) copy-start(bf16[160,640]{1,0:T(8,128)(2,1)S(1)} %get-tuple-element.29.refs_4_) | copy-start | bytes 614404
  15.5 9.0 %collective-permute-start = (bf16[160,640]{1,0:T(8,128)(2,1)S(1)}, bf16[160,640]{1,0:T(8,128)(2,1)S(1)}, u32[]{:S(2)}, u32[]{:S(2)}) collective-permute-start(bf16[160,640]{1,0:T(8,128)(2,1)S(1)} %get-tuple-element.29.refs_4_), channel_id=1, source_target_pairs={{0,4},{4,8},{8,12},{12,0},{256,268},{260,256},{264,260},{268,264},... | collective-permute-start | bytes 614408 | tf_op jit(solution)/shard_map/ppermute | solution.py:420
  19.7 8.9 %collective-permute-start.1 = (bf16[160,640]{1,0:T(8,128)(2,1)S(1)}, bf16[160,640]{1,0:T(8,128)(2,1)S(1)}, u32[]{:S(2)}, u32[]{:S(2)}) collective-permute-start(bf16[160,640]{1,0:T(8,128)(2,1)S(1)} %get-tuple-element.30), channel_id=1, source_target_pairs={{0,12},{4,0},{8,4},{12,8},{256,260},{260,264},{264,268},{268,256},... | collective-permute-start | bytes 614408 | tf_op jit(solution)/shard_map/ppermute | solution.py:420
  24.5 49.1 %copy-start.14 = (bf16[160,640]{1,0:T(8,128)(2,1)}, bf16[160,640]{1,0:T(8,128)(2,1)S(1)}, u32[]{:S(2)}) copy-start(bf16[160,640]{1,0:T(8,128)(2,1)S(1)} %collective-permute-done.refs_6_) | copy-start | bytes 614404
  29.9 43.7 %copy-start.7 = (bf16[480,640]{1,0:T(8,128)(2,1)}, bf16[480,640]{1,0:T(8,128)(2,1)S(1)}, u32[]{:S(2)}) copy-start(bf16[480,640]{1,0:T(8,128)(2,1)S(1)} %get-tuple-element.35.refs_5_) | copy-start | bytes 1843204
  30.0 21.5 %collective-permute-start.2 = (bf16[480,640]{1,0:T(8,128)(2,1)S(1)}, bf16[480,640]{1,0:T(8,128)(2,1)}, u32[]{:S(2)}, u32[]{:S(2)}) collective-permute-start(bf16[480,640]{1,0:T(8,128)(2,1)S(1)} %get-tuple-element.35.refs_5_), channel_id=1, source_target_pairs={{0,4},{4,8},{8,12},{12,0},{256,268},{260,256},{264,260},{268,264},... | collective-permute-start | bytes 1843208 | tf_op jit(solution)/shard_map/ppermute | solution.py:420
  36.1 32.0 %collective-permute-start.3 = (bf16[480,640]{1,0:T(8,128)(2,1)S(1)}, bf16[480,640]{1,0:T(8,128)(2,1)}, u32[]{:S(2)}, u32[]{:S(2)}) collective-permute-start(bf16[480,640]{1,0:T(8,128)(2,1)S(1)} %get-tuple-element.38), channel_id=1, source_target_pairs={{0,12},{4,0},{8,4},{12,8},{256,260},{260,264},{264,268},{268,256},... | collective-permute-start | bytes 1843208 | tf_op jit(solution)/shard_map/ppermute | solution.py:420
  39.0 34.6 %all-to-all-start.1 = ((bf16[4,160,640]{2,1,0:T(8,128)(2,1)}), bf16[4,160,640]{2,1,0:T(8,128)(2,1)S(1)}, u32[]{:S(2)}, u32[]{:S(2)}) async-start(bf16[4,160,640]{2,1,0:T(8,128)(2,1)} %shard_map.62), calls=%async_computation.1 | async-start | bytes 1638400 | tf_op jit(solution)/shard_map/all_to_all | solution.py:440
  44.1 39.1 %collective-permute-start.4 = (bf16[80,640]{1,0:T(8,128)(2,1)S(1)}, bf16[80,640]{1,0:T(8,128)(2,1)S(1)}, u32[]{:S(2)}, u32[]{:S(2)}) collective-permute-start(bf16[80,640]{1,0:T(8,128)(2,1)S(1)} %slice.12), channel_id=1, source_target_pairs={{0,4},{4,8},{8,12},{12,0},{256,268},{260,256},{264,260},{268,264},... | collective-permute-start | bytes 307208 | tf_op jit(solution)/shard_map/ppermute | solution.py:420
  48.4 34.9 %collective-permute-start.5 = (bf16[80,640]{1,0:T(8,128)(2,1)S(1)}, bf16[80,640]{1,0:T(8,128)(2,1)S(1)}, u32[]{:S(2)}, u32[]{:S(2)}) collective-permute-start(bf16[80,640]{1,0:T(8,128)(2,1)S(1)} %slice.13), channel_id=1, source_target_pairs={{0,12},{4,0},{8,4},{12,8},{256,260},{260,264},{264,268},{268,256},... | collective-permute-start | bytes 307208 | tf_op jit(solution)/shard_map/ppermute | solution.py:420
  52.5 30.7 %collective-permute-start.6 = (bf16[240,640]{1,0:T(8,128)(2,1)S(1)}, bf16[240,640]{1,0:T(8,128)(2,1)S(1)}, u32[]{:S(2)}, u32[]{:S(2)}) collective-permute-start(bf16[240,640]{1,0:T(8,128)(2,1)S(1)} %slice.16), channel_id=1, source_target_pairs={{0,4},{4,8},{8,12},{12,0},{256,268},{260,256},{264,260},{268,264},... | collective-permute-start | bytes 921608 | tf_op jit(solution)/shard_map/ppermute | solution.py:420
  69.1 17.1 %collective-permute-start.7 = (bf16[240,640]{1,0:T(8,128)(2,1)S(1)}, bf16[240,640]{1,0:T(8,128)(2,1)S(1)}, u32[]{:S(2)}, u32[]{:S(2)}) collective-permute-start(bf16[240,640]{1,0:T(8,128)(2,1)S(1)} %slice.17), channel_id=1, source_target_pairs={{0,12},{4,0},{8,4},{12,8},{256,260},{260,264},{264,268},{268,256},... | collective-permute-start | bytes 921608 | tf_op jit(solution)/shard_map/ppermute | solution.py:420
  92.3 14.6 %all-to-all-start.2 = ((f32[16,64,128]{2,1,0:T(8,128)}), f32[16,64,128]{2,1,0:T(8,128)S(1)}, u32[]{:S(2)}, u32[]{:S(2)}) async-start(f32[16,64,128]{2,1,0:T(8,128)} %shard_map.64.refs_3_), calls=%async_computation.2 | async-start | bytes 1048576 | tf_op jit(solution)/shard_map/all_to_all | solution.py:456
  97.1 44.1 %copy-start.1 = (bf16[640,160]{1,0:T(8,128)(2,1)S(1)}, bf16[640,160]{1,0:T(8,128)(2,1)}, u32[]{:S(2)}) copy-start(bf16[640,160]{1,0:T(8,128)(2,1)} %get-tuple-element.40.refs_3_.refs_4_.refs_1_) | copy-start | bytes 614404
  97.1 44.1 %copy-start.2 = (bf16[640,160]{1,0:T(8,128)(2,1)S(1)}, bf16[640,160]{1,0:T(8,128)(2,1)}, u32[]{:S(2)}) copy-start(bf16[640,160]{1,0:T(8,128)(2,1)} %get-tuple-element.41.refs_4_.refs_5_.refs_2_) | copy-start | bytes 614404
  102.8 40.6 %copy-start.4 = (bf16[160,640]{1,0:T(8,128)(2,1)S(1)}, bf16[160,640]{1,0:T(8,128)(2,1)}, u32[]{:S(2)}) copy-start(bf16[160,640]{1,0:T(8,128)(2,1)} %get-tuple-element.52.refs_0_) | copy-start | bytes 614404
  102.8 40.6 %copy-start.6 = (s32[3]{0:T(128)S(1)}, s32[3]{0:T(128)}, u32[]{:S(2)}) copy-start(s32[3]{0:T(128)} %copy-done.5) | copy-start | bytes 40
  124.6 11.5 %all-to-all-start.4 = ((f32[16,32,128]{2,1,0:T(8,128)}), f32[16,32,128]{2,1,0:T(8,128)S(1)}, u32[]{:S(2)}, u32[]{:S(2)}) async-start(f32[16,32,128]{2,1,0:T(8,128)} %broadcast_in_dim.22), calls=%async_computation.4 | async-start | bytes 524288 | tf_op jit(solution)/shard_map/all_to_all | solution.py:463
  128.1 15.3 %collective-permute-start.10 = (bf16[160,640]{1,0:T(8,128)(2,1)}, bf16[160,640]{1,0:T(8,128)(2,1)S(1)}, u32[]{:S(2)}, u32[]{:S(2)}) collective-permute-start(bf16[160,640]{1,0:T(8,128)(2,1)} %get-tuple-element.51), channel_id=1, source_target_pairs={{0,3},{1,0},{2,1},{3,2},{4,7},{5,4},{6,5},{7,6},{8,11},{9,8},{10,9... | collective-permute-start | bytes 614408 | tf_op jit(solution)/shard_map/ppermute | solution.py:424
  130.6 12.8 %collective-permute-start.8 = (bf16[160,640]{1,0:T(8,128)(2,1)}, bf16[160,640]{1,0:T(8,128)(2,1)S(1)}, u32[]{:S(2)}, u32[]{:S(2)}) collective-permute-start(bf16[160,640]{1,0:T(8,128)(2,1)} %get-tuple-element.49), channel_id=1, source_target_pairs={{0,1},{1,2},{2,3},{3,0},{4,5},{5,6},{6,7},{7,4},{8,9},{9,10},{10,1... | collective-permute-start | bytes 614408 | tf_op jit(solution)/shard_map/ppermute | solution.py:424
  133.4 10.0 %collective-permute-start.9 = (bf16[160,640]{1,0:T(8,128)(2,1)}, bf16[160,640]{1,0:T(8,128)(2,1)S(1)}, u32[]{:S(2)}, u32[]{:S(2)}) collective-permute-start(bf16[160,640]{1,0:T(8,128)(2,1)} %get-tuple-element.50), channel_id=1, source_target_pairs={{0,2},{1,3},{2,0},{3,1},{4,6},{5,7},{6,4},{7,5},{8,10},{9,11},{10,... | collective-permute-start | bytes 614408 | tf_op jit(solution)/shard_map/ppermute | solution.py:424
  (10 other events, 101.1 us)
Sparse Core Ops, SparseCore 0:
  10.1 60.1 all-gather.2

commit v6 on v5

--- a/solution.py
+++ b/solution.py
@@ -281,7 +281,15 @@
         return jnp.dot(a, b, preferred_element_type=jnp.float32)
 
     grad = grad_block[...]
-    high, low = two_parts(dot(grad, high_block[...]) + dot(grad, low_block[...]))
+    encoded = []
+    for start in range(0, depth, 256):
+        stop = min(start + 256, depth)
+        span = slice(start // GROUP * KEEP, stop // GROUP * KEEP)
+        both = jnp.concatenate([high_block[start:stop, span], low_block[start:stop, span]], 1)
+        parts = dot(grad[:, start:stop], both)
+        wide = span.stop - span.start
+        encoded.append(parts[:, :wide] + parts[:, wide:])
+    high, low = two_parts(jnp.concatenate(encoded, 1))
     for copy in last:
         copy.wait()
     acts = acts_block[...]

time: 155 us -> 154 us (level)
  no operation moved by 1% of the time
where the time goes in v6:
time: 154 us; the launch traced here: 151 us
  starting transfers between devices  56.6 us (37%)
  Pallas kernels  27 us (18%)
  waiting for transfers between devices  24.9 us (16%)
  blocking collectives  22 us (14%)
  between operations  14.4 us (9%)
  local copies, waits for them, and re-layouts  5.19 us (3%)
    ppermute x8, starting transfers between devices, y_shifted(): return lax.ppermute(x, ('ylo', 'yhi'), pairs)  31.4 us
    ppermute x8, waiting for transfers between devices, y_shifted(): return lax.ppermute(x, ('ylo', 'yhi'), pairs)  20.1 us
    all_to_all x1, blocking collectives, per_device(): pieces = lax.all_to_all(summed.reshape(8, *tile), 'z', 0, 0, tiled=True)  16.9 us
    pallas_call x1, Pallas kernels, near(): pl.pallas_call(lambda *refs: near_kernel(scale, *refs), in_specs=[SMEM, H...  8.73 us
    ppermute x3, starting transfers between devices, shifted(): return lax.ppermute(x, axis, [(i, (i + by) % SIDE) for i in range(SIDE)])  7.98 us
    pallas_call x1, Pallas kernels, residual(): pl.pallas_call(lambda *refs: residual_kernel(scale, *refs), in_specs=[SME...  5.69 us
    all_gather x1, blocking collectives, per_device(): total = lax.all_gather(spread, 'core', axis=0).reshape(2, 2, 4, 2, *tile)  5.05 us
    all_to_all x1, starting transfers between devices, per_device(): every = lax.all_to_all(pack_through(out_grad), 'x', 0, 0, tiled=True)  4.85 us
  transfers between devices with their start and end apart: 16, of which 5 were waited for; matrix products, arithmetic and copies ran while one was open for 2% of the time, Pallas kernels for 14%

profile of v6, /device:TPU:1, one launch (start us, length us, event | category | flops | bytes accessed | tf_op | source)
XLA Modules:
  0.0 151.1 jit_solution(7592005327962226235)
XLA Ops:
  9.9 4.9 %all-to-all-start = ((bf16[4,160,640]{2,1,0:T(8,128)(2,1)}), bf16[4,160,640]{2,1,0:T(8,128)(2,1)S(1)}, u32[]{:S(2)}, u32[]{:S(2)}) async-start(bf16[4,160,640]{2,1,0:T(8,128)(2,1)} %shard_map.59), calls=%async_computation | async-start | bytes 1638400 | tf_op jit(solution)/shard_map/all_to_all | solution.py:444
  15.5 4.2 %collective-permute-start = (bf16[160,640]{1,0:T(8,128)(2,1)S(1)}, bf16[160,640]{1,0:T(8,128)(2,1)S(1)}, u32[]{:S(2)}, u32[]{:S(2)}) collective-permute-start(bf16[160,640]{1,0:T(8,128)(2,1)S(1)} %get-tuple-element.29.refs_4_), channel_id=1, source_target_pairs={{0,4},{4,8},{8,12},{12,0},{256,268},{260,256},{264,260},{268,264},... | collective-permute-start | bytes 614408 | tf_op jit(solution)/shard_map/ppermute | solution.py:428
  19.7 3.6 %collective-permute-start.1 = (bf16[160,640]{1,0:T(8,128)(2,1)S(1)}, bf16[160,640]{1,0:T(8,128)(2,1)S(1)}, u32[]{:S(2)}, u32[]{:S(2)}) collective-permute-start(bf16[160,640]{1,0:T(8,128)(2,1)S(1)} %get-tuple-element.30), channel_id=1, source_target_pairs={{0,12},{4,0},{8,4},{12,8},{256,260},{260,264},{264,268},{268,256},... | collective-permute-start | bytes 614408 | tf_op jit(solution)/shard_map/ppermute | solution.py:428
  24.5 4.1 %collective-permute-done.1.refs_8_ = bf16[160,640]{1,0:T(8,128)(2,1)S(1)} collective-permute-done((bf16[160,640]{1,0:T(8,128)(2,1)S(1)}, bf16[160,640]{1,0:T(8,128)(2,1)S(1)}, u32[]{:S(2)}, u32[]{:S(2)}) %collective-permute-start.1) | collective-permute-done | bytes 204832 | tf_op jit(solution)/shard_map/ppermute | solution.py:428
  30.0 6.1 %collective-permute-start.2 = (bf16[480,640]{1,0:T(8,128)(2,1)S(1)}, bf16[480,640]{1,0:T(8,128)(2,1)}, u32[]{:S(2)}, u32[]{:S(2)}) collective-permute-start(bf16[480,640]{1,0:T(8,128)(2,1)S(1)} %get-tuple-element.35.refs_5_), channel_id=1, source_target_pairs={{0,4},{4,8},{8,12},{12,0},{256,268},{260,256},{264,260},{268,264},... | collective-permute-start | bytes 1843208 | tf_op jit(solution)/shard_map/ppermute | solution.py:428
  39.0 4.0 %all-to-all-start.1 = ((bf16[4,160,640]{2,1,0:T(8,128)(2,1)}), bf16[4,160,640]{2,1,0:T(8,128)(2,1)S(1)}, u32[]{:S(2)}, u32[]{:S(2)}) async-start(bf16[4,160,640]{2,1,0:T(8,128)(2,1)} %shard_map.62), calls=%async_computation.1 | async-start | bytes 1638400 | tf_op jit(solution)/shard_map/all_to_all | solution.py:448
  44.1 4.3 %collective-permute-start.4 = (bf16[80,640]{1,0:T(8,128)(2,1)S(1)}, bf16[80,640]{1,0:T(8,128)(2,1)S(1)}, u32[]{:S(2)}, u32[]{:S(2)}) collective-permute-start(bf16[80,640]{1,0:T(8,128)(2,1)S(1)} %slice.12), channel_id=1, source_target_pairs={{0,4},{4,8},{8,12},{12,0},{256,268},{260,256},{264,260},{268,264},... | collective-permute-start | bytes 307208 | tf_op jit(solution)/shard_map/ppermute | solution.py:428
  48.4 3.1 %collective-permute-start.5 = (bf16[80,640]{1,0:T(8,128)(2,1)S(1)}, bf16[80,640]{1,0:T(8,128)(2,1)S(1)}, u32[]{:S(2)}, u32[]{:S(2)}) collective-permute-start(bf16[80,640]{1,0:T(8,128)(2,1)S(1)} %slice.13), channel_id=1, source_target_pairs={{0,12},{4,0},{8,4},{12,8},{256,260},{260,264},{264,268},{268,256},... | collective-permute-start | bytes 307208 | tf_op jit(solution)/shard_map/ppermute | solution.py:428
  52.5 3.7 %collective-permute-start.6 = (bf16[240,640]{1,0:T(8,128)(2,1)S(1)}, bf16[240,640]{1,0:T(8,128)(2,1)S(1)}, u32[]{:S(2)}, u32[]{:S(2)}) collective-permute-start(bf16[240,640]{1,0:T(8,128)(2,1)S(1)} %slice.16), channel_id=1, source_target_pairs={{0,4},{4,8},{8,12},{12,0},{256,268},{260,256},{264,260},{268,264},... | collective-permute-start | bytes 921608 | tf_op jit(solution)/shard_map/ppermute | solution.py:428
  56.2 11.8 %collective-permute-done.3.refs_9_ = bf16[480,640]{1,0:T(8,128)(2,1)} collective-permute-done((bf16[480,640]{1,0:T(8,128)(2,1)S(1)}, bf16[480,640]{1,0:T(8,128)(2,1)}, u32[]{:S(2)}, u32[]{:S(2)}) %collective-permute-start.3) | collective-permute-done | bytes 614432 | tf_op jit(solution)/shard_map/ppermute | solution.py:428
  69.1 4.5 %collective-permute-start.7 = (bf16[240,640]{1,0:T(8,128)(2,1)S(1)}, bf16[240,640]{1,0:T(8,128)(2,1)S(1)}, u32[]{:S(2)}, u32[]{:S(2)}) collective-permute-start(bf16[240,640]{1,0:T(8,128)(2,1)S(1)} %slice.17), channel_id=1, source_target_pairs={{0,12},{4,0},{8,4},{12,8},{256,260},{260,264},{264,268},{268,256},... | collective-permute-start | bytes 921608 | tf_op jit(solution)/shard_map/ppermute | solution.py:428
  74.5 8.7 %shard_map.63 = (f32[640,640]{1,0:T(8,128)}, f32[640,160]{1,0:T(8,128)}, bf16[640,160]{1,0:T(8,128)(2,1)}, bf16[640,160]{1,0:T(8,128)(2,1)}) custom-call(s32[3]{0:T(128)} %copy-done.5, bf16[640,2560]{1,0:T(8,128)(2,1)} %all-gather.3.cloned.1.call-done.refs_1_, bf16[640,640]{1,0:T(8,128)(2,1)} %bitcast.14, f32[64,160]{1,0:T(8,128)} %cosine_multiply_fusion.refs_3_, ...), custom_call_target="tpu_custom_call" | custom-call | flops 31457280000 | bytes 7372800 | tf_op jit(solution)/shard_map/pallas_call | solution.py:224
  83.3 2.9 %collective-permute-done.7.refs_8_.refs_9_ = bf16[240,640]{1,0:T(8,128)(2,1)S(1)} collective-permute-done((bf16[240,640]{1,0:T(8,128)(2,1)S(1)}, bf16[240,640]{1,0:T(8,128)(2,1)S(1)}, u32[]{:S(2)}, u32[]{:S(2)}) %collective-permute-start.7) | collective-permute-done | bytes 307232 | tf_op jit(solution)/shard_map/ppermute | solution.py:428
  86.9 4.7 %shard_map.64.refs_3_ = f32[16,64,128]{2,1,0:T(8,128)} custom-call(s32[3]{0:T(128)} %copy-done.5, bf16[640,2560]{1,0:T(8,128)(2,1)} %all-gather.3.cloned.1.call-done.refs_1_, f32[640,160]{1,0:T(8,128)} %get-tuple-element.39.refs_2_, bf16[640,160]{1,0:T(8,128)(2,1)} %get-tuple-element.40.refs_3_.refs_4_.refs_1_, ...), custom_call_target="tpu_custom_call" | custom-call | flops 524288000 | bytes 5029888 | tf_op jit(solution)/shard_map/pallas_call | solution.py:308
  91.6 4.8 %all-to-all-start.2 = ((f32[16,64,128]{2,1,0:T(8,128)}), f32[16,64,128]{2,1,0:T(8,128)S(1)}, u32[]{:S(2)}, u32[]{:S(2)}) async-start(f32[16,64,128]{2,1,0:T(8,128)} %shard_map.64.refs_3_), calls=%async_computation.2 | async-start | bytes 1048576 | tf_op jit(solution)/shard_map/all_to_all | solution.py:464
  96.4 5.7 %shard_map.65 = (bf16[160,640]{1,0:T(8,128)(2,1)}, bf16[160,640]{1,0:T(8,128)(2,1)}, bf16[160,640]{1,0:T(8,128)(2,1)}, bf16[160,640]{1,0:T(8,128)(2,1)}) custom-call(s32[3]{0:T(128)} %copy-done.5, bf16[640,2560]{1,0:T(8,128)(2,1)} %all-gather.3.cloned.1.call-done.refs_1_, f32[640,640]{1,0:T(8,128)} %get-tuple-element.42.refs_2_, ...), custom_call_target="tpu_custom_call" | custom-call | flops 917504000 | bytes 2981888 | tf_op jit(solution)/shard_map/pallas_call | solution.py:359
  102.1 4.1 %all-to-all-done.2 = f32[16,64,128]{2,1,0:T(8,128)S(1)} async-done(((f32[16,64,128]{2,1,0:T(8,128)}), f32[16,64,128]{2,1,0:T(8,128)S(1)}, u32[]{:S(2)}, u32[]{:S(2)}) %all-to-all-start.2) | async-done | bytes 524320 | tf_op jit(solution)/shard_map/all_to_all | solution.py:464
  106.2 16.9 %all_to_all.25 = f32[8,32,128]{2,1,0:T(8,128)S(1)} all-to-all(f32[8,32,128]{2,1,0:T(8,128)S(1)} %bitcast.16), channel_id=1, replica_groups=mesh['ylo'=2,'z'=8,'core'=2,'yhi'=4,'x'=4] {'z'}, dimensions={0} | all-to-all | bytes 262144 | tf_op jit(solution)/shard_map/all_to_all | solution.py:468
  123.9 3.5 %all-to-all-start.4 = ((f32[16,32,128]{2,1,0:T(8,128)}), f32[16,32,128]{2,1,0:T(8,128)S(1)}, u32[]{:S(2)}, u32[]{:S(2)}) async-start(f32[16,32,128]{2,1,0:T(8,128)} %broadcast_in_dim.22), calls=%async_computation.4 | async-start | bytes 524288 | tf_op jit(solution)/shard_map/all_to_all | solution.py:471
  127.4 2.5 %collective-permute-start.10 = (bf16[160,640]{1,0:T(8,128)(2,1)}, bf16[160,640]{1,0:T(8,128)(2,1)S(1)}, u32[]{:S(2)}, u32[]{:S(2)}) collective-permute-start(bf16[160,640]{1,0:T(8,128)(2,1)} %get-tuple-element.51), channel_id=1, source_target_pairs={{0,3},{1,0},{2,1},{3,2},{4,7},{5,4},{6,5},{7,6},{8,11},{9,8},{10,9... | collective-permute-start | bytes 614408 | tf_op jit(solution)/shard_map/ppermute | solution.py:432
  129.9 2.8 %collective-permute-start.8 = (bf16[160,640]{1,0:T(8,128)(2,1)}, bf16[160,640]{1,0:T(8,128)(2,1)S(1)}, u32[]{:S(2)}, u32[]{:S(2)}) collective-permute-start(bf16[160,640]{1,0:T(8,128)(2,1)} %get-tuple-element.49), channel_id=1, source_target_pairs={{0,1},{1,2},{2,3},{3,0},{4,5},{5,6},{6,7},{7,4},{8,9},{9,10},{10,1... | collective-permute-start | bytes 614408 | tf_op jit(solution)/shard_map/ppermute | solution.py:432
  132.7 2.7 %collective-permute-start.9 = (bf16[160,640]{1,0:T(8,128)(2,1)}, bf16[160,640]{1,0:T(8,128)(2,1)S(1)}, u32[]{:S(2)}, u32[]{:S(2)}) collective-permute-start(bf16[160,640]{1,0:T(8,128)(2,1)} %get-tuple-element.50), channel_id=1, source_target_pairs={{0,2},{1,3},{2,0},{3,1},{4,6},{5,7},{6,4},{7,5},{8,10},{9,11},{10,... | collective-permute-start | bytes 614408 | tf_op jit(solution)/shard_map/ppermute | solution.py:432
  135.4 5.1 %all-gather = f32[32,32,128]{2,1,0:T(8,128)S(1)} all-gather(f32[16,32,128]{2,1,0:T(8,128)S(1)} %all-to-all-done.4), channel_id=2, replica_groups=mesh['ylo'=2,'z'=8,'core'=2,'yhi'=4,'x'=4] {'core'}, dimensions={0}, use_global_device_ids=true | all-gather | bytes 786432 | tf_op jit(solution)/shard_map/all_gather | solution.py:472
  140.5 2.2 %shard_map.66 = bf16[160,2560]{1,0:T(8,128)(2,1)} custom-call(f32[2,2,4,2,32,128]{5,4,3,2,1,0:T(8,128)S(1)} %bitcast.11, bf16[640,160]{1,0:T(8,128)(2,1)S(1)} %copy-done.1, bf16[640,160]{1,0:T(8,128)(2,1)S(1)} %copy-done.2), custom_call_target="tpu_custom_call" | custom-call | flops 503316480 | bytes 1343488 | tf_op jit(solution)/shard_map/pallas_call | solution.py:393
  (72 shorter events, 15.8 us)
Async XLA Ops:
  7.2 66.4 %all-gather.3.cloned.1.call-start = ((), (), s32[]{:S(2)}) async-start(), calls=%async_computation.5 | async-start | bytes 4096000 | tf_op jit(solution)/shard_map/all_gather | solution.py:441
  9.9 19.4 %all-to-all-start = ((bf16[4,160,640]{2,1,0:T(8,128)(2,1)}), bf16[4,160,640]{2,1,0:T(8,128)(2,1)S(1)}, u32[]{:S(2)}, u32[]{:S(2)}) async-start(bf16[4,160,640]{2,1,0:T(8,128)(2,1)} %shard_map.59), calls=%async_computation | async-start | bytes 1638400 | tf_op jit(solution)/shard_map/all_to_all | solution.py:444
  14.9 54.2 %copy-start.5 = (s32[3]{0:T(128)}, s32[3]{0:T(128)S(1)}, u32[]{:S(2)}) copy-start(s32[3]{0:T(128)S(1)} %pad_add_fusion.where_ref.refs_0_) | copy-start | bytes 40
  15.4 58.2 %copy-start.8 = (bf16[160,640]{1,0:T(8,128)(2,1)}, bf16[160,640]{1,0:T(8,128)(2,1)S(1)}, u32[]{:S(2)}) copy-start(bf16[160,640]{1,0:T(8,128)(2,1)S(1)} %get-tuple-element.29.refs_4_) | copy-start | bytes 614404
  15.5 9.0 %collective-permute-start = (bf16[160,640]{1,0:T(8,128)(2,1)S(1)}, bf16[160,640]{1,0:T(8,128)(2,1)S(1)}, u32[]{:S(2)}, u32[]{:S(2)}) collective-permute-start(bf16[160,640]{1,0:T(8,128)(2,1)S(1)} %get-tuple-element.29.refs_4_), channel_id=1, source_target_pairs={{0,4},{4,8},{8,12},{12,0},{256,268},{260,256},{264,260},{268,264},... | collective-permute-start | bytes 614408 | tf_op jit(solution)/shard_map/ppermute | solution.py:428
  19.7 8.9 %collective-permute-start.1 = (bf16[160,640]{1,0:T(8,128)(2,1)S(1)}, bf16[160,640]{1,0:T(8,128)(2,1)S(1)}, u32[]{:S(2)}, u32[]{:S(2)}) collective-permute-start(bf16[160,640]{1,0:T(8,128)(2,1)S(1)} %get-tuple-element.30), channel_id=1, source_target_pairs={{0,12},{4,0},{8,4},{12,8},{256,260},{260,264},{264,268},{268,256},... | collective-permute-start | bytes 614408 | tf_op jit(solution)/shard_map/ppermute | solution.py:428
  24.5 49.1 %copy-start.14 = (bf16[160,640]{1,0:T(8,128)(2,1)}, bf16[160,640]{1,0:T(8,128)(2,1)S(1)}, u32[]{:S(2)}) copy-start(bf16[160,640]{1,0:T(8,128)(2,1)S(1)} %collective-permute-done.refs_6_) | copy-start | bytes 614404
  29.9 43.7 %copy-start.7 = (bf16[480,640]{1,0:T(8,128)(2,1)}, bf16[480,640]{1,0:T(8,128)(2,1)S(1)}, u32[]{:S(2)}) copy-start(bf16[480,640]{1,0:T(8,128)(2,1)S(1)} %get-tuple-element.35.refs_5_) | copy-start | bytes 1843204
  30.0 21.5 %collective-permute-start.2 = (bf16[480,640]{1,0:T(8,128)(2,1)S(1)}, bf16[480,640]{1,0:T(8,128)(2,1)}, u32[]{:S(2)}, u32[]{:S(2)}) collective-permute-start(bf16[480,640]{1,0:T(8,128)(2,1)S(1)} %get-tuple-element.35.refs_5_), channel_id=1, source_target_pairs={{0,4},{4,8},{8,12},{12,0},{256,268},{260,256},{264,260},{268,264},... | collective-permute-start | bytes 1843208 | tf_op jit(solution)/shard_map/ppermute | solution.py:428
  36.1 32.0 %collective-permute-start.3 = (bf16[480,640]{1,0:T(8,128)(2,1)S(1)}, bf16[480,640]{1,0:T(8,128)(2,1)}, u32[]{:S(2)}, u32[]{:S(2)}) collective-permute-start(bf16[480,640]{1,0:T(8,128)(2,1)S(1)} %get-tuple-element.38), channel_id=1, source_target_pairs={{0,12},{4,0},{8,4},{12,8},{256,260},{260,264},{264,268},{268,256},... | collective-permute-start | bytes 1843208 | tf_op jit(solution)/shard_map/ppermute | solution.py:428
  39.0 34.6 %all-to-all-start.1 = ((bf16[4,160,640]{2,1,0:T(8,128)(2,1)}), bf16[4,160,640]{2,1,0:T(8,128)(2,1)S(1)}, u32[]{:S(2)}, u32[]{:S(2)}) async-start(bf16[4,160,640]{2,1,0:T(8,128)(2,1)} %shard_map.62), calls=%async_computation.1 | async-start | bytes 1638400 | tf_op jit(solution)/shard_map/all_to_all | solution.py:448
  44.1 39.1 %collective-permute-start.4 = (bf16[80,640]{1,0:T(8,128)(2,1)S(1)}, bf16[80,640]{1,0:T(8,128)(2,1)S(1)}, u32[]{:S(2)}, u32[]{:S(2)}) collective-permute-start(bf16[80,640]{1,0:T(8,128)(2,1)S(1)} %slice.12), channel_id=1, source_target_pairs={{0,4},{4,8},{8,12},{12,0},{256,268},{260,256},{264,260},{268,264},... | collective-permute-start | bytes 307208 | tf_op jit(solution)/shard_map/ppermute | solution.py:428
  48.4 34.9 %collective-permute-start.5 = (bf16[80,640]{1,0:T(8,128)(2,1)S(1)}, bf16[80,640]{1,0:T(8,128)(2,1)S(1)}, u32[]{:S(2)}, u32[]{:S(2)}) collective-permute-start(bf16[80,640]{1,0:T(8,128)(2,1)S(1)} %slice.13), channel_id=1, source_target_pairs={{0,12},{4,0},{8,4},{12,8},{256,260},{260,264},{264,268},{268,256},... | collective-permute-start | bytes 307208 | tf_op jit(solution)/shard_map/ppermute | solution.py:428
  52.5 30.7 %collective-permute-start.6 = (bf16[240,640]{1,0:T(8,128)(2,1)S(1)}, bf16[240,640]{1,0:T(8,128)(2,1)S(1)}, u32[]{:S(2)}, u32[]{:S(2)}) collective-permute-start(bf16[240,640]{1,0:T(8,128)(2,1)S(1)} %slice.16), channel_id=1, source_target_pairs={{0,4},{4,8},{8,12},{12,0},{256,268},{260,256},{264,260},{268,264},... | collective-permute-start | bytes 921608 | tf_op jit(solution)/shard_map/ppermute | solution.py:428
  69.1 17.1 %collective-permute-start.7 = (bf16[240,640]{1,0:T(8,128)(2,1)S(1)}, bf16[240,640]{1,0:T(8,128)(2,1)S(1)}, u32[]{:S(2)}, u32[]{:S(2)}) collective-permute-start(bf16[240,640]{1,0:T(8,128)(2,1)S(1)} %slice.17), channel_id=1, source_target_pairs={{0,12},{4,0},{8,4},{12,8},{256,260},{260,264},{264,268},{268,256},... | collective-permute-start | bytes 921608 | tf_op jit(solution)/shard_map/ppermute | solution.py:428
  91.6 14.6 %all-to-all-start.2 = ((f32[16,64,128]{2,1,0:T(8,128)}), f32[16,64,128]{2,1,0:T(8,128)S(1)}, u32[]{:S(2)}, u32[]{:S(2)}) async-start(f32[16,64,128]{2,1,0:T(8,128)} %shard_map.64.refs_3_), calls=%async_computation.2 | async-start | bytes 1048576 | tf_op jit(solution)/shard_map/all_to_all | solution.py:464
  96.4 44.1 %copy-start.1 = (bf16[640,160]{1,0:T(8,128)(2,1)S(1)}, bf16[640,160]{1,0:T(8,128)(2,1)}, u32[]{:S(2)}) copy-start(bf16[640,160]{1,0:T(8,128)(2,1)} %get-tuple-element.40.refs_3_.refs_4_.refs_1_) | copy-start | bytes 614404
  96.4 44.1 %copy-start.2 = (bf16[640,160]{1,0:T(8,128)(2,1)S(1)}, bf16[640,160]{1,0:T(8,128)(2,1)}, u32[]{:S(2)}) copy-start(bf16[640,160]{1,0:T(8,128)(2,1)} %get-tuple-element.41.refs_4_.refs_5_.refs_2_) | copy-start | bytes 614404
  102.1 40.6 %copy-start.4 = (bf16[160,640]{1,0:T(8,128)(2,1)S(1)}, bf16[160,640]{1,0:T(8,128)(2,1)}, u32[]{:S(2)}) copy-start(bf16[160,640]{1,0:T(8,128)(2,1)} %get-tuple-element.52.refs_0_) | copy-start | bytes 614404
  102.1 40.6 %copy-start.6 = (s32[3]{0:T(128)S(1)}, s32[3]{0:T(128)}, u32[]{:S(2)}) copy-start(s32[3]{0:T(128)} %copy-done.5) | copy-start | bytes 40
  123.9 11.5 %all-to-all-start.4 = ((f32[16,32,128]{2,1,0:T(8,128)}), f32[16,32,128]{2,1,0:T(8,128)S(1)}, u32[]{:S(2)}, u32[]{:S(2)}) async-start(f32[16,32,128]{2,1,0:T(8,128)} %broadcast_in_dim.22), calls=%async_computation.4 | async-start | bytes 524288 | tf_op jit(solution)/shard_map/all_to_all | solution.py:471
  127.4 15.3 %collective-permute-start.10 = (bf16[160,640]{1,0:T(8,128)(2,1)}, bf16[160,640]{1,0:T(8,128)(2,1)S(1)}, u32[]{:S(2)}, u32[]{:S(2)}) collective-permute-start(bf16[160,640]{1,0:T(8,128)(2,1)} %get-tuple-element.51), channel_id=1, source_target_pairs={{0,3},{1,0},{2,1},{3,2},{4,7},{5,4},{6,5},{7,6},{8,11},{9,8},{10,9... | collective-permute-start | bytes 614408 | tf_op jit(solution)/shard_map/ppermute | solution.py:432
  129.9 12.8 %collective-permute-start.8 = (bf16[160,640]{1,0:T(8,128)(2,1)}, bf16[160,640]{1,0:T(8,128)(2,1)S(1)}, u32[]{:S(2)}, u32[]{:S(2)}) collective-permute-start(bf16[160,640]{1,0:T(8,128)(2,1)} %get-tuple-element.49), channel_id=1, source_target_pairs={{0,1},{1,2},{2,3},{3,0},{4,5},{5,6},{6,7},{7,4},{8,9},{9,10},{10,1... | collective-permute-start | bytes 614408 | tf_op jit(solution)/shard_map/ppermute | solution.py:432
  132.7 10.0 %collective-permute-start.9 = (bf16[160,640]{1,0:T(8,128)(2,1)}, bf16[160,640]{1,0:T(8,128)(2,1)S(1)}, u32[]{:S(2)}, u32[]{:S(2)}) collective-permute-start(bf16[160,640]{1,0:T(8,128)(2,1)} %get-tuple-element.50), channel_id=1, source_target_pairs={{0,2},{1,3},{2,0},{3,1},{4,6},{5,7},{6,4},{7,5},{8,10},{9,11},{10,... | collective-permute-start | bytes 614408 | tf_op jit(solution)/shard_map/ppermute | solution.py:432
  (10 other events, 101.1 us)
Sparse Core Ops, SparseCore 0:
  10.1 60.1 all-gather.2
